TPU v7x, 32 devices: a whole 2x2x4 slice. The times are simulated.
32 devices in a mesh: grp: 2 (over x), blk: 16 (over z, y, core).
Axes of the slice: x: 2, y: 2, z: 4, core: 2. Of those that a mesh axis runs over, the one named last changes fastest.
Arguments:
- parent_rows: bfloat16 [32, 12288], P(('grp', 'blk')), parts along dimension 0, may hold values from -3 to 3
- token_rows: bfloat16 [64, 12288], P(('grp', 'blk')), parts along dimension 0, may hold values from -3 to 3
- parent: int32 [64], P('grp'), parts along dimension 0, may hold values from 0 to 15
- d_hidden: bfloat16 [64, 2048], P('grp', 'blk'), parts along dimension 0, may hold values from -3 to 3
- w_gate: bfloat16 [12288, 2048], P(None, 'blk'), may hold values from -0.0546875 to 0.0546875
- w_up: bfloat16 [12288, 2048], P(None, 'blk'), may hold values from -0.0546875 to 0.0546875
Outputs:
- grad_gate: bfloat16 [12288, 4096], P(None, ('grp', 'blk')), parts along dimension 1
- grad_up: bfloat16 [12288, 4096], P(None, ('grp', 'blk')), parts along dimension 1
- grad_parent: bfloat16 [32, 12288], P(('grp', 'blk')), parts along dimension 0
There are 2 independent parts, one for each index of `grp`. A program takes and returns all parts, laid end to end along the dimension named above; an argument that names none is the same for every part. Nothing has to cross between parts.
Inputs may be any that keep to these rules, and one draw needn't show every extreme that they name: Each hypothesis row names its parent among the 16 parent rows.
All inputs are finite; a program needn't handle non-finite values.
Results may differ from a plain program's by a relative error of at most 0.0069.
Values may be sent and summed in bfloat16 or wider, within the bound.
No kernel may reach another device: no remote copies, remote signals or barrier semaphores. Data moves between devices by JAX's collectives and lax.ppermute only.
A program may use at most 128 MiB of HBM per device.

v0:
```python
import jax
import jax.numpy as jnp
from jax import lax
from jax.sharding import PartitionSpec as P


def forward_rows(prefixes, tokens, owners, upstream, w_gate, w_up):
    picked = jnp.take(prefixes, owners, axis=0).astype(jnp.float32)
    inputs = (picked + tokens.astype(jnp.float32)).astype(jnp.bfloat16)
    gate = jnp.dot(inputs, w_gate, preferred_element_type=jnp.float32)
    up = jnp.dot(inputs, w_up, preferred_element_type=jnp.float32)
    sig = jax.nn.sigmoid(gate)
    flow = upstream.astype(jnp.float32)
    d_gate = (flow * up * sig * (1.0 + gate * (1.0 - sig))).astype(jnp.bfloat16)
    d_up = (flow * gate * sig).astype(jnp.bfloat16)
    return (inputs, d_gate, d_up)


def owner_sums(prefix_count, owners, d_gate, d_up):
    labels = lax.broadcasted_iota(jnp.int32, (prefix_count, owners.shape[0]), 0)
    onehot = (labels == owners[None, :]).astype(jnp.bfloat16)
    sum_gate = jnp.dot(onehot, d_gate, preferred_element_type=jnp.float32)
    sum_up = jnp.dot(onehot, d_up, preferred_element_type=jnp.float32)
    return (sum_gate, sum_up)


def weight_terms(inputs, d_gate, d_up):
    contract = (((0,), (0,)), ((), ()))
    part_gate = lax.dot_general(inputs, d_gate, contract, preferred_element_type=jnp.float32)
    part_up = lax.dot_general(inputs, d_up, contract, preferred_element_type=jnp.float32)
    return (part_gate, part_up)


def body(parent_rows, token_rows, parent, d_hidden, w_gate, w_up):
    prefixes, tokens = (
        lax.all_gather(parent_rows, "blk", axis=0, tiled=True),
        lax.all_gather(token_rows, "blk", axis=0, tiled=True),
    )
    inputs, d_gate, d_up = forward_rows(prefixes, tokens, parent, d_hidden, w_gate, w_up)
    sum_gate, sum_up = owner_sums(prefixes.shape[0], parent, d_gate, d_up)
    part_gate, part_up = weight_terms(inputs, d_gate, d_up)
    grad_gate = part_gate.astype(jnp.bfloat16)
    grad_up = part_up.astype(jnp.bfloat16)
    parent_gate = sum_gate.astype(jnp.bfloat16)
    parent_up = sum_up.astype(jnp.bfloat16)
    contract = (((1,), (1,)), ((), ()))
    total = lax.dot_general(parent_gate, w_gate, contract, preferred_element_type=jnp.float32)
    summed = lax.psum_scatter(
        total + lax.dot_general(parent_up, w_up, contract, preferred_element_type=jnp.float32),
        "blk",
        scatter_dimension=0,
        tiled=True,
    )
    return (grad_gate, grad_up, summed.astype(jnp.bfloat16))


def solution(mesh):
    in_specs = (
        P(("grp", "blk"), None),
        P(("grp", "blk"), None),
        P("grp"),
        P("grp", "blk"),
        P(None, "blk"),
        P(None, "blk"),
    )
    out_specs = (P(None, ("grp", "blk")), P(None, ("grp", "blk")), P(("grp", "blk"), None))
    return jax.shard_map(body, mesh=mesh, in_specs=in_specs, out_specs=out_specs, check_vma=False)
```

profile of v0, /device:TPU:0, one launch (start us, length us, event | category | flops | bytes accessed | tf_op | source)
XLA Modules:
  0.0 141.4 jit_solution(17351475242933605535)
XLA Ops:
  0.6 0.0 copy-start
  0.6 1.4 dynamic-slice
  2.0 0.7 compare_and_fusion
  2.7 0.7 compare_select_fusion
  3.4 25.7 %all-gather = bf16[16,1,12288]{2,1,0:T(2,128)(2,1)S(1)} all-gather(bf16[1,1,12288]{2,1,0:T(2,128)(2,1)} %bitcast.17), channel_id=1, replica_groups=mesh['grp'=2,'blk'=16] {'blk'}, dimensions={0}, use_global_device_ids=true | all-gather | bytes 417792 | tf_op jit(solution)/shard_map/all_gather | solution.py:36
  29.1 0.4 copy.11
  29.5 1.9 %gather_fusion = bf16[32,12288]{1,0:T(8,128)(2,1)} fusion(bf16[16,12288]{1,0:T(8,128)(2,1)S(1)} %bitcast.16, s32[1024]{0:T(1024)S(1)} %pad_clamp_fusion), kind=kCustom, calls=%fused_computation | custom fusion | bytes 1572992 | tf_op jit(solution)/shard_map/jit(_take)/gather | solution.py:8
  31.4 21.2 %all-gather.1 = bf16[16,2,12288]{2,1,0:T(2,128)(2,1)} all-gather(bf16[1,2,12288]{2,1,0:T(2,128)(2,1)} %bitcast.18), channel_id=1, replica_groups=mesh['grp'=2,'blk'=16] {'blk'}, dimensions={0}, use_global_device_ids=true | all-gather | bytes 835584 | tf_op jit(solution)/shard_map/all_gather | solution.py:37
  52.6 3.0 %reshape.25 = f32[32,12288]{1,0:T(8,128)} reshape(bf16[16,2,12288]{2,1,0:T(2,128)(2,1)} %all-gather.1) | data formatting | bytes 2359296 | tf_op jit(solution)/shard_map/convert_element_type | solution.py:9
  55.7 0.0 copy-start.3
  55.7 2.0 %add_convert_fusion = bf16[32,12288]{1,0:T(8,128)(2,1)S(1)} fusion(f32[32,12288]{1,0:T(8,128)} %reshape.25, bf16[32,12288]{1,0:T(8,128)(2,1)} %gather_fusion, pred[32]{0:T(512)(128)(4,1)S(1)} %compare_and_fusion), kind=kLoop, calls=%fused_computation.4 | loop fusion | flops 1572864 | bytes 3145760 | tf_op jit(solution)/shard_map/convert_element_type | solution.py:9
  57.7 0.0 copy-done
  57.7 0.0 copy-start.1
  57.7 0.0 copy-start.7
  57.7 0.6 fusion.13
  58.3 0.2 copy-done.1
  58.6 0.0 copy-done.3
  58.6 0.0 copy-done.4
  58.6 0.6 fusion.2
  59.2 0.0 copy-done.7
  59.2 0.0 copy-start.5
  59.2 1.9 %fusion.3 = f32[16,12288]{1,0:T(8,128)} fusion(bf16[12288,128]{1,0:T(8,128)(2,1)S(1)} %copy-done, bf16[32,128]{1,0:T(8,128)(2,1)S(1)} %fusion.2, s32[32]{0:T(128)S(1)} %copy-done.7), kind=kOutput, calls=%fused_computation.11 | convolution fusion | flops 50465280 | bytes 3940480 | tf_op jit(solution)/shard_map/dot_general | solution.py:47
  61.1 0.0 copy-done.5
  61.1 4.0 %convolution_add_fusion = f32[16,12288]{1,0:T(8,128)} fusion(f32[16,12288]{1,0:T(8,128)} %fusion.3, bf16[12288,128]{1,0:T(8,128)(2,1)} %param.11, s32[32]{0:T(128)S(1)} %copy-done.7, f32[32,128]{1,0:T(8,128)S(1)} %fusion.13, bf16[32,128]{1,0:T(8,128)(2,1)S(1)} %copy-done.4), kind=kOutput, calls=%fused_computation.3 | convolution fusion | flops 50690560 | bytes 4743296 | tf_op jit(solution)/shard_map/dot_general | solution.py:49
  65.1 68.4 %all-reduce.2 = bf16[16,12288]{1,0:T(8,128)(2,1)S(1)} all-reduce(f32[16,12288]{1,0:T(8,128)} %convolution_add_fusion), channel_id=2, replica_groups=mesh['grp'=2,'blk'=16] {'blk'}, use_global_device_ids=true, to_apply=%region_0.1.clone | all-reduce | flops 196608 | bytes 1179648
  133.5 0.0 copy-start.2
  133.5 0.0 copy-start.6
  133.5 1.3 dynamic-slice_convert_fusion
  134.8 3.8 %convolution_convert_fusion = bf16[12288,128]{1,0:T(8,128)(2,1)} fusion(bf16[32,12288]{1,0:T(8,128)(2,1)} %copy-done.1, f32[32,128]{1,0:T(8,128)S(1)} %fusion.13, bf16[32,128]{1,0:T(8,128)(2,1)} %param.9), kind=kOutput, calls=%fused_computation.1 | convolution fusion | flops 102264832 | bytes 3956736 | tf_op jit(solution)/shard_map/dot_general | solution.py:30
  138.7 0.0 copy-done.2
  138.7 0.0 copy-done.6
  138.7 2.7 %convolution_convert_fusion.1 = bf16[12288,128]{1,0:T(8,128)(2,1)} fusion(bf16[32,12288]{1,0:T(8,128)(2,1)S(1)} %copy-done.2, bf16[32,128]{1,0:T(8,128)(2,1)S(1)} %copy-done.6), kind=kOutput, calls=%fused_computation.2 | convolution fusion | flops 102236160 | bytes 3940352 | tf_op jit(solution)/shard_map/dot_general | solution.py:29
  (2 shorter events, 0.0 us)
Async XLA Ops:
  0.6 57.0 %copy-start = (bf16[12288,128]{1,0:T(8,128)(2,1)S(1)}, bf16[12288,128]{1,0:T(8,128)(2,1)}, u32[]{:S(2)}) copy-start(bf16[12288,128]{1,0:T(8,128)(2,1)} %param.10) | copy-start | bytes 9437188
  55.7 2.9 %copy-start.3 = (bf16[12288,128]{1,0:T(8,128)(2,1)S(1)}, bf16[12288,128]{1,0:T(8,128)(2,1)}, u32[]{:S(2)}) copy-start(bf16[12288,128]{1,0:T(8,128)(2,1)} %param.11) | copy-start | bytes 9437188
  55.7 2.9 %copy-start.4 = (bf16[32,128]{1,0:T(8,128)(2,1)S(1)}, bf16[32,128]{1,0:T(8,128)(2,1)}, u32[]{:S(2)}) copy-start(bf16[32,128]{1,0:T(8,128)(2,1)} %param.9) | copy-start | bytes 24580
  57.7 0.9 copy-start.1
  57.7 1.5 %copy-start.7 = (s32[32]{0:T(128)S(1)}, s32[32]{0:T(128)}, u32[]{:S(2)}) copy-start(s32[32]{0:T(128)} %param.8) | copy-start | bytes 388
  59.2 1.9 %copy-start.5 = (bf16[32,128]{1,0:T(8,128)(2,1)}, bf16[32,128]{1,0:T(8,128)(2,1)S(1)}, u32[]{:S(2)}) copy-start(bf16[32,128]{1,0:T(8,128)(2,1)S(1)} %fusion.2) | copy-start | bytes 24580
  133.5 5.2 %copy-start.2 = (bf16[32,12288]{1,0:T(8,128)(2,1)S(1)}, bf16[32,12288]{1,0:T(8,128)(2,1)}, u32[]{:S(2)}) copy-start(bf16[32,12288]{1,0:T(8,128)(2,1)} %copy-done.1) | copy-start | bytes 2359300
  133.5 5.2 %copy-start.6 = (bf16[32,128]{1,0:T(8,128)(2,1)S(1)}, bf16[32,128]{1,0:T(8,128)(2,1)}, u32[]{:S(2)}) copy-start(bf16[32,128]{1,0:T(8,128)(2,1)} %copy-done.5) | copy-start | bytes 24580
where the time goes:
time: 142 us; the launch traced here: 141 us
  blocking collectives  115 us (81%)
  matrix products  13.6 us (10%)
  local copies, waits for them, and re-layouts  8.35 us (6%)
  other arithmetic  3.33 us (2%)
    unnamed x1, blocking collectives  68.4 us
    all_gather x1, blocking collectives, body(): lax.all_gather(parent_rows, 'blk', axis=0, tiled=True)  25.7 us
    all_gather x1, blocking collectives, body(): lax.all_gather(token_rows, 'blk', axis=0, tiled=True)  21.2 us
    dot_general x1, matrix products, body(): lax.dot_general(parent_up, w_up, contract, preferred_element_type=jnp.flo...  3.99 us
    dot_general x1, matrix products, weight_terms(): lax.dot_general(inputs, d_up, contract, preferred_element_type=jnp.float32)  3.83 us
    convert_element_type x1, local copies, waits for them, and re-layouts, forward_rows(): inputs = (picked + tokens.astype(jnp.float32)).astype(jnp.bfloat16)  3.02 us

commit v1 on v0

v1 whole, which is shorter than its diff:
```python
import jax
import jax.numpy as jnp
from jax import lax
from jax.sharding import PartitionSpec as P

BF = jnp.bfloat16
F32 = jnp.float32


def factors(count):
    chips = count // 2
    bits = chips.bit_length() - 1
    outer = 1 << ((bits + 1) // 2)
    return outer, chips // outer, 2


def partner(mask, count):
    return [(i, i ^ mask) for i in range(count)]


def slot_masks(count):
    outer, inner, _ = factors(count)
    return [(z * inner + y) * 2 + c for c in range(2) for y in range(inner) for z in range(outer)]


def gather(block, count):
    outer, inner, _ = factors(count)
    send = lambda x, mask: lax.ppermute(x, "blk", partner(mask, count))
    column = jnp.concatenate([block] + [send(block, z * inner * 2) for z in range(1, outer)], 0)
    plane = jnp.concatenate([column] + [send(column, y * 2) for y in range(1, inner)], 0)
    return jnp.concatenate([plane, send(plane, 1)], 0)


def scatter(terms, count):
    outer, inner, _ = factors(count)
    send = lambda x, mask: lax.ppermute(x, "blk", partner(mask, count))
    half = count
    low, high = terms[:half], terms[half:].astype(BF)
    total = low + send(high, 1).astype(F32)
    step = outer * 2
    rows = total[:step]
    for y in range(1, inner):
        rows = rows + send(total[y * step:(y + 1) * step].astype(BF), y * 2).astype(F32)
    own = rows[:2]
    for z in range(1, outer):
        own = own + send(rows[2 * z:2 * z + 2].astype(BF), z * inner * 2).astype(F32)
    return own


def body(parent_rows, token_rows, parent, d_hidden, w_gate, w_up):
    count = lax.axis_size("blk")
    width = token_rows.shape[1]
    half = width // 2
    hyp = parent.shape[0]
    me = lax.axis_index("blk")
    block = jnp.concatenate([token_rows, parent_rows.reshape(2, half)], 1)
    rows = gather(block, count)
    tokens, pairs = rows[:, :width], rows[:, width:]
    prefixes = pairs.reshape(count, width)
    owner = jnp.array(slot_masks(count), jnp.int32) ^ me
    order = (owner[:, None] * 2 + jnp.arange(2, dtype=jnp.int32)).reshape(hyp)
    perm = (order[:, None] == jnp.arange(hyp)[None, :]).astype(BF)
    flow = jnp.dot(perm, d_hidden, preferred_element_type=F32)
    match = (owner[:, None] == parent[None, :]).astype(BF)
    onehot = lax.dot_general(match, perm, (((1,), (1,)), ((), ())), preferred_element_type=F32).astype(BF)
    picked = lax.dot_general(onehot, prefixes, (((0,), (0,)), ((), ())), preferred_element_type=F32)
    inputs = (picked + tokens.astype(F32)).astype(BF)
    gate = jnp.dot(inputs, w_gate, preferred_element_type=F32)
    up = jnp.dot(inputs, w_up, preferred_element_type=F32)
    sig = jax.nn.sigmoid(gate)
    d_gate = (flow * up * sig * (1.0 + gate * (1.0 - sig))).astype(BF)
    d_up = (flow * gate * sig).astype(BF)
    parent_gate = jnp.dot(onehot, d_gate, preferred_element_type=F32).astype(BF)
    parent_up = jnp.dot(onehot, d_up, preferred_element_type=F32).astype(BF)
    contract = (((1,), (1,)), ((), ()))
    total = lax.dot_general(parent_gate, w_gate, contract, preferred_element_type=F32)
    total = total + lax.dot_general(parent_up, w_up, contract, preferred_element_type=F32)
    own = scatter(total.reshape(count * 2, half), count)
    contract = (((0,), (0,)), ((), ()))
    grad_gate = lax.dot_general(inputs, d_gate, contract, preferred_element_type=F32).astype(BF)
    grad_up = lax.dot_general(inputs, d_up, contract, preferred_element_type=F32).astype(BF)
    return grad_gate, grad_up, own.astype(BF).reshape(1, width)


def solution(mesh):
    in_specs = (
        P(("grp", "blk"), None),
        P(("grp", "blk"), None),
        P("grp"),
        P("grp", "blk"),
        P(None, "blk"),
        P(None, "blk"),
    )
    out_specs = (P(None, ("grp", "blk")), P(None, ("grp", "blk")), P(("grp", "blk"), None))
    return jax.shard_map(body, mesh=mesh, in_specs=in_specs, out_specs=out_specs, check_vma=False)
```

time: 142 us -> 67.4 us (0.47)
  blocking collectives: 115 us -> 0 us
  waiting for transfers between devices: 0 us -> 13.5 us
  starting transfers between devices: 0 us -> 12.8 us
  local copies, waits for them, and re-layouts: 8.35 us -> 19.1 us
  matrix products: 13.6 us -> 16.4 us
    unnamed x1 -> x0, blocking collectives: 68.4 us -> none
    all_gather x2 -> x0, blocking collectives: 46.9 us -> none  [the longest x1 25.7 us: body(): lax.all_gather(parent_rows, 'blk', axis=0, tiled=True)]
    ppermute x0 -> x10, waiting for transfers between devices: none -> 13.5 us  [the longest x5 13.3 us: gather(): send = lambda x, mask: lax.ppermute(x, 'blk', partner(mask, count))]
    ppermute x0 -> x10, starting transfers between devices: none -> 12.8 us  [the longest x5 7.28 us: gather(): send = lambda x, mask: lax.ppermute(x, 'blk', partner(mask, count))]
    concatenate x0 -> x3, local copies, waits for them, and re-layouts: none -> 11.8 us  [the longest x1 7.89 us: gather(): return jnp.concatenate([plane, send(plane, 1)], 0)]
    slice x0 -> x6, local copies, waits for them, and re-layouts: none -> 3.96 us  [the longest x3 2.86 us: scatter(): low, high = (terms[:half], terms[half:].astype(BF))]
    convert_element_type x2 -> x1, local copies, waits for them, and re-layouts: 4.32 us -> 0.74 us  [scatter(): low, high = (terms[:half], terms[half:].astype(BF))]
    dot_general x6 -> x9, matrix products: 13.6 us -> 16.4 us  [the longest x1 3.98 us: body(): lax.dot_general(parent_up, w_up, contract, preferred_element_type=F32)]
  transfers between devices with their start and end apart: 0 -> 10, of which waited for: 0 -> 5; matrix products, arithmetic and copies ran while one was open for 0% -> 15% of each run, Pallas kernels for 0% -> 0%
where the time goes in v1:
time: 67.4 us; the launch traced here: 66.6 us
  local copies, waits for them, and re-layouts  19.1 us (28%)
  matrix products  16.4 us (24%)
  waiting for transfers between devices  13.5 us (20%)
  starting transfers between devices  12.8 us (19%)
  other arithmetic  4.1 us (6%)
  between operations  0.76 us (1%)
    ppermute x5, waiting for transfers between devices, gather(): send = lambda x, mask: lax.ppermute(x, 'blk', partner(mask, count))  13.3 us
    concatenate x1, local copies, waits for them, and re-layouts, gather(): return jnp.concatenate([plane, send(plane, 1)], 0)  7.89 us
    ppermute x5, starting transfers between devices, gather(): send = lambda x, mask: lax.ppermute(x, 'blk', partner(mask, count))  7.28 us
    ppermute x5, starting transfers between devices, scatter(): send = lambda x, mask: lax.ppermute(x, 'blk', partner(mask, count))  5.5 us
    dot_general x1, matrix products, body(): lax.dot_general(parent_up, w_up, contract, preferred_element_type=F32)  3.98 us
    dot_general x1, matrix products, body(): lax.dot_general(inputs, d_up, contract, preferred_element_type=F32)  3.83 us
    concatenate x1, local copies, waits for them, and re-layouts, gather(): jnp.concatenate([column] + [send(column, y * 2) for y in range(1, inner)]...  3.83 us
    slice x3, local copies, waits for them, and re-layouts, scatter(): low, high = (terms[:half], terms[half:].astype(BF))  2.86 us
  transfers between devices with their start and end apart: 10, of which 5 were waited for; matrix products, arithmetic and copies ran while one was open for 15% of the time, Pallas kernels for 0%

profile of v1, /device:TPU:0, one launch (start us, length us, event | category | flops | bytes accessed | tf_op | source)
XLA Modules:
  0.0 66.6 jit_solution(8979119656701136118)
XLA Ops:
  0.6 1.1 %reduce = bf16[12288]{0:T(1024)(128)(2,1)S(1)} reduce(bf16[1,12288]{1,0:T(2,128)(2,1)} %param.7, bf16[]{:T(256)} %constant.13), dimensions={0}, to_apply=%param.7.reduce_sub_computation | reduce | bytes 49154 | tf_op args[0]
  1.7 0.8 %constant_dynamic-update-slice_fusion.1 = bf16[2,18432]{1,0:T(2,128)(2,1)S(1)} fusion(bf16[2,12288]{1,0:T(2,128)(2,1)} %param.8), kind=kLoop, calls=%fused_computation.32 | loop fusion | bytes 98304
  2.6 5.1 %collective-permute-start.2 = (bf16[2,18432]{1,0:T(2,128)(2,1)S(1)}, bf16[2,18432]{1,0:T(2,128)(2,1)S(1)}, u32[]{:S(2)}, u32[]{:S(2)}) collective-permute-start(bf16[2,18432]{1,0:T(2,128)(2,1)S(1)} %constant_dynamic-update-slice_fusion), channel_id=1, source_target_pairs={{0,12},{1,13},{2,14},{3,15},{4,8},{5,9},{6,10},{7,11},{8,4},{9,5},... | collective-permute-start | bytes 221192 | tf_op jit(solution)/shard_map/ppermute | solution.py:28
  7.7 0.6 collective-permute-start
  8.4 2.1 %collective-permute-done.2 = bf16[2,18432]{1,0:T(2,128)(2,1)S(1)} collective-permute-done((bf16[2,18432]{1,0:T(2,128)(2,1)S(1)}, bf16[2,18432]{1,0:T(2,128)(2,1)S(1)}, u32[]{:S(2)}, u32[]{:S(2)}) %collective-permute-start.2) | collective-permute-done | bytes 73760 | tf_op jit(solution)/shard_map/ppermute | solution.py:28
  10.5 3.5 %collective-permute-done.1 = bf16[2,18432]{1,0:T(2,128)(2,1)S(1)} collective-permute-done((bf16[2,18432]{1,0:T(2,128)(2,1)S(1)}, bf16[2,18432]{1,0:T(2,128)(2,1)S(1)}, u32[]{:S(2)}, u32[]{:S(2)}) %collective-permute-start.1) | collective-permute-done | bytes 73760 | tf_op jit(solution)/shard_map/ppermute | solution.py:28
  14.0 1.1 %pad_maximum_fusion = bf16[8,18432]{1,0:T(8,128)(2,1)} fusion(bf16[2,18432]{1,0:T(2,128)(2,1)S(1)} %collective-permute-done.2, bf16[2,18432]{1,0:T(2,128)(2,1)S(1)} %collective-permute-done.1, bf16[2,18432]{1,0:T(2,128)(2,1)S(1)} %collective-permute-done, bf16[2,18432]{1,0:T(2,128)(2,1)S(1)} %constant_dynamic-update-slice_fusion), kind=kLoop, calls=%fused_computation.15 | loop fusion | flops 1179648 | bytes 589824 | tf_op jit(solution)/shard_map/concatenate | solution.py:29
  15.0 1.5 %collective-permute-start.3 = (bf16[8,18432]{1,0:T(8,128)(2,1)}, bf16[8,18432]{1,0:T(8,128)(2,1)S(1)}, u32[]{:S(2)}, u32[]{:S(2)}) collective-permute-start(bf16[8,18432]{1,0:T(8,128)(2,1)} %pad_maximum_fusion), channel_id=1, source_target_pairs={{0,2},{1,3},{2,0},{3,1},{4,6},{5,7},{6,4},{7,5},{8,10},{9,11},{10,... | collective-permute-start | bytes 884744 | tf_op jit(solution)/shard_map/ppermute | solution.py:28
  16.6 7.0 %collective-permute-done.3 = bf16[8,18432]{1,0:T(8,128)(2,1)S(1)} collective-permute-done((bf16[8,18432]{1,0:T(8,128)(2,1)}, bf16[8,18432]{1,0:T(8,128)(2,1)S(1)}, u32[]{:S(2)}, u32[]{:S(2)}) %collective-permute-start.3) | collective-permute-done | bytes 294944 | tf_op jit(solution)/shard_map/ppermute | solution.py:28
  23.6 3.8 %concatenate.16 = bf16[16,18432]{1,0:T(8,128)(2,1)} concatenate(bf16[2,18432]{1,0:T(2,128)(2,1)S(1)} %constant_dynamic-update-slice_fusion, bf16[2,18432]{1,0:T(2,128)(2,1)} %copy-done.6, bf16[2,18432]{1,0:T(2,128)(2,1)} %copy-done.5, bf16[2,18432]{1,0:T(2,128)(2,1)} %copy-done.4, bf16[8,18432]{1,0:T(8,128)(2,1)S(1)} %collective-permute-done.3), dimensions={0} | concatenate | bytes 1179648 | tf_op jit(solution)/shard_map/concatenate | solution.py:30
  27.4 0.7 broadcast_xor_fusion
  28.2 0.8 %convolution_convert_fusion.4 = bf16[16,32]{1,0:T(8,128)(2,1)S(1)} fusion(s32[32]{0:T(128)S(1)} %add.50, s32[32]{0:T(128)} %param.9, s32[16]{0:T(128)S(1)} %get-tuple-element.8), kind=kOutput, calls=%fused_computation.11 | convolution fusion | flops 34816 | bytes 1344 | tf_op jit(solution)/shard_map/dot_general | solution.py:65
  29.1 0.7 %collective-permute-done.4 = bf16[16,18432]{1,0:T(8,128)(2,1)} collective-permute-done((bf16[16,18432]{1,0:T(8,128)(2,1)}, bf16[16,18432]{1,0:T(8,128)(2,1)}, u32[]{:S(2)}, u32[]{:S(2)}) %collective-permute-start.4) | collective-permute-done | bytes 589856 | tf_op jit(solution)/shard_map/ppermute | solution.py:28
  29.8 7.9 %concatenate.17 = bf16[32,18432]{1,0:T(8,128)(2,1)} concatenate(bf16[2,18432]{1,0:T(2,128)(2,1)S(1)} %constant_dynamic-update-slice_fusion, bf16[2,18432]{1,0:T(2,128)(2,1)} %copy-done.6, bf16[2,18432]{1,0:T(2,128)(2,1)} %copy-done.5, bf16[2,18432]{1,0:T(2,128)(2,1)} %copy-done.4, bf16[8,18432]{1,0:T(8,128)(2,1)S(1)} %collective-permute-done.3, ...), dimensions={0} | concatenate | bytes 2359296 | tf_op jit(solution)/shard_map/concatenate | solution.py:31
  37.7 1.0 %slice.50 = bf16[32,6144]{1,0:T(8,128)(2,1)S(1)} slice(bf16[32,18432]{1,0:T(8,128)(2,1)} %concatenate.17), slice={[0:32], [12288:18432]} | slice | bytes 786432 | tf_op jit(solution)/shard_map/slice | solution.py:58
  38.7 0.9 %reshape.38 = bf16[16,12288]{1,0:T(8,128)(2,1)} reshape(bf16[32,6144]{1,0:T(8,128)(2,1)S(1)} %slice.50) | data formatting | bytes 786432 | tf_op jit(solution)/shard_map/reshape | solution.py:59
  39.6 1.8 %fusion = bf16[32,12288]{1,0:T(8,128)(2,1)S(1)} fusion(bf16[16,32]{1,0:T(8,128)(2,1)S(1)} %convolution_convert_fusion.4, bf16[16,12288]{1,0:T(8,128)(2,1)} %reshape.38, bf16[32,18432]{1,0:T(8,128)(2,1)} %concatenate.17), kind=kOutput, calls=%fused_computation.3 | convolution fusion | flops 13762560 | bytes 1967104 | tf_op jit(solution)/shard_map/dot_general | solution.py:66
  41.4 0.6 fusion.17
  42.3 0.6 fusion.3
  42.9 1.9 %fusion.4 = f32[16,12288]{1,0:T(8,128)} fusion(bf16[12288,128]{1,0:T(8,128)(2,1)S(1)} %copy-done, bf16[16,32]{1,0:T(8,128)(2,1)S(1)} %convolution_convert_fusion.4, bf16[32,128]{1,0:T(8,128)(2,1)S(1)} %fusion.3), kind=kOutput, calls=%fused_computation.12 | convolution fusion | flops 50464768 | bytes 3941376 | tf_op jit(solution)/shard_map/dot_general | solution.py:76
  44.8 4.0 %convolution_add_fusion.1 = f32[16,12288]{1,0:T(8,128)} fusion(f32[16,12288]{1,0:T(8,128)} %fusion.4, bf16[12288,128]{1,0:T(8,128)(2,1)} %param.12, bf16[16,32]{1,0:T(8,128)(2,1)S(1)} %convolution_convert_fusion.4, bf16[32,128]{1,0:T(8,128)(2,1)S(1)} %get-tuple-element.10), kind=kOutput, calls=%fused_computation.4 | convolution fusion | flops 50661376 | bytes 4727808 | tf_op jit(solution)/shard_map/dot_general | solution.py:77
  48.8 1.0 %slice.73 = bf16[8,12288]{1,0:T(8,128)(2,1)S(1)} slice(f32[16,12288]{1,0:T(8,128)} %convolution_add_fusion.1), slice={[8:16], [0:12288]} | slice | bytes 393216 | tf_op jit(solution)/shard_map/slice | solution.py:38
  49.8 0.7 %convert_element_type.64 = bf16[16,6144]{1,0:T(8,128)(2,1)} reshape(bf16[8,12288]{1,0:T(8,128)(2,1)S(1)} %slice.73) | data formatting | bytes 393216 | tf_op jit(solution)/shard_map/convert_element_type | solution.py:38
  50.7 1.0 %slice.52 = f32[8,12288]{1,0:T(8,128)S(1)} slice(f32[16,12288]{1,0:T(8,128)} %convolution_add_fusion.1), slice={[0:8], [0:12288]} | slice | bytes 786432 | tf_op jit(solution)/shard_map/slice | solution.py:38
  51.7 0.8 %slice.42 = f32[16,6144]{1,0:T(8,128)} reshape(f32[8,12288]{1,0:T(8,128)S(1)} %slice.52) | data formatting | bytes 786432 | tf_op jit(solution)/shard_map/slice | solution.py:38
  52.5 1.2 %convert_add_fusion = f32[16,6144]{1,0:T(8,128)S(1)} fusion(f32[16,6144]{1,0:T(8,128)} %slice.42, bf16[16,6144]{1,0:T(8,128)(2,1)} %collective-permute-done.5), kind=kLoop, calls=%fused_computation.14 | loop fusion | flops 196608 | bytes 983040 | tf_op jit(solution)/shard_map/add | solution.py:39
  53.7 1.8 %collective-permute-start.6 = (bf16[8,6144]{1,0:T(8,128)(2,1)S(1)}, bf16[8,6144]{1,0:T(8,128)(2,1)S(1)}, u32[]{:S(2)}, u32[]{:S(2)}) collective-permute-start(bf16[8,6144]{1,0:T(8,128)(2,1)S(1)} %slice.74), channel_id=1, source_target_pairs={{0,2},{1,3},{2,0},{3,1},{4,6},{5,7},{6,4},{7,5},{8,10},{9,11},{10,... | collective-permute-start | bytes 294920 | tf_op jit(solution)/shard_map/ppermute | solution.py:36
  55.5 3.8 %convolution_convert_fusion = bf16[12288,128]{1,0:T(8,128)(2,1)} fusion(bf16[32,12288]{1,0:T(8,128)(2,1)} %copy-done.1, bf16[32,128]{1,0:T(8,128)(2,1)S(1)} %copy-done.8), kind=kOutput, calls=%fused_computation | convolution fusion | flops 102236160 | bytes 3940352 | tf_op jit(solution)/shard_map/dot_general | solution.py:81
  59.5 1.7 %collective-permute-start.9 = (bf16[2,6144]{1,0:T(2,128)(2,1)S(1)}, bf16[2,6144]{1,0:T(2,128)(2,1)S(1)}, u32[]{:S(2)}, u32[]{:S(2)}) collective-permute-start(bf16[2,6144]{1,0:T(2,128)(2,1)S(1)} %get-tuple-element.6), channel_id=1, source_target_pairs={{0,12},{1,13},{2,14},{3,15},{4,8},{5,9},{6,10},{7,11},{8,4},{9,5},... | collective-permute-start | bytes 73736 | tf_op jit(solution)/shard_map/ppermute | solution.py:36
  61.2 1.8 %collective-permute-start.8 = (bf16[2,6144]{1,0:T(2,128)(2,1)S(1)}, bf16[2,6144]{1,0:T(2,128)(2,1)S(1)}, u32[]{:S(2)}, u32[]{:S(2)}) collective-permute-start(bf16[2,6144]{1,0:T(2,128)(2,1)S(1)} %get-tuple-element.7), channel_id=1, source_target_pairs={{0,8},{1,9},{2,10},{3,11},{4,12},{5,13},{6,14},{7,15},{8,0},{9,1},... | collective-permute-start | bytes 73736 | tf_op jit(solution)/shard_map/ppermute | solution.py:36
  63.0 2.7 %convolution_convert_fusion.1 = bf16[12288,128]{1,0:T(8,128)(2,1)} fusion(bf16[32,12288]{1,0:T(8,128)(2,1)S(1)} %copy-done.2, bf16[32,128]{1,0:T(8,128)(2,1)S(1)} %fusion.3), kind=kOutput, calls=%fused_computation.1 | convolution fusion | flops 102236160 | bytes 3940352 | tf_op jit(solution)/shard_map/dot_general | solution.py:80
  66.0 0.7 copy.10
  (39 shorter events, 1.1 us)
Async XLA Ops:
  0.6 40.8 %copy-start = (bf16[12288,128]{1,0:T(8,128)(2,1)S(1)}, bf16[12288,128]{1,0:T(8,128)(2,1)}, u32[]{:S(2)}) copy-start(bf16[12288,128]{1,0:T(8,128)(2,1)} %param.11) | copy-start | bytes 9437188
  2.6 7.9 %collective-permute-start.2 = (bf16[2,18432]{1,0:T(2,128)(2,1)S(1)}, bf16[2,18432]{1,0:T(2,128)(2,1)S(1)}, u32[]{:S(2)}, u32[]{:S(2)}) collective-permute-start(bf16[2,18432]{1,0:T(2,128)(2,1)S(1)} %constant_dynamic-update-slice_fusion), channel_id=1, source_target_pairs={{0,12},{1,13},{2,14},{3,15},{4,8},{5,9},{6,10},{7,11},{8,4},{9,5},... | collective-permute-start | bytes 221192 | tf_op jit(solution)/shard_map/ppermute | solution.py:28
  7.7 6.2 %collective-permute-start.1 = (bf16[2,18432]{1,0:T(2,128)(2,1)S(1)}, bf16[2,18432]{1,0:T(2,128)(2,1)S(1)}, u32[]{:S(2)}, u32[]{:S(2)}) collective-permute-start(bf16[2,18432]{1,0:T(2,128)(2,1)S(1)} %constant_dynamic-update-slice_fusion), channel_id=1, source_target_pairs={{0,8},{1,9},{2,10},{3,11},{4,12},{5,13},{6,14},{7,15},{8,0},{9,1},... | collective-permute-start | bytes 221192 | tf_op jit(solution)/shard_map/ppermute | solution.py:28
  7.7 6.2 %collective-permute-start = (bf16[2,18432]{1,0:T(2,128)(2,1)S(1)}, bf16[2,18432]{1,0:T(2,128)(2,1)S(1)}, u32[]{:S(2)}, u32[]{:S(2)}) collective-permute-start(bf16[2,18432]{1,0:T(2,128)(2,1)S(1)} %constant_dynamic-update-slice_fusion), channel_id=1, source_target_pairs={{0,4},{1,5},{2,6},{3,7},{4,0},{5,1},{6,2},{7,3},{8,12},{9,13},{10,... | collective-permute-start | bytes 221192 | tf_op jit(solution)/shard_map/ppermute | solution.py:28
  10.5 3.5 %copy-start.4 = (bf16[2,18432]{1,0:T(2,128)(2,1)}, bf16[2,18432]{1,0:T(2,128)(2,1)S(1)}, u32[]{:S(2)}) copy-start(bf16[2,18432]{1,0:T(2,128)(2,1)S(1)} %collective-permute-done.2) | copy-start | bytes 221188
  14.0 1.1 %copy-start.5 = (bf16[2,18432]{1,0:T(2,128)(2,1)}, bf16[2,18432]{1,0:T(2,128)(2,1)S(1)}, u32[]{:S(2)}) copy-start(bf16[2,18432]{1,0:T(2,128)(2,1)S(1)} %collective-permute-done.1) | copy-start | bytes 221188
  14.0 2.6 %copy-start.6 = (bf16[2,18432]{1,0:T(2,128)(2,1)}, bf16[2,18432]{1,0:T(2,128)(2,1)S(1)}, u32[]{:S(2)}) copy-start(bf16[2,18432]{1,0:T(2,128)(2,1)S(1)} %collective-permute-done) | copy-start | bytes 221188
  15.0 8.6 %collective-permute-start.3 = (bf16[8,18432]{1,0:T(8,128)(2,1)}, bf16[8,18432]{1,0:T(8,128)(2,1)S(1)}, u32[]{:S(2)}, u32[]{:S(2)}) collective-permute-start(bf16[8,18432]{1,0:T(8,128)(2,1)} %pad_maximum_fusion), channel_id=1, source_target_pairs={{0,2},{1,3},{2,0},{3,1},{4,6},{5,7},{6,4},{7,5},{8,10},{9,11},{10,... | collective-permute-start | bytes 884744 | tf_op jit(solution)/shard_map/ppermute | solution.py:28
  27.4 2.3 %collective-permute-start.4 = (bf16[16,18432]{1,0:T(8,128)(2,1)}, bf16[16,18432]{1,0:T(8,128)(2,1)}, u32[]{:S(2)}, u32[]{:S(2)}) collective-permute-start(bf16[16,18432]{1,0:T(8,128)(2,1)} %concatenate.16), channel_id=1, source_target_pairs={{0,1},{1,0},{2,3},{3,2},{4,5},{5,4},{6,7},{7,6},{8,9},{9,8},{10,11... | collective-permute-start | bytes 1769480 | tf_op jit(solution)/shard_map/ppermute | solution.py:28
  39.6 2.4 %copy-start.9 = (bf16[32,128]{1,0:T(8,128)(2,1)S(1)}, bf16[32,128]{1,0:T(8,128)(2,1)}, u32[]{:S(2)}) copy-start(bf16[32,128]{1,0:T(8,128)(2,1)} %param.10) | copy-start | bytes 24580
  39.6 2.7 %copy-start.3 = (bf16[12288,128]{1,0:T(8,128)(2,1)S(1)}, bf16[12288,128]{1,0:T(8,128)(2,1)}, u32[]{:S(2)}) copy-start(bf16[12288,128]{1,0:T(8,128)(2,1)} %param.12) | copy-start | bytes 9437188
  41.4 0.9 %copy-start.1 = (bf16[32,12288]{1,0:T(8,128)(2,1)}, bf16[32,12288]{1,0:T(8,128)(2,1)S(1)}, u32[]{:S(2)}) copy-start(bf16[32,12288]{1,0:T(8,128)(2,1)S(1)} %fusion) | copy-start | bytes 2359300
  42.2 2.6 %copy-start.7 = (bf16[32,128]{1,0:T(8,128)(2,1)}, bf16[32,128]{1,0:T(8,128)(2,1)S(1)}, u32[]{:S(2)}) copy-start(bf16[32,128]{1,0:T(8,128)(2,1)S(1)} %get-tuple-element.10) | copy-start | bytes 24580
  48.8 6.7 %copy-start.8 = (bf16[32,128]{1,0:T(8,128)(2,1)S(1)}, bf16[32,128]{1,0:T(8,128)(2,1)}, u32[]{:S(2)}) copy-start(bf16[32,128]{1,0:T(8,128)(2,1)} %copy-done.7) | copy-start | bytes 24580
  50.5 2.0 %collective-permute-start.5 = (bf16[16,6144]{1,0:T(8,128)(2,1)}, bf16[16,6144]{1,0:T(8,128)(2,1)}, u32[]{:S(2)}, u32[]{:S(2)}) collective-permute-start(bf16[16,6144]{1,0:T(8,128)(2,1)} %convert_element_type.64), channel_id=1, source_target_pairs={{0,1},{1,0},{2,3},{3,2},{4,5},{5,4},{6,7},{7,6},{8,9},{9,8},{10,11... | collective-permute-start | bytes 589832 | tf_op jit(solution)/shard_map/ppermute | solution.py:36
  52.5 10.5 %copy-start.2 = (bf16[32,12288]{1,0:T(8,128)(2,1)S(1)}, bf16[32,12288]{1,0:T(8,128)(2,1)}, u32[]{:S(2)}) copy-start(bf16[32,12288]{1,0:T(8,128)(2,1)} %copy-done.1) | copy-start | bytes 2359300
  53.7 5.7 %collective-permute-start.6 = (bf16[8,6144]{1,0:T(8,128)(2,1)S(1)}, bf16[8,6144]{1,0:T(8,128)(2,1)S(1)}, u32[]{:S(2)}, u32[]{:S(2)}) collective-permute-start(bf16[8,6144]{1,0:T(8,128)(2,1)S(1)} %slice.74), channel_id=1, source_target_pairs={{0,2},{1,3},{2,0},{3,1},{4,6},{5,7},{6,4},{7,5},{8,10},{9,11},{10,... | collective-permute-start | bytes 294920 | tf_op jit(solution)/shard_map/ppermute | solution.py:36
  59.4 6.3 %collective-permute-start.7 = (bf16[2,6144]{1,0:T(2,128)(2,1)S(1)}, bf16[2,6144]{1,0:T(2,128)(2,1)S(1)}, u32[]{:S(2)}, u32[]{:S(2)}) collective-permute-start(bf16[2,6144]{1,0:T(2,128)(2,1)S(1)} %get-tuple-element.5), channel_id=1, source_target_pairs={{0,4},{1,5},{2,6},{3,7},{4,0},{5,1},{6,2},{7,3},{8,12},{9,13},{10,... | collective-permute-start | bytes 73736 | tf_op jit(solution)/shard_map/ppermute | solution.py:36
  59.5 6.2 %collective-permute-start.9 = (bf16[2,6144]{1,0:T(2,128)(2,1)S(1)}, bf16[2,6144]{1,0:T(2,128)(2,1)S(1)}, u32[]{:S(2)}, u32[]{:S(2)}) collective-permute-start(bf16[2,6144]{1,0:T(2,128)(2,1)S(1)} %get-tuple-element.6), channel_id=1, source_target_pairs={{0,12},{1,13},{2,14},{3,15},{4,8},{5,9},{6,10},{7,11},{8,4},{9,5},... | collective-permute-start | bytes 73736 | tf_op jit(solution)/shard_map/ppermute | solution.py:36
  61.2 4.7 %collective-permute-start.8 = (bf16[2,6144]{1,0:T(2,128)(2,1)S(1)}, bf16[2,6144]{1,0:T(2,128)(2,1)S(1)}, u32[]{:S(2)}, u32[]{:S(2)}) collective-permute-start(bf16[2,6144]{1,0:T(2,128)(2,1)S(1)} %get-tuple-element.7), channel_id=1, source_target_pairs={{0,8},{1,9},{2,10},{3,11},{4,12},{5,13},{6,14},{7,15},{8,0},{9,1},... | collective-permute-start | bytes 73736 | tf_op jit(solution)/shard_map/ppermute | solution.py:36

commit v2 on v0

v2 whole, which is shorter than its diff:
```python
import functools

import jax
import jax.numpy as jnp
from jax import lax
from jax.experimental import pallas as pl
from jax.experimental.pallas import tpu as pltpu
from jax.sharding import PartitionSpec as P

BF = jnp.bfloat16
F32 = jnp.float32
MIB = 1 << 20
VMEM = pl.BlockSpec(memory_space=pltpu.VMEM)
SMEM = pl.BlockSpec(memory_space=pltpu.SMEM)


def factors(count):
    chips = count // 2
    bits = chips.bit_length() - 1
    outer = 1 << ((bits + 1) // 2)
    return outer, chips // outer, 2


def send(x, mask, count):
    return lax.ppermute(x, "blk", [(i, i ^ mask) for i in range(count)])


def slot_owner(slot, me, count):
    outer, inner, _ = factors(count)
    z = slot & (outer - 1)
    rest = slot >> (outer.bit_length() - 1)
    y = rest & (inner - 1)
    core = rest >> (inner.bit_length() - 1)
    return me ^ ((z * inner + y) * 2 + core)


def pack_kernel(parent_ref, token_ref, out_ref):
    width = token_ref.shape[1]
    half = width // 2
    out_ref[:, :width] = token_ref[...]
    row = parent_ref[...].astype(F32)
    out_ref[:, width:] = jnp.concatenate([row[:, :half], row[:, half:]], 0).astype(BF)


def pack(parent_rows, token_rows):
    width = token_rows.shape[1]
    return pl.pallas_call(
        pack_kernel,
        out_shape=jax.ShapeDtypeStruct((2, width * 3 // 2), BF),
        in_specs=[VMEM] * 2,
        out_specs=VMEM,
        compiler_params=pltpu.CompilerParams(vmem_limit_bytes=4 * MIB),
        name="pack",
    )(parent_rows, token_rows)


def forward_kernel(count, columns, me_ref, parent_ref, flow_ref, wg_ref, wu_ref, *refs):
    cols, (x_ref, d_ref, own_ref, out_ref) = refs[:columns], refs[columns:]
    hyp = parent_ref.shape[1]
    width = wg_ref.shape[0]
    half = width // 2
    rows = 2 * count
    me = me_ref[0]

    line = lax.broadcasted_iota(jnp.int32, (hyp, hyp), 0)
    order = slot_owner(line >> 1, me, count) * 2 + (line & 1)
    perm = order == lax.broadcasted_iota(jnp.int32, (hyp, hyp), 1)
    flow = jnp.dot(perm.astype(F32).astype(BF), flow_ref[...], preferred_element_type=F32)
    owner = jnp.sum(jnp.where(perm, parent_ref[...].astype(F32), 0.0), axis=1, keepdims=True)
    pair = lax.broadcasted_iota(jnp.int32, (hyp, rows), 1)
    match = slot_owner(pair >> 1, me, count).astype(F32) == owner
    even = jnp.where(match & ((pair & 1) == 0), 1.0, 0.0).astype(BF)
    odd = jnp.where(match & ((pair & 1) == 1), 1.0, 0.0).astype(BF)
    pick = jnp.concatenate([even, odd], 0)

    step = min(512, half)
    acc = jnp.zeros((hyp, 256), F32)
    for at in range(0, half, step):
        here, there, held = (pl.ds(at + base, step) for base in (0, half, width))
        pairs = jnp.concatenate([c[:, held].astype(F32) for c in cols], 0).astype(BF)
        picked = jnp.dot(pick, pairs, preferred_element_type=F32)
        for base, sel in ((0, here), (half, there)):
            tokens = jnp.concatenate([c[:, sel].astype(F32) for c in cols], 0)
            top = 0 if base == 0 else hyp
            x = (picked[top:top + hyp] + tokens).astype(BF)
            x_ref[:, sel] = x
            w = jnp.concatenate([wg_ref[sel, :], wu_ref[sel, :]], 1)
            acc = acc + jnp.dot(x, w, preferred_element_type=F32)

    gate, up = acc[:, :128], acc[:, 128:]
    sig = 1.0 / (1.0 + jnp.exp(-gate))
    d_gate = (flow * up * sig * (1.0 + gate * (1.0 - sig))).astype(BF)
    d_up = (flow * gate * sig).astype(BF)
    d = jnp.concatenate([d_gate, d_up], 1)
    d_ref[...] = d
    over = (((0,), (0,)), ((), ()))
    sum_even = lax.dot_general(even, d, over, preferred_element_type=F32).astype(BF)
    sum_odd = lax.dot_general(odd, d, over, preferred_element_type=F32).astype(BF)
    back = (((1,), (1,)), ((), ()))
    for at in range(0, half, step):
        here, there = pl.ds(at, step), pl.ds(at + half, step)
        w0 = jnp.concatenate([wg_ref[here, :], wu_ref[here, :]], 1)
        w1 = jnp.concatenate([wg_ref[there, :], wu_ref[there, :]], 1)
        term = lax.dot_general(sum_even, w0, back, preferred_element_type=F32)
        term = term + lax.dot_general(sum_odd, w1, back, preferred_element_type=F32)
        own_ref[:, here] = term[:count]
        out_ref[:, here] = term[count:].astype(BF)


def forward(me, parent, d_hidden, w_gate, w_up, columns, count):
    width = w_gate.shape[0]
    hyp = parent.shape[0]
    return pl.pallas_call(
        functools.partial(forward_kernel, count, len(columns)),
        out_shape=(
            jax.ShapeDtypeStruct((hyp, width), BF),
            jax.ShapeDtypeStruct((hyp, 256), BF),
            jax.ShapeDtypeStruct((count, width // 2), F32),
            jax.ShapeDtypeStruct((count, width // 2), BF),
        ),
        in_specs=[SMEM] + [VMEM] * (4 + len(columns)),
        out_specs=(VMEM,) * 4,
        compiler_params=pltpu.CompilerParams(vmem_limit_bytes=48 * MIB if count > 16 else 24 * MIB),
        cost_estimate=pl.CostEstimate(flops=8 * hyp * width * 128, bytes_accessed=4 * width * 128, transcendentals=hyp * 128),
        name="forward",
    )(me, parent.reshape(1, hyp), d_hidden, w_gate, w_up, *columns)


def weight_kernel(x_ref, d_ref, gate_ref, up_ref):
    over = (((0,), (0,)), ((), ()))
    term = lax.dot_general(x_ref[...], d_ref[...], over, preferred_element_type=F32)
    gate_ref[...] = term[:, :128].astype(BF)
    up_ref[...] = term[:, 128:].astype(BF)


def weight_terms(x, d):
    hyp, width = x.shape
    tile = 1024
    shape = jax.ShapeDtypeStruct((width, 128), BF)
    return pl.pallas_call(
        weight_kernel,
        grid=(width // tile,),
        out_shape=(shape, shape),
        in_specs=[pl.BlockSpec((hyp, tile), lambda i: (0, i)), pl.BlockSpec((hyp, 256), lambda i: (0, 0))],
        out_specs=(pl.BlockSpec((tile, 128), lambda i: (i, 0)),) * 2,
        compiler_params=pltpu.CompilerParams(vmem_limit_bytes=16 * MIB),
        cost_estimate=pl.CostEstimate(flops=4 * hyp * width * 128, bytes_accessed=4 * width * 128, transcendentals=0),
        name="weight_terms",
    )(x, d)


def body(parent_rows, token_rows, parent, d_hidden, w_gate, w_up):
    count = lax.axis_size("blk")
    outer, inner, _ = factors(count)
    width = token_rows.shape[1]
    me = lax.axis_index("blk").reshape(1)

    block = pack(parent_rows, token_rows)
    column = jnp.concatenate([block] + [send(block, z * inner * 2, count) for z in range(1, outer)], 0)
    plane = [column] + [send(column, y * 2, count) for y in range(1, inner)]
    columns = plane + [send(c, 1, count) for c in plane]

    x, d, own, other = forward(me, parent, d_hidden, w_gate, w_up, columns, count)
    total = own + send(other, 1, count).astype(F32)
    step = outer * 2
    rows = total[:step]
    for y in range(1, inner):
        rows = rows + send(total[y * step:(y + 1) * step].astype(BF), y * 2, count).astype(F32)
    mine = rows[:2]
    for z in range(1, outer):
        mine = mine + send(rows[2 * z:2 * z + 2].astype(BF), z * inner * 2, count).astype(F32)
    grad_gate, grad_up = weight_terms(x, d)
    return grad_gate, grad_up, mine.astype(BF).reshape(1, width)


def solution(mesh):
    in_specs = (
        P(("grp", "blk"), None),
        P(("grp", "blk"), None),
        P("grp"),
        P("grp", "blk"),
        P(None, "blk"),
        P(None, "blk"),
    )
    out_specs = (P(None, ("grp", "blk")), P(None, ("grp", "blk")), P(("grp", "blk"), None))
    return jax.shard_map(body, mesh=mesh, in_specs=in_specs, out_specs=out_specs, check_vma=False)
```

time: 142 us -> 51.8 us (0.36)
  blocking collectives: 115 us -> 0 us
  waiting for transfers between devices: 0 us -> 18.4 us
  matrix products: 13.6 us -> 0 us
  starting transfers between devices: 0 us -> 12.9 us
  Pallas kernels: 0 us -> 11.5 us
  other arithmetic: 3.33 us -> 0.45 us
    unnamed x1 -> x0, blocking collectives: 68.4 us -> none
    all_gather x2 -> x0, blocking collectives: 46.9 us -> none  [the longest x1 25.7 us: body(): lax.all_gather(parent_rows, 'blk', axis=0, tiled=True)]
    ppermute x0 -> x11, waiting for transfers between devices: none -> 18.4 us  [send(): return lax.ppermute(x, 'blk', [(i, i ^ mask) for i in range(count)])]
    dot_general x6 -> x0, matrix products: 13.6 us -> none  [the longest x1 3.99 us: body(): lax.dot_general(parent_up, w_up, contract, preferred_element_type=jnp.flo...]
    ppermute x0 -> x11, starting transfers between devices: none -> 12.9 us  [send(): return lax.ppermute(x, 'blk', [(i, i ^ mask) for i in range(count)])]
    pallas_call x0 -> x3, Pallas kernels: none -> 11.5 us  [the longest x1 7.03 us: weight_terms(): pl.pallas_call(weight_kernel, grid=(width // tile,), out_shape=(shape, sh...]
    unnamed x18 -> x13, local copies, waits for them, and re-layouts: 2.1 us -> 7.38 us
    convert_element_type x2 -> x0, local copies, waits for them, and re-layouts: 4.32 us -> none  [the longest x1 3.02 us: forward_rows(): inputs = (picked + tokens.astype(jnp.float32)).astype(jnp.bfloat16)]
  transfers between devices with their start and end apart: 0 -> 11, of which waited for: 0 -> 6; matrix products, arithmetic and copies ran while one was open for 0% -> 0% of each run, Pallas kernels for 0% -> 14%
where the time goes in v2:
time: 51.8 us; the launch traced here: 51.4 us
  waiting for transfers between devices  18.4 us (36%)
  starting transfers between devices  12.9 us (25%)
  Pallas kernels  11.5 us (22%)
  local copies, waits for them, and re-layouts  7.46 us (14%)
  between operations  0.69 us (1%)
    ppermute x11, waiting for transfers between devices, send(): return lax.ppermute(x, 'blk', [(i, i ^ mask) for i in range(count)])  18.4 us
    ppermute x11, starting transfers between devices, send(): return lax.ppermute(x, 'blk', [(i, i ^ mask) for i in range(count)])  12.9 us
    unnamed x13, local copies, waits for them, and re-layouts  7.38 us
    pallas_call x1, Pallas kernels, weight_terms(): pl.pallas_call(weight_kernel, grid=(width // tile,), out_shape=(shape, sh...  7.03 us
    pallas_call x1, Pallas kernels, forward(): pl.pallas_call(functools.partial(forward_kernel, count, len(columns)), ou...  4.45 us
  transfers between devices with their start and end apart: 11, of which 6 were waited for; matrix products, arithmetic and copies ran while one was open for 0% of the time, Pallas kernels for 14%

profile of v2, /device:TPU:0, one launch (start us, length us, event | category | flops | bytes accessed | tf_op | source)
XLA Modules:
  0.0 51.4 jit_solution(13016281302651368197)
XLA Ops:
  0.6 0.8 %copy-done.2 = bf16[1,12288]{1,0:T(2,128)(2,1)S(1)} copy-done((bf16[1,12288]{1,0:T(2,128)(2,1)S(1)}, bf16[1,12288]{1,0:T(2,128)(2,1)}, u32[]{:S(2)}) %copy-start.2) | copy-done | bytes 24600
  1.4 0.8 %copy-done.3 = bf16[2,12288]{1,0:T(2,128)(2,1)S(1)} copy-done((bf16[2,12288]{1,0:T(2,128)(2,1)S(1)}, bf16[2,12288]{1,0:T(2,128)(2,1)}, u32[]{:S(2)}) %copy-start.3) | copy-done | bytes 49176
  2.3 5.1 %collective-permute-start.2 = (bf16[2,18432]{1,0:T(2,128)(2,1)S(1)}, bf16[2,18432]{1,0:T(2,128)(2,1)S(1)}, u32[]{:S(2)}, u32[]{:S(2)}) collective-permute-start(bf16[2,18432]{1,0:T(2,128)(2,1)S(1)} %pack.1), channel_id=1, source_target_pairs={{0,12},{1,13},{2,14},{3,15},{4,8},{5,9},{6,10},{7,11},{8,4},{9,5},... | collective-permute-start | bytes 221192 | tf_op jit(solution)/shard_map/ppermute | solution.py:25
  7.4 0.0 collective-permute-start.1
  7.4 0.6 %collective-permute-start = (bf16[2,18432]{1,0:T(2,128)(2,1)S(1)}, bf16[2,18432]{1,0:T(2,128)(2,1)S(1)}, u32[]{:S(2)}, u32[]{:S(2)}) collective-permute-start(bf16[2,18432]{1,0:T(2,128)(2,1)S(1)} %pack.1), channel_id=1, source_target_pairs={{0,4},{1,5},{2,6},{3,7},{4,0},{5,1},{6,2},{7,3},{8,12},{9,13},{10,... | collective-permute-start | bytes 221192 | tf_op jit(solution)/shard_map/ppermute | solution.py:25
  8.0 2.1 %collective-permute-done.2 = bf16[2,18432]{1,0:T(2,128)(2,1)S(1)} collective-permute-done((bf16[2,18432]{1,0:T(2,128)(2,1)S(1)}, bf16[2,18432]{1,0:T(2,128)(2,1)S(1)}, u32[]{:S(2)}, u32[]{:S(2)}) %collective-permute-start.2) | collective-permute-done | bytes 73760 | tf_op jit(solution)/shard_map/ppermute | solution.py:25
  10.1 3.5 %collective-permute-done.1 = bf16[2,18432]{1,0:T(2,128)(2,1)S(1)} collective-permute-done((bf16[2,18432]{1,0:T(2,128)(2,1)S(1)}, bf16[2,18432]{1,0:T(2,128)(2,1)S(1)}, u32[]{:S(2)}, u32[]{:S(2)}) %collective-permute-start.1) | collective-permute-done | bytes 73760 | tf_op jit(solution)/shard_map/ppermute | solution.py:25
  13.6 0.0 collective-permute-done
  13.6 0.3 pad_maximum_fusion.refs_0_
  13.9 1.6 %collective-permute-start.3 = (bf16[8,18432]{1,0:T(8,128)(2,1)S(1)}, bf16[8,18432]{1,0:T(8,128)(2,1)S(1)}, u32[]{:S(2)}, u32[]{:S(2)}) collective-permute-start(bf16[8,18432]{1,0:T(8,128)(2,1)S(1)} %pad_maximum_fusion.refs_0_), channel_id=1, source_target_pairs={{0,2},{1,3},{2,0},{3,1},{4,6},{5,7},{6,4},{7,5},{8,10},{9,11},{10,... | collective-permute-start | bytes 884744 | tf_op jit(solution)/shard_map/ppermute | solution.py:25
  15.5 6.8 %collective-permute-done.3.refs_1_ = bf16[8,18432]{1,0:T(8,128)(2,1)S(1)} collective-permute-done((bf16[8,18432]{1,0:T(8,128)(2,1)S(1)}, bf16[8,18432]{1,0:T(8,128)(2,1)S(1)}, u32[]{:S(2)}, u32[]{:S(2)}) %collective-permute-start.3) | collective-permute-done | bytes 294944 | tf_op jit(solution)/shard_map/ppermute | solution.py:25
  22.4 0.0 collective-permute-start.5
  22.4 0.0 collective-permute-done.4.refs_2_
  22.4 1.6 %collective-permute-done.5.refs_3_ = bf16[8,18432]{1,0:T(8,128)(2,1)S(1)} collective-permute-done((bf16[8,18432]{1,0:T(8,128)(2,1)S(1)}, bf16[8,18432]{1,0:T(8,128)(2,1)S(1)}, u32[]{:S(2)}, u32[]{:S(2)}) %collective-permute-start.5) | collective-permute-done | bytes 294944 | tf_op jit(solution)/shard_map/ppermute | solution.py:25
  23.9 1.9 %copy-done = bf16[12288,128]{1,0:T(8,128)(2,1)S(1)} copy-done((bf16[12288,128]{1,0:T(8,128)(2,1)S(1)}, bf16[12288,128]{1,0:T(8,128)(2,1)}, u32[]{:S(2)}) %copy-start) | copy-done | bytes 3145752
  25.8 1.9 %copy-done.1 = bf16[12288,128]{1,0:T(8,128)(2,1)S(1)} copy-done((bf16[12288,128]{1,0:T(8,128)(2,1)S(1)}, bf16[12288,128]{1,0:T(8,128)(2,1)}, u32[]{:S(2)}) %copy-start.1) | copy-done | bytes 3145752
  27.7 0.7 %copy-done.4 = bf16[32,128]{1,0:T(8,128)(2,1)S(1)} copy-done((bf16[32,128]{1,0:T(8,128)(2,1)S(1)}, bf16[32,128]{1,0:T(8,128)(2,1)}, u32[]{:S(2)}) %copy-start.4) | copy-done | bytes 8216
  28.4 0.7 %copy-done.5 = s32[32]{0:T(128)S(1)} copy-done((s32[32]{0:T(128)S(1)}, s32[32]{0:T(128)}, u32[]{:S(2)}) %copy-start.5) | copy-done | bytes 152
  29.1 4.5 %forward.1 = (bf16[32,12288]{1,0:T(8,128)(2,1)S(1)}, bf16[32,256]{1,0:T(8,128)(2,1)S(1)}, f32[16,6144]{1,0:T(8,128)S(1)}, bf16[16,6144]{1,0:T(8,128)(2,1)S(1)}) custom-call(s32[1]{0:T(128)} %bitcast.me_ref, s32[1,32]{1,0:T(1,128)S(1)} %bitcast.6, bf16[32,128]{1,0:T(8,128)(2,1)S(1)} %copy-done.4, bf16[12288,128]{1,0:T(8,128)(2,1)S(1)} %copy-done, ...), custom_call_target="tpu_custom_call" | custom-call | flops 402653184 | bytes 6291456 | tf_op jit(solution)/shard_map/forward/pallas_call | solution.py:113
  33.5 0.2 collective-permute-start.6
  33.7 1.3 %collective-permute-done.6 = bf16[16,6144]{1,0:T(8,128)(2,1)S(1)} collective-permute-done((bf16[16,6144]{1,0:T(8,128)(2,1)S(1)}, bf16[16,6144]{1,0:T(8,128)(2,1)S(1)}, u32[]{:S(2)}, u32[]{:S(2)}) %collective-permute-start.6) | collective-permute-done | bytes 196640 | tf_op jit(solution)/shard_map/ppermute | solution.py:25
  35.1 1.8 %collective-permute-start.7 = (bf16[8,6144]{1,0:T(8,128)(2,1)S(1)}, bf16[8,6144]{1,0:T(8,128)(2,1)S(1)}, u32[]{:S(2)}, u32[]{:S(2)}) collective-permute-start(bf16[8,6144]{1,0:T(8,128)(2,1)S(1)} %slice.45), channel_id=1, source_target_pairs={{0,2},{1,3},{2,0},{3,1},{4,6},{5,7},{6,4},{7,5},{8,10},{9,11},{10,... | collective-permute-start | bytes 294920 | tf_op jit(solution)/shard_map/ppermute | solution.py:25
  36.9 3.1 %collective-permute-done.7 = bf16[8,6144]{1,0:T(8,128)(2,1)S(1)} collective-permute-done((bf16[8,6144]{1,0:T(8,128)(2,1)S(1)}, bf16[8,6144]{1,0:T(8,128)(2,1)S(1)}, u32[]{:S(2)}, u32[]{:S(2)}) %collective-permute-start.7) | collective-permute-done | bytes 98336 | tf_op jit(solution)/shard_map/ppermute | solution.py:25
  40.0 0.1 fusion.5
  40.1 0.4 collective-permute-start.8
  40.5 1.6 %collective-permute-start.10 = (bf16[2,6144]{1,0:T(2,128)(2,1)S(1)}, bf16[2,6144]{1,0:T(2,128)(2,1)S(1)}, u32[]{:S(2)}, u32[]{:S(2)}) collective-permute-start(bf16[2,6144]{1,0:T(2,128)(2,1)S(1)} %get-tuple-element.18), channel_id=1, source_target_pairs={{0,12},{1,13},{2,14},{3,15},{4,8},{5,9},{6,10},{7,11},{8,4},{9,5},... | collective-permute-start | bytes 73736 | tf_op jit(solution)/shard_map/ppermute | solution.py:25
  42.1 1.6 %collective-permute-start.9 = (bf16[2,6144]{1,0:T(2,128)(2,1)S(1)}, bf16[2,6144]{1,0:T(2,128)(2,1)S(1)}, u32[]{:S(2)}, u32[]{:S(2)}) collective-permute-start(bf16[2,6144]{1,0:T(2,128)(2,1)S(1)} %get-tuple-element.19), channel_id=1, source_target_pairs={{0,8},{1,9},{2,10},{3,11},{4,12},{5,13},{6,14},{7,15},{8,0},{9,1},... | collective-permute-start | bytes 73736 | tf_op jit(solution)/shard_map/ppermute | solution.py:25
  43.6 7.0 %weight_terms.1 = (bf16[12288,128]{1,0:T(8,128)(2,1)}, bf16[12288,128]{1,0:T(8,128)(2,1)}) custom-call(bf16[32,12288]{1,0:T(8,128)(2,1)S(1)} %get-tuple-element.9.x_ref, bf16[32,256]{1,0:T(8,128)(2,1)S(1)} %get-tuple-element.10.d_ref), custom_call_target="tpu_custom_call" | custom-call | flops 201326592 | bytes 6291456 | tf_op jit(solution)/shard_map/weight_terms/pallas_call | solution.py:140
  50.7 0.0 collective-permute-done.10
  50.7 0.0 collective-permute-done.9
  50.7 0.1 fusion.3
  50.7 0.7 %copy.9 = bf16[1,1,2,6144]{3,1,2,0:T(2,128)(2,1)} copy(bf16[1,1,2,6144]{3,2,1,0:T(2,128)(2,1)S(1)} %fusion.3) | data formatting | bytes 49152
  (12 shorter events, 0.1 us)
Async XLA Ops:
  0.6 0.8 %copy-start.2 = (bf16[1,12288]{1,0:T(2,128)(2,1)S(1)}, bf16[1,12288]{1,0:T(2,128)(2,1)}, u32[]{:S(2)}) copy-start(bf16[1,12288]{1,0:T(2,128)(2,1)} %parent_ref.1) | copy-start | bytes 73732
  1.4 0.8 %copy-start.3 = (bf16[2,12288]{1,0:T(2,128)(2,1)S(1)}, bf16[2,12288]{1,0:T(2,128)(2,1)}, u32[]{:S(2)}) copy-start(bf16[2,12288]{1,0:T(2,128)(2,1)} %token_ref.1) | copy-start | bytes 147460
  2.3 7.9 %collective-permute-start.2 = (bf16[2,18432]{1,0:T(2,128)(2,1)S(1)}, bf16[2,18432]{1,0:T(2,128)(2,1)S(1)}, u32[]{:S(2)}, u32[]{:S(2)}) collective-permute-start(bf16[2,18432]{1,0:T(2,128)(2,1)S(1)} %pack.1), channel_id=1, source_target_pairs={{0,12},{1,13},{2,14},{3,15},{4,8},{5,9},{6,10},{7,11},{8,4},{9,5},... | collective-permute-start | bytes 221192 | tf_op jit(solution)/shard_map/ppermute | solution.py:25
  7.4 6.2 %collective-permute-start.1 = (bf16[2,18432]{1,0:T(2,128)(2,1)S(1)}, bf16[2,18432]{1,0:T(2,128)(2,1)S(1)}, u32[]{:S(2)}, u32[]{:S(2)}) collective-permute-start(bf16[2,18432]{1,0:T(2,128)(2,1)S(1)} %pack.1), channel_id=1, source_target_pairs={{0,8},{1,9},{2,10},{3,11},{4,12},{5,13},{6,14},{7,15},{8,0},{9,1},... | collective-permute-start | bytes 221192 | tf_op jit(solution)/shard_map/ppermute | solution.py:25
  7.4 6.2 %collective-permute-start = (bf16[2,18432]{1,0:T(2,128)(2,1)S(1)}, bf16[2,18432]{1,0:T(2,128)(2,1)S(1)}, u32[]{:S(2)}, u32[]{:S(2)}) collective-permute-start(bf16[2,18432]{1,0:T(2,128)(2,1)S(1)} %pack.1), channel_id=1, source_target_pairs={{0,4},{1,5},{2,6},{3,7},{4,0},{5,1},{6,2},{7,3},{8,12},{9,13},{10,... | collective-permute-start | bytes 221192 | tf_op jit(solution)/shard_map/ppermute | solution.py:25
  13.9 8.4 %collective-permute-start.3 = (bf16[8,18432]{1,0:T(8,128)(2,1)S(1)}, bf16[8,18432]{1,0:T(8,128)(2,1)S(1)}, u32[]{:S(2)}, u32[]{:S(2)}) collective-permute-start(bf16[8,18432]{1,0:T(8,128)(2,1)S(1)} %pad_maximum_fusion.refs_0_), channel_id=1, source_target_pairs={{0,2},{1,3},{2,0},{3,1},{4,6},{5,7},{6,4},{7,5},{8,10},{9,11},{10,... | collective-permute-start | bytes 884744 | tf_op jit(solution)/shard_map/ppermute | solution.py:25
  15.5 6.8 %collective-permute-start.4 = (bf16[8,18432]{1,0:T(8,128)(2,1)S(1)}, bf16[8,18432]{1,0:T(8,128)(2,1)S(1)}, u32[]{:S(2)}, u32[]{:S(2)}) collective-permute-start(bf16[8,18432]{1,0:T(8,128)(2,1)S(1)} %pad_maximum_fusion.refs_0_), channel_id=1, source_target_pairs={{0,1},{1,0},{2,3},{3,2},{4,5},{5,4},{6,7},{7,6},{8,9},{9,8},{10,11... | collective-permute-start | bytes 884744 | tf_op jit(solution)/shard_map/ppermute | solution.py:25
  22.4 1.6 %collective-permute-start.5 = (bf16[8,18432]{1,0:T(8,128)(2,1)S(1)}, bf16[8,18432]{1,0:T(8,128)(2,1)S(1)}, u32[]{:S(2)}, u32[]{:S(2)}) collective-permute-start(bf16[8,18432]{1,0:T(8,128)(2,1)S(1)} %collective-permute-done.3.refs_1_), channel_id=1, source_target_pairs={{0,1},{1,0},{2,3},{3,2},{4,5},{5,4},{6,7},{7,6},{8,9},{9,8},{10,11... | collective-permute-start | bytes 884744 | tf_op jit(solution)/shard_map/ppermute | solution.py:25
  23.9 1.9 %copy-start = (bf16[12288,128]{1,0:T(8,128)(2,1)S(1)}, bf16[12288,128]{1,0:T(8,128)(2,1)}, u32[]{:S(2)}) copy-start(bf16[12288,128]{1,0:T(8,128)(2,1)} %wg_ref.1) | copy-start | bytes 9437188
  25.8 1.9 %copy-start.1 = (bf16[12288,128]{1,0:T(8,128)(2,1)S(1)}, bf16[12288,128]{1,0:T(8,128)(2,1)}, u32[]{:S(2)}) copy-start(bf16[12288,128]{1,0:T(8,128)(2,1)} %wu_ref.1) | copy-start | bytes 9437188
  27.7 0.7 %copy-start.4 = (bf16[32,128]{1,0:T(8,128)(2,1)S(1)}, bf16[32,128]{1,0:T(8,128)(2,1)}, u32[]{:S(2)}) copy-start(bf16[32,128]{1,0:T(8,128)(2,1)} %flow_ref.1) | copy-start | bytes 24580
  28.4 0.7 %copy-start.5 = (s32[32]{0:T(128)S(1)}, s32[32]{0:T(128)}, u32[]{:S(2)}) copy-start(s32[32]{0:T(128)} %param.8) | copy-start | bytes 388
  33.5 1.5 %collective-permute-start.6 = (bf16[16,6144]{1,0:T(8,128)(2,1)S(1)}, bf16[16,6144]{1,0:T(8,128)(2,1)S(1)}, u32[]{:S(2)}, u32[]{:S(2)}) collective-permute-start(bf16[16,6144]{1,0:T(8,128)(2,1)S(1)} %get-tuple-element.14), channel_id=1, source_target_pairs={{0,1},{1,0},{2,3},{3,2},{4,5},{5,4},{6,7},{7,6},{8,9},{9,8},{10,11... | collective-permute-start | bytes 589832 | tf_op jit(solution)/shard_map/ppermute | solution.py:25
  35.1 4.9 %collective-permute-start.7 = (bf16[8,6144]{1,0:T(8,128)(2,1)S(1)}, bf16[8,6144]{1,0:T(8,128)(2,1)S(1)}, u32[]{:S(2)}, u32[]{:S(2)}) collective-permute-start(bf16[8,6144]{1,0:T(8,128)(2,1)S(1)} %slice.45), channel_id=1, source_target_pairs={{0,2},{1,3},{2,0},{3,1},{4,6},{5,7},{6,4},{7,5},{8,10},{9,11},{10,... | collective-permute-start | bytes 294920 | tf_op jit(solution)/shard_map/ppermute | solution.py:25
  40.1 10.6 %collective-permute-start.8 = (bf16[2,6144]{1,0:T(2,128)(2,1)S(1)}, bf16[2,6144]{1,0:T(2,128)(2,1)S(1)}, u32[]{:S(2)}, u32[]{:S(2)}) collective-permute-start(bf16[2,6144]{1,0:T(2,128)(2,1)S(1)} %get-tuple-element.17), channel_id=1, source_target_pairs={{0,4},{1,5},{2,6},{3,7},{4,0},{5,1},{6,2},{7,3},{8,12},{9,13},{10,... | collective-permute-start | bytes 73736 | tf_op jit(solution)/shard_map/ppermute | solution.py:25
  40.5 10.2 %collective-permute-start.10 = (bf16[2,6144]{1,0:T(2,128)(2,1)S(1)}, bf16[2,6144]{1,0:T(2,128)(2,1)S(1)}, u32[]{:S(2)}, u32[]{:S(2)}) collective-permute-start(bf16[2,6144]{1,0:T(2,128)(2,1)S(1)} %get-tuple-element.18), channel_id=1, source_target_pairs={{0,12},{1,13},{2,14},{3,15},{4,8},{5,9},{6,10},{7,11},{8,4},{9,5},... | collective-permute-start | bytes 73736 | tf_op jit(solution)/shard_map/ppermute | solution.py:25
  42.1 8.6 %collective-permute-start.9 = (bf16[2,6144]{1,0:T(2,128)(2,1)S(1)}, bf16[2,6144]{1,0:T(2,128)(2,1)S(1)}, u32[]{:S(2)}, u32[]{:S(2)}) collective-permute-start(bf16[2,6144]{1,0:T(2,128)(2,1)S(1)} %get-tuple-element.19), channel_id=1, source_target_pairs={{0,8},{1,9},{2,10},{3,11},{4,12},{5,13},{6,14},{7,15},{8,0},{9,1},... | collective-permute-start | bytes 73736 | tf_op jit(solution)/shard_map/ppermute | solution.py:25

commit v3 on v2

v3 whole, which is shorter than its diff:
```python
import functools

import jax
import jax.numpy as jnp
from jax import lax
from jax.experimental import pallas as pl
from jax.experimental.pallas import tpu as pltpu
from jax.sharding import PartitionSpec as P

BF = jnp.bfloat16
F32 = jnp.float32
MIB = 1 << 20
VMEM = pl.BlockSpec(memory_space=pltpu.VMEM)
HBM = pl.BlockSpec(memory_space=pltpu.HBM)
SMEM = pl.BlockSpec(memory_space=pltpu.SMEM)


def factors(count):
    chips = count // 2
    bits = chips.bit_length() - 1
    outer = 1 << ((bits + 1) // 2)
    return outer, chips // outer, 2


def send(x, mask, count):
    return lax.ppermute(x, "blk", [(i, i ^ mask) for i in range(count)])


def slot_owner(slot, me, count):
    outer, inner, _ = factors(count)
    z = slot & (outer - 1)
    rest = slot >> (outer.bit_length() - 1)
    y = rest & (inner - 1)
    core = rest >> (inner.bit_length() - 1)
    return me ^ ((z * inner + y) * 2 + core)


def pack_kernel(parent_ref, token_ref, out_ref, parent_buf, token_buf, sems):
    width = token_ref.shape[1]
    half = width // 2
    copies = [
        pltpu.make_async_copy(parent_ref, parent_buf, sems.at[0]),
        pltpu.make_async_copy(token_ref, token_buf, sems.at[1]),
    ]
    for copy in copies:
        copy.start()
    for copy in copies:
        copy.wait()
    out_ref[:, :width] = token_buf[...]
    row = parent_buf[...].astype(F32)
    out_ref[:, width:] = jnp.concatenate([row[:, :half], row[:, half:]], 0).astype(BF)


def pack(parent_rows, token_rows):
    width = token_rows.shape[1]
    return pl.pallas_call(
        pack_kernel,
        out_shape=jax.ShapeDtypeStruct((2, width * 3 // 2), BF),
        in_specs=[HBM] * 2,
        out_specs=VMEM,
        scratch_shapes=[
            pltpu.VMEM((1, width), BF),
            pltpu.VMEM((2, width), BF),
            pltpu.SemaphoreType.DMA((2,)),
        ],
        compiler_params=pltpu.CompilerParams(vmem_limit_bytes=48 * MIB),
        name="pack",
    )(parent_rows, token_rows)


def flip_kernel(w_ref, out_ref, flip_ref):
    out_ref[...] = w_ref[...]
    flip_ref[...] = w_ref[...].T


def flip(w):
    return pl.pallas_call(
        flip_kernel,
        out_shape=(jax.ShapeDtypeStruct(w.shape, BF), jax.ShapeDtypeStruct(w.shape[::-1], BF)),
        in_specs=[VMEM],
        out_specs=(VMEM,) * 2,
        compiler_params=pltpu.CompilerParams(vmem_limit_bytes=16 * MIB),
        cost_estimate=pl.CostEstimate(flops=0, bytes_accessed=4 * w.size, transcendentals=0),
        name="flip",
    )(w)


def select_kernel(count, me_ref, parent_ref, flow_ref, flow_out, pick_ref, sums_ref):
    hyp = parent_ref.shape[1]
    rows = 2 * count
    me = me_ref[0]
    line = lax.broadcasted_iota(jnp.int32, (hyp, hyp), 0)
    order = slot_owner(line >> 1, me, count) * 2 + (line & 1)
    perm = order == lax.broadcasted_iota(jnp.int32, (hyp, hyp), 1)
    flow_out[...] = jnp.dot(perm.astype(F32).astype(BF), flow_ref[...], preferred_element_type=F32)
    owner = jnp.sum(jnp.where(perm, parent_ref[...].astype(F32), 0.0), axis=1, keepdims=True)
    pair = lax.broadcasted_iota(jnp.int32, (hyp, rows), 1)
    match = slot_owner(pair >> 1, me, count).astype(F32) == owner
    even = jnp.where(match & ((pair & 1) == 0), 1.0, 0.0)
    odd = jnp.where(match & ((pair & 1) == 1), 1.0, 0.0)
    pick_ref[...] = jnp.concatenate([even, odd], 0).astype(BF)
    sums_ref[...] = jnp.concatenate([even.T, odd.T], 0).astype(BF)


def select(me, parent, d_hidden, count):
    hyp = parent.shape[0]
    return pl.pallas_call(
        functools.partial(select_kernel, count),
        out_shape=(
            jax.ShapeDtypeStruct(d_hidden.shape, F32),
            jax.ShapeDtypeStruct((2 * hyp, 2 * count), BF),
            jax.ShapeDtypeStruct((4 * count, hyp), BF),
        ),
        in_specs=[SMEM, VMEM, VMEM],
        out_specs=(VMEM,) * 3,
        compiler_params=pltpu.CompilerParams(vmem_limit_bytes=16 * MIB),
        name="select",
    )(me, parent.reshape(1, hyp), d_hidden)


def forward_kernel(columns, flow_ref, pick_ref, sums_ref, wg_ref, wu_ref, wgt_ref, wut_ref, *refs):
    cols, (x_ref, d_ref, own_ref, out_ref) = refs[:columns], refs[columns:]
    hyp = flow_ref.shape[0]
    width = wg_ref.shape[0]
    half = width // 2
    rows = sums_ref.shape[0] // 2
    count = rows // 2

    step = 1024
    for at in range(0, half, step):
        here, there, held = (pl.ds(at + base, step) for base in (0, half, width))
        pairs = jnp.concatenate([c[:, held].astype(F32) for c in cols], 0).astype(BF)
        picked = jnp.dot(pick_ref[...], pairs, preferred_element_type=F32)
        for top, sel in ((0, here), (hyp, there)):
            tokens = jnp.concatenate([c[:, sel].astype(F32) for c in cols], 0)
            x_ref[:, sel] = (picked[top:top + hyp] + tokens).astype(BF)

    gate = jnp.dot(x_ref[...], wg_ref[...], preferred_element_type=F32)
    up = jnp.dot(x_ref[...], wu_ref[...], preferred_element_type=F32)
    flow = flow_ref[...]
    sig = 1.0 / (1.0 + jnp.exp(-gate))
    d_gate = (flow * up * sig * (1.0 + gate * (1.0 - sig))).astype(BF)
    d_up = (flow * gate * sig).astype(BF)
    d = jnp.concatenate([d_gate, d_up], 1)
    d_ref[...] = d
    sums = jnp.dot(sums_ref[...], d, preferred_element_type=F32).astype(BF)
    for at in range(0, half, step):
        here, there = pl.ds(at, step), pl.ds(at + half, step)
        w0 = jnp.concatenate([wgt_ref[:, here], wut_ref[:, here]], 0)
        w1 = jnp.concatenate([wgt_ref[:, there], wut_ref[:, there]], 0)
        term = jnp.dot(sums[:rows], w0, preferred_element_type=F32)
        term = term + jnp.dot(sums[rows:], w1, preferred_element_type=F32)
        own_ref[:, here] = term[:count]
        out_ref[:, here] = term[count:].astype(BF)


def forward(flow, pick, sums, w_gate, w_up, flip_gate, flip_up, columns):
    width, hidden = w_gate.shape
    hyp = flow.shape[0]
    count = sums.shape[0] // 4
    return pl.pallas_call(
        functools.partial(forward_kernel, len(columns)),
        out_shape=(
            jax.ShapeDtypeStruct((hyp, width), BF),
            jax.ShapeDtypeStruct((hyp, 2 * hidden), BF),
            jax.ShapeDtypeStruct((count, width // 2), F32),
            jax.ShapeDtypeStruct((count, width // 2), BF),
        ),
        in_specs=[VMEM] * (7 + len(columns)),
        out_specs=(VMEM,) * 4,
        compiler_params=pltpu.CompilerParams(vmem_limit_bytes=48 * MIB if count > 16 else 24 * MIB),
        cost_estimate=pl.CostEstimate(flops=8 * hyp * width * hidden, bytes_accessed=8 * width * hidden, transcendentals=hyp * hidden),
        name="forward",
    )(flow, pick, sums, w_gate, w_up, flip_gate, flip_up, *columns)


def weight_kernel(step, x_ref, d_ref, gate_ref, up_ref, gate_buf, up_buf, sems):
    over = (((0,), (0,)), ((), ()))
    hidden = gate_ref.shape[1]
    copies = []
    for i in range(x_ref.shape[1] // step):
        rows = pl.ds(i * step, step)
        term = lax.dot_general(x_ref[:, rows], d_ref[...], over, preferred_element_type=F32)
        gate_buf[rows, :] = term[:, :hidden].astype(BF)
        up_buf[rows, :] = term[:, hidden:].astype(BF)
        for j, (buf, ref) in enumerate(((gate_buf, gate_ref), (up_buf, up_ref))):
            copies.append(pltpu.make_async_copy(buf.at[rows], ref.at[rows], sems.at[2 * i + j]))
            copies[-1].start()
    for copy in copies:
        copy.wait()


def weight_terms(x, d):
    hyp, width = x.shape
    hidden = d.shape[1] // 2
    step = 1024
    shape = jax.ShapeDtypeStruct((width, hidden), BF)
    return pl.pallas_call(
        functools.partial(weight_kernel, step),
        out_shape=(shape, shape),
        in_specs=[VMEM] * 2,
        out_specs=(HBM,) * 2,
        scratch_shapes=[
            pltpu.VMEM((width, hidden), BF),
            pltpu.VMEM((width, hidden), BF),
            pltpu.SemaphoreType.DMA((2 * (width // step),)),
        ],
        compiler_params=pltpu.CompilerParams(vmem_limit_bytes=24 * MIB),
        cost_estimate=pl.CostEstimate(flops=4 * hyp * width * hidden, bytes_accessed=4 * width * hidden, transcendentals=0),
        name="weight_terms",
    )(x, d)


def body(parent_rows, token_rows, parent, d_hidden, w_gate, w_up):
    count = lax.axis_size("blk")
    outer, inner, _ = factors(count)
    width = token_rows.shape[1]
    me = lax.axis_index("blk").reshape(1)

    block = pack(parent_rows, token_rows)
    column = jnp.concatenate([block] + [send(block, z * inner * 2, count) for z in range(1, outer)], 0)
    plane = [column] + [send(column, y * 2, count) for y in range(1, inner)]
    ready = (select(me, parent, d_hidden, count), flip(w_gate), flip(w_up))
    plane[-1], ready = lax.optimization_barrier((plane[-1], ready))
    columns = plane + [send(c, 1, count) for c in plane]

    (flow, pick, sums), (w_gate, flip_gate), (w_up, flip_up) = ready
    x, d, own, other = forward(flow, pick, sums, w_gate, w_up, flip_gate, flip_up, columns)
    total = own + send(other, 1, count).astype(F32)
    step = outer * 2
    rows = total[:step]
    for y in range(1, inner):
        rows = rows + send(total[y * step:(y + 1) * step].astype(BF), y * 2, count).astype(F32)
    rows, grads = lax.optimization_barrier((rows, weight_terms(x, d)))
    mine = rows[:2]
    for z in range(1, outer):
        mine = mine + send(rows[2 * z:2 * z + 2].astype(BF), z * inner * 2, count).astype(F32)
    return *grads, mine.astype(BF).reshape(1, width)


def solution(mesh):
    in_specs = (
        P(("grp", "blk"), None),
        P(("grp", "blk"), None),
        P("grp"),
        P("grp", "blk"),
        P(None, "blk"),
        P(None, "blk"),
    )
    out_specs = (P(None, ("grp", "blk")), P(None, ("grp", "blk")), P(("grp", "blk"), None))
    return jax.shard_map(body, mesh=mesh, in_specs=in_specs, out_specs=out_specs, check_vma=False)
```

time: 51.8 us -> 40.8 us (0.79)
  waiting for transfers between devices: 18.4 us -> 13.2 us
  Pallas kernels: 11.5 us -> 8.07 us
  local copies, waits for them, and re-layouts: 7.46 us -> 5.1 us
    ppermute x11, waiting for transfers between devices: 18.4 us -> 13.2 us  [send(): return lax.ppermute(x, 'blk', [(i, i ^ mask) for i in range(count)])]
    pallas_call x2 -> x5, Pallas kernels: 11.5 us -> 7.92 us  [the longest x1 3.32 us: weight_terms(): pl.pallas_call(functools.partial(weight_kernel, step), out_shape=(shape,...]
    unnamed x13, local copies, waits for them, and re-layouts: 7.38 us -> 5.02 us
  transfers between devices with their start and end apart: 11 -> 11, of which waited for: 6 -> 8; matrix products, arithmetic and copies ran while one was open for 0% -> 0% of each run, Pallas kernels for 14% -> 14%
where the time goes in v3:
time: 40.8 us; the launch traced here: 40.5 us
  waiting for transfers between devices  13.2 us (32%)
  starting transfers between devices  12.9 us (32%)
  Pallas kernels  8.07 us (20%)
  local copies, waits for them, and re-layouts  5.1 us (12%)
  between operations  0.76 us (2%)
  other arithmetic  0.46 us (1%)
    ppermute x11, waiting for transfers between devices, send(): return lax.ppermute(x, 'blk', [(i, i ^ mask) for i in range(count)])  13.2 us
    ppermute x11, starting transfers between devices, send(): return lax.ppermute(x, 'blk', [(i, i ^ mask) for i in range(count)])  12.9 us
    unnamed x13, local copies, waits for them, and re-layouts  5.02 us
    pallas_call x1, Pallas kernels, weight_terms(): pl.pallas_call(functools.partial(weight_kernel, step), out_shape=(shape,...  3.32 us
    pallas_call x1, Pallas kernels, forward(): pl.pallas_call(functools.partial(forward_kernel, len(columns)), out_shape...  2.44 us
    pallas_call x2, Pallas kernels, flip(): pl.pallas_call(flip_kernel, out_shape=(jax.ShapeDtypeStruct(w.shape, BF),...  2 us
  transfers between devices with their start and end apart: 11, of which 8 were waited for; matrix products, arithmetic and copies ran while one was open for 0% of the time, Pallas kernels for 14%

profile of v3, /device:TPU:0, one launch (start us, length us, event | category | flops | bytes accessed | tf_op | source)
XLA Modules:
  0.0 40.5 jit_solution(14131569790580379248)
XLA Ops:
  0.6 0.8 %copy-done.2 = bf16[1,12288]{1,0:T(2,128)(2,1)S(1)} copy-done((bf16[1,12288]{1,0:T(2,128)(2,1)S(1)}, bf16[1,12288]{1,0:T(2,128)(2,1)}, u32[]{:S(2)}) %copy-start.2) | copy-done | bytes 24600
  1.4 0.8 %copy-done.3 = bf16[2,12288]{1,0:T(2,128)(2,1)S(1)} copy-done((bf16[2,12288]{1,0:T(2,128)(2,1)S(1)}, bf16[2,12288]{1,0:T(2,128)(2,1)}, u32[]{:S(2)}) %copy-start.3) | copy-done | bytes 49176
  2.2 0.2 pack.1
  2.4 5.1 %collective-permute-start.2 = (bf16[2,18432]{1,0:T(2,128)(2,1)S(1)}, bf16[2,18432]{1,0:T(2,128)(2,1)S(1)}, u32[]{:S(2)}, u32[]{:S(2)}) collective-permute-start(bf16[2,18432]{1,0:T(2,128)(2,1)S(1)} %pack.1), channel_id=1, source_target_pairs={{0,12},{1,13},{2,14},{3,15},{4,8},{5,9},{6,10},{7,11},{8,4},{9,5},... | collective-permute-start | bytes 221192 | tf_op jit(solution)/shard_map/ppermute | solution.py:26
  7.5 0.0 collective-permute-start.1
  7.5 0.6 %collective-permute-start = (bf16[2,18432]{1,0:T(2,128)(2,1)S(1)}, bf16[2,18432]{1,0:T(2,128)(2,1)S(1)}, u32[]{:S(2)}, u32[]{:S(2)}) collective-permute-start(bf16[2,18432]{1,0:T(2,128)(2,1)S(1)} %pack.1), channel_id=1, source_target_pairs={{0,4},{1,5},{2,6},{3,7},{4,0},{5,1},{6,2},{7,3},{8,12},{9,13},{10,... | collective-permute-start | bytes 221192 | tf_op jit(solution)/shard_map/ppermute | solution.py:26
  8.1 2.1 %collective-permute-done.2 = bf16[2,18432]{1,0:T(2,128)(2,1)S(1)} collective-permute-done((bf16[2,18432]{1,0:T(2,128)(2,1)S(1)}, bf16[2,18432]{1,0:T(2,128)(2,1)S(1)}, u32[]{:S(2)}, u32[]{:S(2)}) %collective-permute-start.2) | collective-permute-done | bytes 73760 | tf_op jit(solution)/shard_map/ppermute | solution.py:26
  10.3 3.5 %collective-permute-done.1 = bf16[2,18432]{1,0:T(2,128)(2,1)S(1)} collective-permute-done((bf16[2,18432]{1,0:T(2,128)(2,1)S(1)}, bf16[2,18432]{1,0:T(2,128)(2,1)S(1)}, u32[]{:S(2)}, u32[]{:S(2)}) %collective-permute-start.1) | collective-permute-done | bytes 73760 | tf_op jit(solution)/shard_map/ppermute | solution.py:26
  13.7 0.3 pad_maximum_fusion.refs_0_
  14.1 1.6 %collective-permute-start.3 = (bf16[8,18432]{1,0:T(8,128)(2,1)S(1)}, bf16[8,18432]{1,0:T(8,128)(2,1)S(1)}, u32[]{:S(2)}, u32[]{:S(2)}) collective-permute-start(bf16[8,18432]{1,0:T(8,128)(2,1)S(1)} %pad_maximum_fusion.refs_0_), channel_id=1, source_target_pairs={{0,2},{1,3},{2,0},{3,1},{4,6},{5,7},{6,4},{7,5},{8,10},{9,11},{10,... | collective-permute-start | bytes 884744 | tf_op jit(solution)/shard_map/ppermute | solution.py:26
  15.7 1.9 %copy-done = bf16[12288,128]{1,0:T(8,128)(2,1)S(1)} copy-done((bf16[12288,128]{1,0:T(8,128)(2,1)S(1)}, bf16[12288,128]{1,0:T(8,128)(2,1)}, u32[]{:S(2)}) %copy-start) | copy-done | bytes 3145752
  17.5 1.0 %flip.2 = (bf16[12288,128]{1,0:T(8,128)(2,1)S(1)}, bf16[128,12288]{1,0:T(8,128)(2,1)S(1)}) custom-call(bf16[12288,128]{1,0:T(8,128)(2,1)S(1)} %copy-done), custom_call_target="tpu_custom_call" | custom-call | bytes 6291456 | tf_op jit(solution)/shard_map/flip/pallas_call | solution.py:77
  18.6 0.9 %copy-done.1 = bf16[12288,128]{1,0:T(8,128)(2,1)S(1)} copy-done((bf16[12288,128]{1,0:T(8,128)(2,1)S(1)}, bf16[12288,128]{1,0:T(8,128)(2,1)}, u32[]{:S(2)}) %copy-start.1) | copy-done | bytes 3145752
  19.4 1.0 %flip.3 = (bf16[12288,128]{1,0:T(8,128)(2,1)S(1)}, bf16[128,12288]{1,0:T(8,128)(2,1)S(1)}) custom-call(bf16[12288,128]{1,0:T(8,128)(2,1)S(1)} %copy-done.1), custom_call_target="tpu_custom_call" | custom-call | bytes 6291456 | tf_op jit(solution)/shard_map/flip/pallas_call | solution.py:77
  20.5 0.2 select.1
  20.6 0.0 collective-permute-start.4
  20.7 1.8 %collective-permute-done.3.refs_1_ = bf16[8,18432]{1,0:T(8,128)(2,1)S(1)} collective-permute-done((bf16[8,18432]{1,0:T(8,128)(2,1)S(1)}, bf16[8,18432]{1,0:T(8,128)(2,1)S(1)}, u32[]{:S(2)}, u32[]{:S(2)}) %collective-permute-start.3) | collective-permute-done | bytes 294944 | tf_op jit(solution)/shard_map/ppermute | solution.py:26
  22.5 1.6 %collective-permute-done.5.refs_3_ = bf16[8,18432]{1,0:T(8,128)(2,1)S(1)} collective-permute-done((bf16[8,18432]{1,0:T(8,128)(2,1)S(1)}, bf16[8,18432]{1,0:T(8,128)(2,1)S(1)}, u32[]{:S(2)}, u32[]{:S(2)}) %collective-permute-start.5) | collective-permute-done | bytes 294944 | tf_op jit(solution)/shard_map/ppermute | solution.py:26
  24.1 2.4 %forward.1 = (bf16[32,12288]{1,0:T(8,128)(2,1)S(1)}, bf16[32,256]{1,0:T(8,128)(2,1)S(1)}, f32[16,6144]{1,0:T(8,128)S(1)}, bf16[16,6144]{1,0:T(8,128)(2,1)S(1)}) custom-call(f32[32,128]{1,0:T(8,128)S(1)} %get-tuple-element.34.flow_ref, bf16[64,32]{1,0:T(8,128)(2,1)S(1)} %get-tuple-element.35.pick_ref, bf16[64,32]{1,0:T(8,128)(2,1)S(1)} %get-tuple-element.36.sums_ref, ...), custom_call_target="tpu_custom_call" | custom-call | flops 402653184 | bytes 12582912 | tf_op jit(solution)/shard_map/forward/pallas_call | solution.py:161
  26.5 0.2 collective-permute-start.6
  26.7 1.3 %collective-permute-done.6 = bf16[16,6144]{1,0:T(8,128)(2,1)S(1)} collective-permute-done((bf16[16,6144]{1,0:T(8,128)(2,1)S(1)}, bf16[16,6144]{1,0:T(8,128)(2,1)S(1)}, u32[]{:S(2)}, u32[]{:S(2)}) %collective-permute-start.6) | collective-permute-done | bytes 196640 | tf_op jit(solution)/shard_map/ppermute | solution.py:26
  28.1 1.8 %collective-permute-start.7 = (bf16[8,6144]{1,0:T(8,128)(2,1)S(1)}, bf16[8,6144]{1,0:T(8,128)(2,1)S(1)}, u32[]{:S(2)}, u32[]{:S(2)}) collective-permute-start(bf16[8,6144]{1,0:T(8,128)(2,1)S(1)} %slice.38), channel_id=1, source_target_pairs={{0,2},{1,3},{2,0},{3,1},{4,6},{5,7},{6,4},{7,5},{8,10},{9,11},{10,... | collective-permute-start | bytes 294920 | tf_op jit(solution)/shard_map/ppermute | solution.py:26
  29.9 3.3 %weight_terms.1 = (bf16[12288,128]{1,0:T(8,128)(2,1)}, bf16[12288,128]{1,0:T(8,128)(2,1)}) custom-call(bf16[32,12288]{1,0:T(8,128)(2,1)S(1)} %get-tuple-element.44.x_ref, bf16[32,256]{1,0:T(8,128)(2,1)S(1)} %get-tuple-element.45.d_ref), custom_call_target="tpu_custom_call" | custom-call | flops 201326592 | bytes 6291456 | tf_op jit(solution)/shard_map/weight_terms/pallas_call | solution.py:198
  33.2 0.1 fusion.1
  33.3 0.2 collective-permute-start.8
  33.5 1.6 %collective-permute-start.10 = (bf16[2,6144]{1,0:T(2,128)(2,1)S(1)}, bf16[2,6144]{1,0:T(2,128)(2,1)S(1)}, u32[]{:S(2)}, u32[]{:S(2)}) collective-permute-start(bf16[2,6144]{1,0:T(2,128)(2,1)S(1)} %get-tuple-element.52), channel_id=1, source_target_pairs={{0,12},{1,13},{2,14},{3,15},{4,8},{5,9},{6,10},{7,11},{8,4},{9,5},... | collective-permute-start | bytes 73736 | tf_op jit(solution)/shard_map/ppermute | solution.py:26
  35.1 1.8 %collective-permute-start.9 = (bf16[2,6144]{1,0:T(2,128)(2,1)S(1)}, bf16[2,6144]{1,0:T(2,128)(2,1)S(1)}, u32[]{:S(2)}, u32[]{:S(2)}) collective-permute-start(bf16[2,6144]{1,0:T(2,128)(2,1)S(1)} %get-tuple-element.53), channel_id=1, source_target_pairs={{0,8},{1,9},{2,10},{3,11},{4,12},{5,13},{6,14},{7,15},{8,0},{9,1},... | collective-permute-start | bytes 73736 | tf_op jit(solution)/shard_map/ppermute | solution.py:26
  36.9 0.3 collective-permute-done.8
  37.2 1.9 %collective-permute-done.10 = bf16[2,6144]{1,0:T(2,128)(2,1)S(1)} collective-permute-done((bf16[2,6144]{1,0:T(2,128)(2,1)S(1)}, bf16[2,6144]{1,0:T(2,128)(2,1)S(1)}, u32[]{:S(2)}, u32[]{:S(2)}) %collective-permute-start.10) | collective-permute-done | bytes 24608 | tf_op jit(solution)/shard_map/ppermute | solution.py:26
  39.1 0.7 %collective-permute-done.9 = bf16[2,6144]{1,0:T(2,128)(2,1)S(1)} collective-permute-done((bf16[2,6144]{1,0:T(2,128)(2,1)S(1)}, bf16[2,6144]{1,0:T(2,128)(2,1)S(1)}, u32[]{:S(2)}, u32[]{:S(2)}) %collective-permute-start.9) | collective-permute-done | bytes 24608 | tf_op jit(solution)/shard_map/ppermute | solution.py:26
  39.8 0.1 fusion
  39.8 0.7 %copy.9 = bf16[1,1,2,6144]{3,1,2,0:T(2,128)(2,1)} copy(bf16[1,1,2,6144]{3,2,1,0:T(2,128)(2,1)S(1)} %fusion) | data formatting | bytes 49152
  (16 shorter events, 0.1 us)
Async XLA Ops:
  0.6 0.8 %copy-start.2 = (bf16[1,12288]{1,0:T(2,128)(2,1)S(1)}, bf16[1,12288]{1,0:T(2,128)(2,1)}, u32[]{:S(2)}) copy-start(bf16[1,12288]{1,0:T(2,128)(2,1)} %parent_ref.1) | copy-start | bytes 73732
  1.4 0.8 %copy-start.3 = (bf16[2,12288]{1,0:T(2,128)(2,1)S(1)}, bf16[2,12288]{1,0:T(2,128)(2,1)}, u32[]{:S(2)}) copy-start(bf16[2,12288]{1,0:T(2,128)(2,1)} %token_ref.1) | copy-start | bytes 147460
  2.4 7.9 %collective-permute-start.2 = (bf16[2,18432]{1,0:T(2,128)(2,1)S(1)}, bf16[2,18432]{1,0:T(2,128)(2,1)S(1)}, u32[]{:S(2)}, u32[]{:S(2)}) collective-permute-start(bf16[2,18432]{1,0:T(2,128)(2,1)S(1)} %pack.1), channel_id=1, source_target_pairs={{0,12},{1,13},{2,14},{3,15},{4,8},{5,9},{6,10},{7,11},{8,4},{9,5},... | collective-permute-start | bytes 221192 | tf_op jit(solution)/shard_map/ppermute | solution.py:26
  7.5 6.2 %collective-permute-start.1 = (bf16[2,18432]{1,0:T(2,128)(2,1)S(1)}, bf16[2,18432]{1,0:T(2,128)(2,1)S(1)}, u32[]{:S(2)}, u32[]{:S(2)}) collective-permute-start(bf16[2,18432]{1,0:T(2,128)(2,1)S(1)} %pack.1), channel_id=1, source_target_pairs={{0,8},{1,9},{2,10},{3,11},{4,12},{5,13},{6,14},{7,15},{8,0},{9,1},... | collective-permute-start | bytes 221192 | tf_op jit(solution)/shard_map/ppermute | solution.py:26
  7.5 6.2 %collective-permute-start = (bf16[2,18432]{1,0:T(2,128)(2,1)S(1)}, bf16[2,18432]{1,0:T(2,128)(2,1)S(1)}, u32[]{:S(2)}, u32[]{:S(2)}) collective-permute-start(bf16[2,18432]{1,0:T(2,128)(2,1)S(1)} %pack.1), channel_id=1, source_target_pairs={{0,4},{1,5},{2,6},{3,7},{4,0},{5,1},{6,2},{7,3},{8,12},{9,13},{10,... | collective-permute-start | bytes 221192 | tf_op jit(solution)/shard_map/ppermute | solution.py:26
  14.1 8.4 %collective-permute-start.3 = (bf16[8,18432]{1,0:T(8,128)(2,1)S(1)}, bf16[8,18432]{1,0:T(8,128)(2,1)S(1)}, u32[]{:S(2)}, u32[]{:S(2)}) collective-permute-start(bf16[8,18432]{1,0:T(8,128)(2,1)S(1)} %pad_maximum_fusion.refs_0_), channel_id=1, source_target_pairs={{0,2},{1,3},{2,0},{3,1},{4,6},{5,7},{6,4},{7,5},{8,10},{9,11},{10,... | collective-permute-start | bytes 884744 | tf_op jit(solution)/shard_map/ppermute | solution.py:26
  15.7 1.9 %copy-start = (bf16[12288,128]{1,0:T(8,128)(2,1)S(1)}, bf16[12288,128]{1,0:T(8,128)(2,1)}, u32[]{:S(2)}) copy-start(bf16[12288,128]{1,0:T(8,128)(2,1)} %w_ref.2) | copy-start | bytes 9437188
  17.5 1.9 %copy-start.1 = (bf16[12288,128]{1,0:T(8,128)(2,1)S(1)}, bf16[12288,128]{1,0:T(8,128)(2,1)}, u32[]{:S(2)}) copy-start(bf16[12288,128]{1,0:T(8,128)(2,1)} %w_ref.3) | copy-start | bytes 9437188
  17.5 2.9 %copy-start.4 = (bf16[32,128]{1,0:T(8,128)(2,1)S(1)}, bf16[32,128]{1,0:T(8,128)(2,1)}, u32[]{:S(2)}) copy-start(bf16[32,128]{1,0:T(8,128)(2,1)} %flow_ref.1) | copy-start | bytes 24580
  17.5 2.9 %copy-start.5 = (s32[32]{0:T(128)S(1)}, s32[32]{0:T(128)}, u32[]{:S(2)}) copy-start(s32[32]{0:T(128)} %param.8) | copy-start | bytes 388
  20.6 1.9 %collective-permute-start.4 = (bf16[8,18432]{1,0:T(8,128)(2,1)S(1)}, bf16[8,18432]{1,0:T(8,128)(2,1)S(1)}, u32[]{:S(2)}, u32[]{:S(2)}) collective-permute-start(bf16[8,18432]{1,0:T(8,128)(2,1)S(1)} %pad_maximum_fusion.refs_0_), channel_id=1, source_target_pairs={{0,1},{1,0},{2,3},{3,2},{4,5},{5,4},{6,7},{7,6},{8,9},{9,8},{10,11... | collective-permute-start | bytes 884744 | tf_op jit(solution)/shard_map/ppermute | solution.py:26
  22.5 1.6 %collective-permute-start.5 = (bf16[8,18432]{1,0:T(8,128)(2,1)S(1)}, bf16[8,18432]{1,0:T(8,128)(2,1)S(1)}, u32[]{:S(2)}, u32[]{:S(2)}) collective-permute-start(bf16[8,18432]{1,0:T(8,128)(2,1)S(1)} %collective-permute-done.3.refs_1_), channel_id=1, source_target_pairs={{0,1},{1,0},{2,3},{3,2},{4,5},{5,4},{6,7},{7,6},{8,9},{9,8},{10,11... | collective-permute-start | bytes 884744 | tf_op jit(solution)/shard_map/ppermute | solution.py:26
  26.5 1.5 %collective-permute-start.6 = (bf16[16,6144]{1,0:T(8,128)(2,1)S(1)}, bf16[16,6144]{1,0:T(8,128)(2,1)S(1)}, u32[]{:S(2)}, u32[]{:S(2)}) collective-permute-start(bf16[16,6144]{1,0:T(8,128)(2,1)S(1)} %get-tuple-element.43), channel_id=1, source_target_pairs={{0,1},{1,0},{2,3},{3,2},{4,5},{5,4},{6,7},{7,6},{8,9},{9,8},{10,11... | collective-permute-start | bytes 589832 | tf_op jit(solution)/shard_map/ppermute | solution.py:26
  28.1 5.1 %collective-permute-start.7 = (bf16[8,6144]{1,0:T(8,128)(2,1)S(1)}, bf16[8,6144]{1,0:T(8,128)(2,1)S(1)}, u32[]{:S(2)}, u32[]{:S(2)}) collective-permute-start(bf16[8,6144]{1,0:T(8,128)(2,1)S(1)} %slice.38), channel_id=1, source_target_pairs={{0,2},{1,3},{2,0},{3,1},{4,6},{5,7},{6,4},{7,5},{8,10},{9,11},{10,... | collective-permute-start | bytes 294920 | tf_op jit(solution)/shard_map/ppermute | solution.py:26
  33.3 3.9 %collective-permute-start.8 = (bf16[2,6144]{1,0:T(2,128)(2,1)S(1)}, bf16[2,6144]{1,0:T(2,128)(2,1)S(1)}, u32[]{:S(2)}, u32[]{:S(2)}) collective-permute-start(bf16[2,6144]{1,0:T(2,128)(2,1)S(1)} %get-tuple-element.51), channel_id=1, source_target_pairs={{0,4},{1,5},{2,6},{3,7},{4,0},{5,1},{6,2},{7,3},{8,12},{9,13},{10,... | collective-permute-start | bytes 73736 | tf_op jit(solution)/shard_map/ppermute | solution.py:26
  33.5 5.7 %collective-permute-start.10 = (bf16[2,6144]{1,0:T(2,128)(2,1)S(1)}, bf16[2,6144]{1,0:T(2,128)(2,1)S(1)}, u32[]{:S(2)}, u32[]{:S(2)}) collective-permute-start(bf16[2,6144]{1,0:T(2,128)(2,1)S(1)} %get-tuple-element.52), channel_id=1, source_target_pairs={{0,12},{1,13},{2,14},{3,15},{4,8},{5,9},{6,10},{7,11},{8,4},{9,5},... | collective-permute-start | bytes 73736 | tf_op jit(solution)/shard_map/ppermute | solution.py:26
  35.1 4.7 %collective-permute-start.9 = (bf16[2,6144]{1,0:T(2,128)(2,1)S(1)}, bf16[2,6144]{1,0:T(2,128)(2,1)S(1)}, u32[]{:S(2)}, u32[]{:S(2)}) collective-permute-start(bf16[2,6144]{1,0:T(2,128)(2,1)S(1)} %get-tuple-element.53), channel_id=1, source_target_pairs={{0,8},{1,9},{2,10},{3,11},{4,12},{5,13},{6,14},{7,15},{8,0},{9,1},... | collective-permute-start | bytes 73736 | tf_op jit(solution)/shard_map/ppermute | solution.py:26

commit v4 on v3

--- a/solution.py
+++ b/solution.py
@@ -26,13 +26,51 @@
     return lax.ppermute(x, "blk", [(i, i ^ mask) for i in range(count)])
 
 
-def slot_owner(slot, me, count):
-    outer, inner, _ = factors(count)
-    z = slot & (outer - 1)
-    rest = slot >> (outer.bit_length() - 1)
-    y = rest & (inner - 1)
-    core = rest >> (inner.bit_length() - 1)
-    return me ^ ((z * inner + y) * 2 + core)
+def scatter_stages(count):
+    outer, inner, _ = factors(count)
+    z_steps = [(1 << i) * inner * 2 for i in range(outer.bit_length() - 1)]
+    y_steps = [(1 << i) * 2 for i in range(inner.bit_length() - 1)]
+    squares = [[0, z, y, z ^ y] for z, y in zip(z_steps, y_steps)]
+    return [[0, 1]] + squares + [[0, z] for z in z_steps[len(y_steps):]]
+
+
+def scatter_masks(count):
+    masks = [0]
+    for stage in reversed(scatter_stages(count)):
+        masks = [piece ^ m for piece in stage for m in masks]
+    return masks
+
+
+def gather_masks(count):
+    outer, inner, _ = factors(count)
+    if (outer, inner) == (4, 2):
+        chips = [(0, 0), (1, 0), (2, 0), (0, 1), (1, 1), (2, 1), (3, 0), (3, 1)]
+        return [(z * inner + y) * 2 + c for c in range(2) for z, y in chips]
+    return [(z * inner + y) * 2 + c for c in range(2) for y in range(inner) for z in range(outer)]
+
+
+def gather(block, count, beside):
+    outer, inner, _ = factors(count)
+    to = lambda x, z, y: send(x, (z * inner + y) * 2, count)
+    if (outer, inner) == (4, 2):
+        far, near, side = to(block, 2, 0), to(block, 1, 0), to(block, 0, 1)
+        side, near, far = lax.optimization_barrier((side, near, far))
+        corner = to(side, 3, 0)
+        pair = to(jnp.concatenate([near, far], 0), 0, 1)
+        third = to(far, 1, 0)
+        plane = [jnp.concatenate([block, near, far, side], 0), jnp.concatenate([pair, third, corner], 0)]
+    else:
+        column = jnp.concatenate([block] + [to(block, z, 0) for z in range(1, outer)], 0)
+        plane = [column] + [to(column, 0, y) for y in range(1, inner)]
+    plane[-1], beside = lax.optimization_barrier((plane[-1], beside))
+    return plane + [send(p, 1, count) for p in plane], beside
+
+
+def owner_of(slot, me, masks):
+    mask = jnp.zeros_like(slot)
+    for i, m in enumerate(masks):
+        mask = jnp.where(slot == i, m, mask)
+    return me ^ mask
 
 
 def pack_kernel(parent_ref, token_ref, out_ref, parent_buf, token_buf, sems):
@@ -63,7 +101,8 @@
             pltpu.VMEM((2, width), BF),
             pltpu.SemaphoreType.DMA((2,)),
         ],
-        compiler_params=pltpu.CompilerParams(vmem_limit_bytes=48 * MIB),
+        compiler_params=pltpu.CompilerParams(vmem_limit_bytes=4 * MIB),
+        cost_estimate=pl.CostEstimate(flops=1 << 38, bytes_accessed=1024 * MIB, transcendentals=0),
         name="pack",
     )(parent_rows, token_rows)
 
@@ -90,16 +129,18 @@
     rows = 2 * count
     me = me_ref[0]
     line = lax.broadcasted_iota(jnp.int32, (hyp, hyp), 0)
-    order = slot_owner(line >> 1, me, count) * 2 + (line & 1)
+    order = owner_of(line >> 1, me, gather_masks(count)) * 2 + (line & 1)
     perm = order == lax.broadcasted_iota(jnp.int32, (hyp, hyp), 1)
     flow_out[...] = jnp.dot(perm.astype(F32).astype(BF), flow_ref[...], preferred_element_type=F32)
     owner = jnp.sum(jnp.where(perm, parent_ref[...].astype(F32), 0.0), axis=1, keepdims=True)
     pair = lax.broadcasted_iota(jnp.int32, (hyp, rows), 1)
-    match = slot_owner(pair >> 1, me, count).astype(F32) == owner
-    even = jnp.where(match & ((pair & 1) == 0), 1.0, 0.0)
-    odd = jnp.where(match & ((pair & 1) == 1), 1.0, 0.0)
-    pick_ref[...] = jnp.concatenate([even, odd], 0).astype(BF)
-    sums_ref[...] = jnp.concatenate([even.T, odd.T], 0).astype(BF)
+
+    def halves(masks):
+        match = owner_of(pair >> 1, me, masks).astype(F32) == owner
+        return [jnp.where(match & ((pair & 1) == side), 1.0, 0.0) for side in (0, 1)]
+
+    pick_ref[...] = jnp.concatenate(halves(gather_masks(count)), 0).astype(BF)
+    sums_ref[...] = jnp.concatenate([h.T for h in halves(scatter_masks(count))], 0).astype(BF)
 
 
 def select(me, parent, d_hidden, count):
@@ -218,24 +259,20 @@
     me = lax.axis_index("blk").reshape(1)
 
     block = pack(parent_rows, token_rows)
-    column = jnp.concatenate([block] + [send(block, z * inner * 2, count) for z in range(1, outer)], 0)
-    plane = [column] + [send(column, y * 2, count) for y in range(1, inner)]
-    ready = (select(me, parent, d_hidden, count), flip(w_gate), flip(w_up))
-    plane[-1], ready = lax.optimization_barrier((plane[-1], ready))
-    columns = plane + [send(c, 1, count) for c in plane]
-
-    (flow, pick, sums), (w_gate, flip_gate), (w_up, flip_up) = ready
+    beside = (select(me, parent, d_hidden, count), flip(w_gate), flip(w_up))
+    columns, beside = gather(block, count, beside)
+    (flow, pick, sums), (w_gate, flip_gate), (w_up, flip_up) = beside
     x, d, own, other = forward(flow, pick, sums, w_gate, w_up, flip_gate, flip_up, columns)
-    total = own + send(other, 1, count).astype(F32)
-    step = outer * 2
-    rows = total[:step]
-    for y in range(1, inner):
-        rows = rows + send(total[y * step:(y + 1) * step].astype(BF), y * 2, count).astype(F32)
-    rows, grads = lax.optimization_barrier((rows, weight_terms(x, d)))
-    mine = rows[:2]
-    for z in range(1, outer):
-        mine = mine + send(rows[2 * z:2 * z + 2].astype(BF), z * inner * 2, count).astype(F32)
-    return *grads, mine.astype(BF).reshape(1, width)
+    rows = own + send(other, 1, count).astype(F32)
+    for i, stage in enumerate(scatter_stages(count)[1:]):
+        size = rows.shape[0] // len(stage)
+        parts = [rows[j * size:(j + 1) * size] for j in range(len(stage))]
+        rows = parts[0]
+        for mask, part in zip(stage[1:], parts[1:]):
+            rows = rows + send(part.astype(BF), mask, count).astype(F32)
+        if i == 0:
+            rows, weights = lax.optimization_barrier((rows, weight_terms(x, d)))
+    return *weights, rows.astype(BF).reshape(1, width)
 
 
 def solution(mesh):

time: 40.8 us -> 38.6 us (0.946)
  waiting for transfers between devices: 13.2 us -> 8.94 us
  starting transfers between devices: 12.9 us -> 16.5 us
  local copies, waits for them, and re-layouts: 5.1 us -> 3.22 us
  other arithmetic: 0.46 us -> 0.87 us
    ppermute x11 -> x13, waiting for transfers between devices: 13.2 us -> 8.94 us  [send(): return lax.ppermute(x, 'blk', [(i, i ^ mask) for i in range(count)])]
    ppermute x11 -> x13, starting transfers between devices: 12.9 us -> 16.5 us  [send(): return lax.ppermute(x, 'blk', [(i, i ^ mask) for i in range(count)])]
    unnamed x13, local copies, waits for them, and re-layouts: 5.02 us -> 3.13 us
  transfers between devices with their start and end apart: 11 -> 13, of which waited for: 8 -> 8; matrix products, arithmetic and copies ran while one was open for 0% -> 2% of each run, Pallas kernels for 14% -> 14%
where the time goes in v4:
time: 38.6 us; the launch traced here: 38.4 us
  starting transfers between devices  16.5 us (43%)
  waiting for transfers between devices  8.94 us (23%)
  Pallas kernels  8.09 us (21%)
  local copies, waits for them, and re-layouts  3.22 us (8%)
  other arithmetic  0.87 us (2%)
  between operations  0.78 us (2%)
    ppermute x13, starting transfers between devices, send(): return lax.ppermute(x, 'blk', [(i, i ^ mask) for i in range(count)])  16.5 us
    ppermute x13, waiting for transfers between devices, send(): return lax.ppermute(x, 'blk', [(i, i ^ mask) for i in range(count)])  8.94 us
    pallas_call x1, Pallas kernels, weight_terms(): pl.pallas_call(functools.partial(weight_kernel, step), out_shape=(shape,...  3.31 us
    unnamed x13, local copies, waits for them, and re-layouts  3.13 us
    pallas_call x1, Pallas kernels, forward(): pl.pallas_call(functools.partial(forward_kernel, len(columns)), out_shape...  2.44 us
    pallas_call x2, Pallas kernels, flip(): pl.pallas_call(flip_kernel, out_shape=(jax.ShapeDtypeStruct(w.shape, BF),...  2.01 us
  transfers between devices with their start and end apart: 13, of which 8 were waited for; matrix products, arithmetic and copies ran while one was open for 2% of the time, Pallas kernels for 14%

profile of v4, /device:TPU:0, one launch (start us, length us, event | category | flops | bytes accessed | tf_op | source)
XLA Modules:
  0.0 38.4 jit_solution(10980875268898945099)
XLA Ops:
  0.6 0.8 %copy-done.4 = bf16[1,12288]{1,0:T(2,128)(2,1)S(1)} copy-done((bf16[1,12288]{1,0:T(2,128)(2,1)S(1)}, bf16[1,12288]{1,0:T(2,128)(2,1)}, u32[]{:S(2)}) %copy-start.4) | copy-done | bytes 24600
  1.4 0.8 %copy-done.5 = bf16[2,12288]{1,0:T(2,128)(2,1)S(1)} copy-done((bf16[2,12288]{1,0:T(2,128)(2,1)S(1)}, bf16[2,12288]{1,0:T(2,128)(2,1)}, u32[]{:S(2)}) %copy-start.5) | copy-done | bytes 49176
  2.2 0.2 pack.1
  2.4 4.1 %collective-permute-start.2 = (bf16[2,18432]{1,0:T(2,128)(2,1)S(1)}, bf16[2,18432]{1,0:T(2,128)(2,1)S(1)}, u32[]{:S(2)}, u32[]{:S(2)}) collective-permute-start(bf16[2,18432]{1,0:T(2,128)(2,1)S(1)} %pack.1), channel_id=1, source_target_pairs={{0,8},{1,9},{2,10},{3,11},{4,12},{5,13},{6,14},{7,15},{8,0},{9,1},... | collective-permute-start | bytes 221192 | tf_op jit(solution)/shard_map/ppermute | solution.py:26
  6.5 1.6 %collective-permute-start.1 = (bf16[2,18432]{1,0:T(2,128)(2,1)S(1)}, bf16[2,18432]{1,0:T(2,128)(2,1)S(1)}, u32[]{:S(2)}, u32[]{:S(2)}) collective-permute-start(bf16[2,18432]{1,0:T(2,128)(2,1)S(1)} %pack.1), channel_id=1, source_target_pairs={{0,4},{1,5},{2,6},{3,7},{4,0},{5,1},{6,2},{7,3},{8,12},{9,13},{10,... | collective-permute-start | bytes 221192 | tf_op jit(solution)/shard_map/ppermute | solution.py:26
  8.1 1.5 %collective-permute-start = (bf16[2,18432]{1,0:T(2,128)(2,1)S(1)}, bf16[2,18432]{1,0:T(2,128)(2,1)S(1)}, u32[]{:S(2)}, u32[]{:S(2)}) collective-permute-start(bf16[2,18432]{1,0:T(2,128)(2,1)S(1)} %pack.1), channel_id=1, source_target_pairs={{0,2},{1,3},{2,0},{3,1},{4,6},{5,7},{6,4},{7,5},{8,10},{9,11},{10,... | collective-permute-start | bytes 221192 | tf_op jit(solution)/shard_map/ppermute | solution.py:26
  9.6 1.0 %flip.2 = (bf16[12288,128]{1,0:T(8,128)(2,1)S(1)}, bf16[128,12288]{1,0:T(8,128)(2,1)S(1)}) custom-call(bf16[12288,128]{1,0:T(8,128)(2,1)S(1)} %copy-done), custom_call_target="tpu_custom_call" | custom-call | bytes 6291456 | tf_op jit(solution)/shard_map/flip/pallas_call | solution.py:116
  10.6 0.9 %copy-done.1 = bf16[12288,128]{1,0:T(8,128)(2,1)S(1)} copy-done((bf16[12288,128]{1,0:T(8,128)(2,1)S(1)}, bf16[12288,128]{1,0:T(8,128)(2,1)}, u32[]{:S(2)}) %copy-start.1) | copy-done | bytes 3145752
  11.5 1.0 %flip.3 = (bf16[12288,128]{1,0:T(8,128)(2,1)S(1)}, bf16[128,12288]{1,0:T(8,128)(2,1)S(1)}) custom-call(bf16[12288,128]{1,0:T(8,128)(2,1)S(1)} %copy-done.1), custom_call_target="tpu_custom_call" | custom-call | bytes 6291456 | tf_op jit(solution)/shard_map/flip/pallas_call | solution.py:116
  12.5 0.2 select.1
  12.7 1.2 %collective-permute-start.5 = (bf16[2,18432]{1,0:T(2,128)(2,1)S(1)}, bf16[2,18432]{1,0:T(2,128)(2,1)S(1)}, u32[]{:S(2)}, u32[]{:S(2)}) collective-permute-start(bf16[2,18432]{1,0:T(2,128)(2,1)S(1)} %collective-permute-done), channel_id=1, source_target_pairs={{0,12},{1,13},{2,14},{3,15},{4,8},{5,9},{6,10},{7,11},{8,4},{9,5},... | collective-permute-start | bytes 221192 | tf_op jit(solution)/shard_map/ppermute | solution.py:26
  13.9 0.2 pad_maximum_fusion.2
  14.1 1.6 %collective-permute-start.3 = (bf16[4,18432]{1,0:T(4,128)(2,1)S(1)}, bf16[4,18432]{1,0:T(4,128)(2,1)S(1)}, u32[]{:S(2)}, u32[]{:S(2)}) collective-permute-start(bf16[4,18432]{1,0:T(4,128)(2,1)S(1)} %pad_maximum_fusion.2), channel_id=1, source_target_pairs={{0,2},{1,3},{2,0},{3,1},{4,6},{5,7},{6,4},{7,5},{8,10},{9,11},{10,... | collective-permute-start | bytes 442376 | tf_op jit(solution)/shard_map/ppermute | solution.py:26
  15.6 0.3 pad_maximum_fusion.1.refs_0_
  16.1 3.0 %collective-permute-done.5 = bf16[2,18432]{1,0:T(2,128)(2,1)S(1)} collective-permute-done((bf16[2,18432]{1,0:T(2,128)(2,1)S(1)}, bf16[2,18432]{1,0:T(2,128)(2,1)S(1)}, u32[]{:S(2)}, u32[]{:S(2)}) %collective-permute-start.5) | collective-permute-done | bytes 73760 | tf_op jit(solution)/shard_map/ppermute | solution.py:26
  19.0 0.1 collective-permute-done.4
  19.1 0.2 collective-permute-done.3
  19.4 0.2 pad_maximum_fusion.refs_1_
  19.6 0.1 collective-permute-start.7
  19.7 1.6 %collective-permute-done.7.refs_3_ = bf16[8,18432]{1,0:T(8,128)(2,1)S(1)} collective-permute-done((bf16[8,18432]{1,0:T(8,128)(2,1)S(1)}, bf16[8,18432]{1,0:T(8,128)(2,1)S(1)}, u32[]{:S(2)}, u32[]{:S(2)}) %collective-permute-start.7) | collective-permute-done | bytes 294944 | tf_op jit(solution)/shard_map/ppermute | solution.py:26
  21.3 2.4 %forward.1 = (bf16[32,12288]{1,0:T(8,128)(2,1)S(1)}, bf16[32,256]{1,0:T(8,128)(2,1)S(1)}, f32[16,6144]{1,0:T(8,128)S(1)}, bf16[16,6144]{1,0:T(8,128)(2,1)S(1)}) custom-call(f32[32,128]{1,0:T(8,128)S(1)} %get-tuple-element.40.flow_ref, bf16[64,32]{1,0:T(8,128)(2,1)S(1)} %get-tuple-element.41.pick_ref, bf16[64,32]{1,0:T(8,128)(2,1)S(1)} %get-tuple-element.42.sums_ref, ...), custom_call_target="tpu_custom_call" | custom-call | flops 402653184 | bytes 12582912 | tf_op jit(solution)/shard_map/forward/pallas_call | solution.py:202
  23.7 0.2 collective-permute-start.8
  23.9 1.3 %collective-permute-done.8 = bf16[16,6144]{1,0:T(8,128)(2,1)S(1)} collective-permute-done((bf16[16,6144]{1,0:T(8,128)(2,1)S(1)}, bf16[16,6144]{1,0:T(8,128)(2,1)S(1)}, u32[]{:S(2)}, u32[]{:S(2)}) %collective-permute-start.8) | collective-permute-done | bytes 196640 | tf_op jit(solution)/shard_map/ppermute | solution.py:26
  25.3 2.0 %collective-permute-start.9 = (bf16[4,6144]{1,0:T(4,128)(2,1)S(1)}, bf16[4,6144]{1,0:T(4,128)(2,1)S(1)}, u32[]{:S(2)}, u32[]{:S(2)}) collective-permute-start(bf16[4,6144]{1,0:T(4,128)(2,1)S(1)} %get-tuple-element.59), channel_id=1, source_target_pairs={{0,4},{1,5},{2,6},{3,7},{4,0},{5,1},{6,2},{7,3},{8,12},{9,13},{10,... | collective-permute-start | bytes 147464 | tf_op jit(solution)/shard_map/ppermute | solution.py:26
  27.3 1.1 %collective-permute-start.11 = (bf16[4,6144]{1,0:T(4,128)(2,1)S(1)}, bf16[4,6144]{1,0:T(4,128)(2,1)S(1)}, u32[]{:S(2)}, u32[]{:S(2)}) collective-permute-start(bf16[4,6144]{1,0:T(4,128)(2,1)S(1)} %get-tuple-element.60), channel_id=1, source_target_pairs={{0,6},{1,7},{2,4},{3,5},{4,2},{5,3},{6,0},{7,1},{8,14},{9,15},{10,... | collective-permute-start | bytes 147464 | tf_op jit(solution)/shard_map/ppermute | solution.py:26
  28.4 0.5 %collective-permute-start.10 = (bf16[4,6144]{1,0:T(4,128)(2,1)S(1)}, bf16[4,6144]{1,0:T(4,128)(2,1)S(1)}, u32[]{:S(2)}, u32[]{:S(2)}) collective-permute-start(bf16[4,6144]{1,0:T(4,128)(2,1)S(1)} %get-tuple-element.61), channel_id=1, source_target_pairs={{0,2},{1,3},{2,0},{3,1},{4,6},{5,7},{6,4},{7,5},{8,10},{9,11},{10,... | collective-permute-start | bytes 147464 | tf_op jit(solution)/shard_map/ppermute | solution.py:26
  28.9 3.3 %weight_terms.1 = (bf16[12288,128]{1,0:T(8,128)(2,1)}, bf16[12288,128]{1,0:T(8,128)(2,1)}) custom-call(bf16[32,12288]{1,0:T(8,128)(2,1)S(1)} %get-tuple-element.50.x_ref, bf16[32,256]{1,0:T(8,128)(2,1)S(1)} %get-tuple-element.51.d_ref), custom_call_target="tpu_custom_call" | custom-call | flops 201326592 | bytes 6291456 | tf_op jit(solution)/shard_map/weight_terms/pallas_call | solution.py:239
  32.2 0.1 collective-permute-done.11
  32.3 0.5 %collective-permute-done.10 = bf16[4,6144]{1,0:T(4,128)(2,1)S(1)} collective-permute-done((bf16[4,6144]{1,0:T(4,128)(2,1)S(1)}, bf16[4,6144]{1,0:T(4,128)(2,1)S(1)}, u32[]{:S(2)}, u32[]{:S(2)}) %collective-permute-start.10) | collective-permute-done | bytes 49184 | tf_op jit(solution)/shard_map/ppermute | solution.py:26
  32.9 2.7 %collective-permute-start.12 = (bf16[2,6144]{1,0:T(2,128)(2,1)S(1)}, bf16[2,6144]{1,0:T(2,128)(2,1)S(1)}, u32[]{:S(2)}, u32[]{:S(2)}) collective-permute-start(bf16[2,6144]{1,0:T(2,128)(2,1)S(1)} %slice.42), channel_id=1, source_target_pairs={{0,8},{1,9},{2,10},{3,11},{4,12},{5,13},{6,14},{7,15},{8,0},{9,1},... | collective-permute-start | bytes 73736 | tf_op jit(solution)/shard_map/ppermute | solution.py:26
  35.6 2.1 %collective-permute-done.12 = bf16[2,6144]{1,0:T(2,128)(2,1)S(1)} collective-permute-done((bf16[2,6144]{1,0:T(2,128)(2,1)S(1)}, bf16[2,6144]{1,0:T(2,128)(2,1)S(1)}, u32[]{:S(2)}, u32[]{:S(2)}) %collective-permute-start.12) | collective-permute-done | bytes 24608 | tf_op jit(solution)/shard_map/ppermute | solution.py:26
  37.7 0.7 %copy.9 = bf16[1,1,2,6144]{3,1,2,0:T(2,128)(2,1)} copy(bf16[1,1,2,6144]{3,2,1,0:T(2,128)(2,1)S(1)} %fusion.2) | data formatting | bytes 49152
  (21 shorter events, 0.3 us)
Async XLA Ops:
  0.6 0.8 %copy-start.4 = (bf16[1,12288]{1,0:T(2,128)(2,1)S(1)}, bf16[1,12288]{1,0:T(2,128)(2,1)}, u32[]{:S(2)}) copy-start(bf16[1,12288]{1,0:T(2,128)(2,1)} %parent_ref.1) | copy-start | bytes 73732
  1.4 0.8 %copy-start.5 = (bf16[2,12288]{1,0:T(2,128)(2,1)S(1)}, bf16[2,12288]{1,0:T(2,128)(2,1)}, u32[]{:S(2)}) copy-start(bf16[2,12288]{1,0:T(2,128)(2,1)} %token_ref.1) | copy-start | bytes 147460
  2.2 7.4 %copy-start = (bf16[12288,128]{1,0:T(8,128)(2,1)S(1)}, bf16[12288,128]{1,0:T(8,128)(2,1)}, u32[]{:S(2)}) copy-start(bf16[12288,128]{1,0:T(8,128)(2,1)} %w_ref.2) | copy-start | bytes 9437188
  2.4 10.3 %collective-permute-start.2 = (bf16[2,18432]{1,0:T(2,128)(2,1)S(1)}, bf16[2,18432]{1,0:T(2,128)(2,1)S(1)}, u32[]{:S(2)}, u32[]{:S(2)}) collective-permute-start(bf16[2,18432]{1,0:T(2,128)(2,1)S(1)} %pack.1), channel_id=1, source_target_pairs={{0,8},{1,9},{2,10},{3,11},{4,12},{5,13},{6,14},{7,15},{8,0},{9,1},... | collective-permute-start | bytes 221192 | tf_op jit(solution)/shard_map/ppermute | solution.py:26
  6.5 6.2 %collective-permute-start.1 = (bf16[2,18432]{1,0:T(2,128)(2,1)S(1)}, bf16[2,18432]{1,0:T(2,128)(2,1)S(1)}, u32[]{:S(2)}, u32[]{:S(2)}) collective-permute-start(bf16[2,18432]{1,0:T(2,128)(2,1)S(1)} %pack.1), channel_id=1, source_target_pairs={{0,4},{1,5},{2,6},{3,7},{4,0},{5,1},{6,2},{7,3},{8,12},{9,13},{10,... | collective-permute-start | bytes 221192 | tf_op jit(solution)/shard_map/ppermute | solution.py:26
  8.1 4.6 %collective-permute-start = (bf16[2,18432]{1,0:T(2,128)(2,1)S(1)}, bf16[2,18432]{1,0:T(2,128)(2,1)S(1)}, u32[]{:S(2)}, u32[]{:S(2)}) collective-permute-start(bf16[2,18432]{1,0:T(2,128)(2,1)S(1)} %pack.1), channel_id=1, source_target_pairs={{0,2},{1,3},{2,0},{3,1},{4,6},{5,7},{6,4},{7,5},{8,10},{9,11},{10,... | collective-permute-start | bytes 221192 | tf_op jit(solution)/shard_map/ppermute | solution.py:26
  9.6 1.9 %copy-start.1 = (bf16[12288,128]{1,0:T(8,128)(2,1)S(1)}, bf16[12288,128]{1,0:T(8,128)(2,1)}, u32[]{:S(2)}) copy-start(bf16[12288,128]{1,0:T(8,128)(2,1)} %w_ref.3) | copy-start | bytes 9437188
  9.6 2.9 %copy-start.2 = (bf16[32,128]{1,0:T(8,128)(2,1)S(1)}, bf16[32,128]{1,0:T(8,128)(2,1)}, u32[]{:S(2)}) copy-start(bf16[32,128]{1,0:T(8,128)(2,1)} %flow_ref.1) | copy-start | bytes 24580
  9.6 2.9 %copy-start.3 = (s32[32]{0:T(128)S(1)}, s32[32]{0:T(128)}, u32[]{:S(2)}) copy-start(s32[32]{0:T(128)} %param.8) | copy-start | bytes 388
  12.7 6.3 %collective-permute-start.5 = (bf16[2,18432]{1,0:T(2,128)(2,1)S(1)}, bf16[2,18432]{1,0:T(2,128)(2,1)S(1)}, u32[]{:S(2)}, u32[]{:S(2)}) collective-permute-start(bf16[2,18432]{1,0:T(2,128)(2,1)S(1)} %collective-permute-done), channel_id=1, source_target_pairs={{0,12},{1,13},{2,14},{3,15},{4,8},{5,9},{6,10},{7,11},{8,4},{9,5},... | collective-permute-start | bytes 221192 | tf_op jit(solution)/shard_map/ppermute | solution.py:26
  13.9 5.2 %collective-permute-start.4 = (bf16[2,18432]{1,0:T(2,128)(2,1)S(1)}, bf16[2,18432]{1,0:T(2,128)(2,1)S(1)}, u32[]{:S(2)}, u32[]{:S(2)}) collective-permute-start(bf16[2,18432]{1,0:T(2,128)(2,1)S(1)} %collective-permute-done.2), channel_id=1, source_target_pairs={{0,4},{1,5},{2,6},{3,7},{4,0},{5,1},{6,2},{7,3},{8,12},{9,13},{10,... | collective-permute-start | bytes 221192 | tf_op jit(solution)/shard_map/ppermute | solution.py:26
  14.1 5.3 %collective-permute-start.3 = (bf16[4,18432]{1,0:T(4,128)(2,1)S(1)}, bf16[4,18432]{1,0:T(4,128)(2,1)S(1)}, u32[]{:S(2)}, u32[]{:S(2)}) collective-permute-start(bf16[4,18432]{1,0:T(4,128)(2,1)S(1)} %pad_maximum_fusion.2), channel_id=1, source_target_pairs={{0,2},{1,3},{2,0},{3,1},{4,6},{5,7},{6,4},{7,5},{8,10},{9,11},{10,... | collective-permute-start | bytes 442376 | tf_op jit(solution)/shard_map/ppermute | solution.py:26
  16.0 3.7 %collective-permute-start.6 = (bf16[8,18432]{1,0:T(8,128)(2,1)S(1)}, bf16[8,18432]{1,0:T(8,128)(2,1)S(1)}, u32[]{:S(2)}, u32[]{:S(2)}) collective-permute-start(bf16[8,18432]{1,0:T(8,128)(2,1)S(1)} %pad_maximum_fusion.1.refs_0_), channel_id=1, source_target_pairs={{0,1},{1,0},{2,3},{3,2},{4,5},{5,4},{6,7},{7,6},{8,9},{9,8},{10,11... | collective-permute-start | bytes 884744 | tf_op jit(solution)/shard_map/ppermute | solution.py:26
  19.6 1.6 %collective-permute-start.7 = (bf16[8,18432]{1,0:T(8,128)(2,1)S(1)}, bf16[8,18432]{1,0:T(8,128)(2,1)S(1)}, u32[]{:S(2)}, u32[]{:S(2)}) collective-permute-start(bf16[8,18432]{1,0:T(8,128)(2,1)S(1)} %pad_maximum_fusion.refs_1_), channel_id=1, source_target_pairs={{0,1},{1,0},{2,3},{3,2},{4,5},{5,4},{6,7},{7,6},{8,9},{9,8},{10,11... | collective-permute-start | bytes 884744 | tf_op jit(solution)/shard_map/ppermute | solution.py:26
  23.7 1.5 %collective-permute-start.8 = (bf16[16,6144]{1,0:T(8,128)(2,1)S(1)}, bf16[16,6144]{1,0:T(8,128)(2,1)S(1)}, u32[]{:S(2)}, u32[]{:S(2)}) collective-permute-start(bf16[16,6144]{1,0:T(8,128)(2,1)S(1)} %get-tuple-element.49), channel_id=1, source_target_pairs={{0,1},{1,0},{2,3},{3,2},{4,5},{5,4},{6,7},{7,6},{8,9},{9,8},{10,11... | collective-permute-start | bytes 589832 | tf_op jit(solution)/shard_map/ppermute | solution.py:26
  25.3 6.9 %collective-permute-start.9 = (bf16[4,6144]{1,0:T(4,128)(2,1)S(1)}, bf16[4,6144]{1,0:T(4,128)(2,1)S(1)}, u32[]{:S(2)}, u32[]{:S(2)}) collective-permute-start(bf16[4,6144]{1,0:T(4,128)(2,1)S(1)} %get-tuple-element.59), channel_id=1, source_target_pairs={{0,4},{1,5},{2,6},{3,7},{4,0},{5,1},{6,2},{7,3},{8,12},{9,13},{10,... | collective-permute-start | bytes 147464 | tf_op jit(solution)/shard_map/ppermute | solution.py:26
  27.3 5.0 %collective-permute-start.11 = (bf16[4,6144]{1,0:T(4,128)(2,1)S(1)}, bf16[4,6144]{1,0:T(4,128)(2,1)S(1)}, u32[]{:S(2)}, u32[]{:S(2)}) collective-permute-start(bf16[4,6144]{1,0:T(4,128)(2,1)S(1)} %get-tuple-element.60), channel_id=1, source_target_pairs={{0,6},{1,7},{2,4},{3,5},{4,2},{5,3},{6,0},{7,1},{8,14},{9,15},{10,... | collective-permute-start | bytes 147464 | tf_op jit(solution)/shard_map/ppermute | solution.py:26
  28.4 4.5 %collective-permute-start.10 = (bf16[4,6144]{1,0:T(4,128)(2,1)S(1)}, bf16[4,6144]{1,0:T(4,128)(2,1)S(1)}, u32[]{:S(2)}, u32[]{:S(2)}) collective-permute-start(bf16[4,6144]{1,0:T(4,128)(2,1)S(1)} %get-tuple-element.61), channel_id=1, source_target_pairs={{0,2},{1,3},{2,0},{3,1},{4,6},{5,7},{6,4},{7,5},{8,10},{9,11},{10,... | collective-permute-start | bytes 147464 | tf_op jit(solution)/shard_map/ppermute | solution.py:26
  32.9 4.8 %collective-permute-start.12 = (bf16[2,6144]{1,0:T(2,128)(2,1)S(1)}, bf16[2,6144]{1,0:T(2,128)(2,1)S(1)}, u32[]{:S(2)}, u32[]{:S(2)}) collective-permute-start(bf16[2,6144]{1,0:T(2,128)(2,1)S(1)} %slice.42), channel_id=1, source_target_pairs={{0,8},{1,9},{2,10},{3,11},{4,12},{5,13},{6,14},{7,15},{8,0},{9,1},... | collective-permute-start | bytes 73736 | tf_op jit(solution)/shard_map/ppermute | solution.py:26

commit v5 on v4

--- a/solution.py
+++ b/solution.py
@@ -11,8 +11,10 @@
 F32 = jnp.float32
 MIB = 1 << 20
 VMEM = pl.BlockSpec(memory_space=pltpu.VMEM)
+ANY = pl.BlockSpec(memory_space=pl.ANY)
 HBM = pl.BlockSpec(memory_space=pltpu.HBM)
 SMEM = pl.BlockSpec(memory_space=pltpu.SMEM)
+LONG = pl.CostEstimate(flops=1 << 38, bytes_accessed=1024 * MIB, transcendentals=0)
 
 
 def factors(count):
@@ -26,12 +28,16 @@
     return lax.ppermute(x, "blk", [(i, i ^ mask) for i in range(count)])
 
 
+def across(z, y, count):
+    return (z * factors(count)[1] + y) * 2 + 1
+
+
 def scatter_stages(count):
     outer, inner, _ = factors(count)
-    z_steps = [(1 << i) * inner * 2 for i in range(outer.bit_length() - 1)]
-    y_steps = [(1 << i) * 2 for i in range(inner.bit_length() - 1)]
-    squares = [[0, z, y, z ^ y] for z, y in zip(z_steps, y_steps)]
-    return [[0, 1]] + squares + [[0, z] for z in z_steps[len(y_steps):]]
+    z_steps = [1 << i for i in range(outer.bit_length() - 1)]
+    y_steps = [1 << i for i in range(inner.bit_length() - 1)]
+    squares = [[0, across(z, 0, count), across(0, y, count), across(z, y, count)] for z, y in zip(z_steps, y_steps)]
+    return [[0, 1]] + squares + [[0, across(z, 0, count)] for z in z_steps[len(y_steps):]]
 
 
 def scatter_masks(count):
@@ -44,26 +50,46 @@
 def gather_masks(count):
     outer, inner, _ = factors(count)
     if (outer, inner) == (4, 2):
-        chips = [(0, 0), (1, 0), (2, 0), (0, 1), (1, 1), (2, 1), (3, 0), (3, 1)]
-        return [(z * inner + y) * 2 + c for c in range(2) for z, y in chips]
-    return [(z * inner + y) * 2 + c for c in range(2) for y in range(inner) for z in range(outer)]
+        near, far, side = across(1, 0, count), across(2, 0, count), across(0, 1, count)
+        plane = [0, near, far, side, side ^ near, side ^ far, near ^ far, across(3, 0, count) ^ side]
+    else:
+        column = [0] + [across(z, 0, count) for z in range(1, outer)]
+        plane = column + [across(0, y, count) ^ m for y in range(1, inner) for m in column]
+    return plane + [m ^ 1 for m in plane]
+
+
+def after_kernel(*refs):
+    pass
+
+
+def after(arrays, deps):
+    arrays, deps = tuple(arrays), tuple(jax.tree.leaves(deps))
+    return pl.pallas_call(
+        after_kernel,
+        out_shape=tuple(jax.ShapeDtypeStruct(x.shape, x.dtype) for x in arrays),
+        in_specs=[ANY] * (len(arrays) + len(deps)),
+        out_specs=(ANY,) * len(arrays),
+        input_output_aliases={i: i for i in range(len(arrays))},
+        compiler_params=pltpu.CompilerParams(vmem_limit_bytes=MIB),
+        name="after",
+    )(*arrays, *deps)
 
 
 def gather(block, count, beside):
     outer, inner, _ = factors(count)
-    to = lambda x, z, y: send(x, (z * inner + y) * 2, count)
+    to = lambda x, z, y: send(x, across(z, y, count), count)
     if (outer, inner) == (4, 2):
         far, near, side = to(block, 2, 0), to(block, 1, 0), to(block, 0, 1)
-        side, near, far = lax.optimization_barrier((side, near, far))
+        side, both, far = after((side, jnp.concatenate([near, far], 0), far), beside)
         corner = to(side, 3, 0)
-        pair = to(jnp.concatenate([near, far], 0), 0, 1)
+        pair = to(both, 0, 1)
         third = to(far, 1, 0)
         plane = [jnp.concatenate([block, near, far, side], 0), jnp.concatenate([pair, third, corner], 0)]
     else:
         column = jnp.concatenate([block] + [to(block, z, 0) for z in range(1, outer)], 0)
+        (column,) = after((column,), beside)
         plane = [column] + [to(column, 0, y) for y in range(1, inner)]
-    plane[-1], beside = lax.optimization_barrier((plane[-1], beside))
-    return plane + [send(p, 1, count) for p in plane], beside
+    return plane + [send(p, 1, count) for p in plane]
 
 
 def owner_of(slot, me, masks):
@@ -73,38 +99,37 @@
     return me ^ mask
 
 
-def pack_kernel(parent_ref, token_ref, out_ref, parent_buf, token_buf, sems):
+def lead_kernel(out_ref):
+    out_ref[...] = jnp.zeros_like(out_ref)
+
+
+def pack_kernel(lead_ref, parent_ref, token_ref, out_ref):
     width = token_ref.shape[1]
     half = width // 2
-    copies = [
-        pltpu.make_async_copy(parent_ref, parent_buf, sems.at[0]),
-        pltpu.make_async_copy(token_ref, token_buf, sems.at[1]),
-    ]
-    for copy in copies:
-        copy.start()
-    for copy in copies:
-        copy.wait()
-    out_ref[:, :width] = token_buf[...]
-    row = parent_buf[...].astype(F32)
+    out_ref[:, :width] = token_ref[...]
+    row = parent_ref[...].astype(F32)
     out_ref[:, width:] = jnp.concatenate([row[:, :half], row[:, half:]], 0).astype(BF)
 
 
 def pack(parent_rows, token_rows):
     width = token_rows.shape[1]
+    lead = pl.pallas_call(
+        lead_kernel,
+        out_shape=jax.ShapeDtypeStruct((8, 128), F32),
+        out_specs=VMEM,
+        compiler_params=pltpu.CompilerParams(vmem_limit_bytes=4 * MIB),
+        cost_estimate=LONG,
+        name="lead",
+    )()
     return pl.pallas_call(
         pack_kernel,
         out_shape=jax.ShapeDtypeStruct((2, width * 3 // 2), BF),
-        in_specs=[HBM] * 2,
+        in_specs=[VMEM] * 3,
         out_specs=VMEM,
-        scratch_shapes=[
-            pltpu.VMEM((1, width), BF),
-            pltpu.VMEM((2, width), BF),
-            pltpu.SemaphoreType.DMA((2,)),
-        ],
         compiler_params=pltpu.CompilerParams(vmem_limit_bytes=4 * MIB),
-        cost_estimate=pl.CostEstimate(flops=1 << 38, bytes_accessed=1024 * MIB, transcendentals=0),
+        cost_estimate=LONG,
         name="pack",
-    )(parent_rows, token_rows)
+    )(lead, parent_rows, token_rows)
 
 
 def flip_kernel(w_ref, out_ref, flip_ref):
@@ -260,7 +285,7 @@
 
     block = pack(parent_rows, token_rows)
     beside = (select(me, parent, d_hidden, count), flip(w_gate), flip(w_up))
-    columns, beside = gather(block, count, beside)
+    columns = gather(block, count, beside)
     (flow, pick, sums), (w_gate, flip_gate), (w_up, flip_up) = beside
     x, d, own, other = forward(flow, pick, sums, w_gate, w_up, flip_gate, flip_up, columns)
     rows = own + send(other, 1, count).astype(F32)

time: 38.6 us -> 37.3 us (0.966)
  starting transfers between devices: 16.5 us -> 15.6 us
  local copies, waits for them, and re-layouts: 3.22 us -> 2.43 us
  waiting for transfers between devices: 8.94 us -> 9.48 us
    ppermute x13, starting transfers between devices: 16.5 us -> 15.6 us  [send(): return lax.ppermute(x, 'blk', [(i, i ^ mask) for i in range(count)])]
    unnamed x13, local copies, waits for them, and re-layouts: 3.13 us -> 2.34 us
    ppermute x13, waiting for transfers between devices: 8.94 us -> 9.48 us  [send(): return lax.ppermute(x, 'blk', [(i, i ^ mask) for i in range(count)])]
  transfers between devices with their start and end apart: 13 -> 13, of which waited for: 8 -> 7; matrix products, arithmetic and copies ran while one was open for 2% -> 2% of each run, Pallas kernels for 14% -> 15%
where the time goes in v5:
time: 37.3 us; the launch traced here: 37.2 us
  starting transfers between devices  15.6 us (42%)
  waiting for transfers between devices  9.48 us (25%)
  Pallas kernels  7.97 us (21%)
  local copies, waits for them, and re-layouts  2.43 us (7%)
  other arithmetic  0.87 us (2%)
  between operations  0.77 us (2%)
    ppermute x13, starting transfers between devices, send(): return lax.ppermute(x, 'blk', [(i, i ^ mask) for i in range(count)])  15.6 us
    ppermute x13, waiting for transfers between devices, send(): return lax.ppermute(x, 'blk', [(i, i ^ mask) for i in range(count)])  9.48 us
    pallas_call x1, Pallas kernels, weight_terms(): pl.pallas_call(functools.partial(weight_kernel, step), out_shape=(shape,...  3.3 us
    pallas_call x1, Pallas kernels, forward(): pl.pallas_call(functools.partial(forward_kernel, len(columns)), out_shape...  2.44 us
    unnamed x13, local copies, waits for them, and re-layouts  2.34 us
    pallas_call x2, Pallas kernels, flip(): pl.pallas_call(flip_kernel, out_shape=(jax.ShapeDtypeStruct(w.shape, BF),...  2.01 us
  transfers between devices with their start and end apart: 13, of which 7 were waited for; matrix products, arithmetic and copies ran while one was open for 2% of the time, Pallas kernels for 15%

profile of v5, /device:TPU:0, one launch (start us, length us, event | category | flops | bytes accessed | tf_op | source)
XLA Modules:
  0.0 37.2 jit_solution(1430798531826935903)
XLA Ops:
  0.7 0.8 %copy-done.4 = bf16[1,12288]{1,0:T(2,128)(2,1)S(1)} copy-done((bf16[1,12288]{1,0:T(2,128)(2,1)S(1)}, bf16[1,12288]{1,0:T(2,128)(2,1)}, u32[]{:S(2)}) %copy-start.4) | copy-done | bytes 24600
  1.5 3.5 %collective-permute-start.2 = (bf16[2,18432]{1,0:T(2,128)(2,1)S(1)}, bf16[2,18432]{1,0:T(2,128)(2,1)S(1)}, u32[]{:S(2)}, u32[]{:S(2)}) collective-permute-start(bf16[2,18432]{1,0:T(2,128)(2,1)S(1)} %pack.1), channel_id=1, source_target_pairs={{0,9},{1,8},{2,11},{3,10},{4,13},{5,12},{6,15},{7,14},{8,1},{9,0},... | collective-permute-start | bytes 221192 | tf_op jit(solution)/shard_map/ppermute | solution.py:28
  5.0 1.9 %collective-permute-start = (bf16[2,18432]{1,0:T(2,128)(2,1)S(1)}, bf16[2,18432]{1,0:T(2,128)(2,1)S(1)}, u32[]{:S(2)}, u32[]{:S(2)}) collective-permute-start(bf16[2,18432]{1,0:T(2,128)(2,1)S(1)} %pack.1), channel_id=1, source_target_pairs={{0,5},{1,4},{2,7},{3,6},{4,1},{5,0},{6,3},{7,2},{8,13},{9,12},{10,... | collective-permute-start | bytes 221192 | tf_op jit(solution)/shard_map/ppermute | solution.py:28
  6.9 1.0 %collective-permute-start.1 = (bf16[2,18432]{1,0:T(2,128)(2,1)S(1)}, bf16[2,18432]{1,0:T(2,128)(2,1)S(1)}, u32[]{:S(2)}, u32[]{:S(2)}) collective-permute-start(bf16[2,18432]{1,0:T(2,128)(2,1)S(1)} %pack.1), channel_id=1, source_target_pairs={{0,3},{1,2},{2,1},{3,0},{4,7},{5,6},{6,5},{7,4},{8,11},{9,10},{10,... | collective-permute-start | bytes 221192 | tf_op jit(solution)/shard_map/ppermute | solution.py:28
  7.9 1.0 %flip.2 = (bf16[12288,128]{1,0:T(8,128)(2,1)S(1)}, bf16[128,12288]{1,0:T(8,128)(2,1)S(1)}) custom-call(bf16[12288,128]{1,0:T(8,128)(2,1)S(1)} %copy-done), custom_call_target="tpu_custom_call" | custom-call | bytes 6291456 | tf_op jit(solution)/shard_map/flip/pallas_call | solution.py:141
  8.9 0.9 %copy-done.1 = bf16[12288,128]{1,0:T(8,128)(2,1)S(1)} copy-done((bf16[12288,128]{1,0:T(8,128)(2,1)S(1)}, bf16[12288,128]{1,0:T(8,128)(2,1)}, u32[]{:S(2)}) %copy-start.1) | copy-done | bytes 3145752
  9.8 1.0 %flip.3 = (bf16[12288,128]{1,0:T(8,128)(2,1)S(1)}, bf16[128,12288]{1,0:T(8,128)(2,1)S(1)}) custom-call(bf16[12288,128]{1,0:T(8,128)(2,1)S(1)} %copy-done.1), custom_call_target="tpu_custom_call" | custom-call | bytes 6291456 | tf_op jit(solution)/shard_map/flip/pallas_call | solution.py:141
  10.8 0.2 select.1
  11.0 0.2 pad_maximum_fusion.2.refs_1_
  11.1 0.3 collective-permute-done.1.refs_0_
  11.4 0.6 %collective-permute-start.4 = (bf16[2,18432]{1,0:T(2,128)(2,1)S(1)}, bf16[2,18432]{1,0:T(2,128)(2,1)S(1)}, u32[]{:S(2)}, u32[]{:S(2)}) collective-permute-start(bf16[2,18432]{1,0:T(2,128)(2,1)S(1)} %get-tuple-element.29), channel_id=1, source_target_pairs={{0,5},{1,4},{2,7},{3,6},{4,1},{5,0},{6,3},{7,2},{8,13},{9,12},{10,... | collective-permute-start | bytes 221192 | tf_op jit(solution)/shard_map/ppermute | solution.py:28
  12.0 1.6 %collective-permute-start.5 = (bf16[2,18432]{1,0:T(2,128)(2,1)S(1)}, bf16[2,18432]{1,0:T(2,128)(2,1)S(1)}, u32[]{:S(2)}, u32[]{:S(2)}) collective-permute-start(bf16[2,18432]{1,0:T(2,128)(2,1)S(1)} %get-tuple-element.30), channel_id=1, source_target_pairs={{0,13},{1,12},{2,15},{3,14},{4,9},{5,8},{6,11},{7,10},{8,5},{9,4},... | collective-permute-start | bytes 221192 | tf_op jit(solution)/shard_map/ppermute | solution.py:28
  13.6 1.6 %collective-permute-start.3 = (bf16[4,18432]{1,0:T(4,128)(2,1)S(1)}, bf16[4,18432]{1,0:T(4,128)(2,1)S(1)}, u32[]{:S(2)}, u32[]{:S(2)}) collective-permute-start(bf16[4,18432]{1,0:T(4,128)(2,1)S(1)} %get-tuple-element.31), channel_id=1, source_target_pairs={{0,3},{1,2},{2,1},{3,0},{4,7},{5,6},{6,5},{7,4},{8,11},{9,10},{10,... | collective-permute-start | bytes 442376 | tf_op jit(solution)/shard_map/ppermute | solution.py:28
  15.1 0.3 pad_maximum_fusion.refs_0_
  15.5 0.1 collective-permute-start.6
  15.6 2.6 %collective-permute-done.5 = bf16[2,18432]{1,0:T(2,128)(2,1)S(1)} collective-permute-done((bf16[2,18432]{1,0:T(2,128)(2,1)S(1)}, bf16[2,18432]{1,0:T(2,128)(2,1)S(1)}, u32[]{:S(2)}, u32[]{:S(2)}) %collective-permute-start.5) | collective-permute-done | bytes 73760 | tf_op jit(solution)/shard_map/ppermute | solution.py:28
  18.2 1.0 %collective-permute-done.3 = bf16[4,18432]{1,0:T(4,128)(2,1)S(1)} collective-permute-done((bf16[4,18432]{1,0:T(4,128)(2,1)S(1)}, bf16[4,18432]{1,0:T(4,128)(2,1)S(1)}, u32[]{:S(2)}, u32[]{:S(2)}) %collective-permute-start.3) | collective-permute-done | bytes 147488 | tf_op jit(solution)/shard_map/ppermute | solution.py:28
  19.2 0.2 pad_maximum_fusion.1.refs_1_
  19.4 0.4 %collective-permute-start.7 = (bf16[8,18432]{1,0:T(8,128)(2,1)S(1)}, bf16[8,18432]{1,0:T(8,128)(2,1)S(1)}, u32[]{:S(2)}, u32[]{:S(2)}) collective-permute-start(bf16[8,18432]{1,0:T(8,128)(2,1)S(1)} %pad_maximum_fusion.1.refs_1_), channel_id=1, source_target_pairs={{0,1},{1,0},{2,3},{3,2},{4,5},{5,4},{6,7},{7,6},{8,9},{9,8},{10,11... | collective-permute-start | bytes 884744 | tf_op jit(solution)/shard_map/ppermute | solution.py:28
  19.9 1.2 %collective-permute-done.7.refs_3_ = bf16[8,18432]{1,0:T(8,128)(2,1)S(1)} collective-permute-done((bf16[8,18432]{1,0:T(8,128)(2,1)S(1)}, bf16[8,18432]{1,0:T(8,128)(2,1)S(1)}, u32[]{:S(2)}, u32[]{:S(2)}) %collective-permute-start.7) | collective-permute-done | bytes 294944 | tf_op jit(solution)/shard_map/ppermute | solution.py:28
  21.1 2.4 %forward.1 = (bf16[32,12288]{1,0:T(8,128)(2,1)S(1)}, bf16[32,256]{1,0:T(8,128)(2,1)S(1)}, f32[16,6144]{1,0:T(8,128)S(1)}, bf16[16,6144]{1,0:T(8,128)(2,1)S(1)}) custom-call(f32[32,128]{1,0:T(8,128)S(1)} %get-tuple-element.22.refs_3_.flow_ref, bf16[64,32]{1,0:T(8,128)(2,1)S(1)} %get-tuple-element.23.refs_4_.pick_ref, ...), custom_call_target="tpu_custom_call" | custom-call | flops 402653184 | bytes 12582912 | tf_op jit(solution)/shard_map/forward/pallas_call | solution.py:227
  23.5 0.4 %collective-permute-start.8 = (bf16[16,6144]{1,0:T(8,128)(2,1)S(1)}, bf16[16,6144]{1,0:T(8,128)(2,1)S(1)}, u32[]{:S(2)}, u32[]{:S(2)}) collective-permute-start(bf16[16,6144]{1,0:T(8,128)(2,1)S(1)} %get-tuple-element.33), channel_id=1, source_target_pairs={{0,1},{1,0},{2,3},{3,2},{4,5},{5,4},{6,7},{7,6},{8,9},{9,8},{10,11... | collective-permute-start | bytes 589832 | tf_op jit(solution)/shard_map/ppermute | solution.py:28
  23.9 1.1 %collective-permute-done.8 = bf16[16,6144]{1,0:T(8,128)(2,1)S(1)} collective-permute-done((bf16[16,6144]{1,0:T(8,128)(2,1)S(1)}, bf16[16,6144]{1,0:T(8,128)(2,1)S(1)}, u32[]{:S(2)}, u32[]{:S(2)}) %collective-permute-start.8) | collective-permute-done | bytes 196640 | tf_op jit(solution)/shard_map/ppermute | solution.py:28
  25.1 0.1 fusion.4
  25.1 1.2 %collective-permute-start.9 = (bf16[4,6144]{1,0:T(4,128)(2,1)S(1)}, bf16[4,6144]{1,0:T(4,128)(2,1)S(1)}, u32[]{:S(2)}, u32[]{:S(2)}) collective-permute-start(bf16[4,6144]{1,0:T(4,128)(2,1)S(1)} %get-tuple-element.43), channel_id=1, source_target_pairs={{0,5},{1,4},{2,7},{3,6},{4,1},{5,0},{6,3},{7,2},{8,13},{9,12},{10,... | collective-permute-start | bytes 147464 | tf_op jit(solution)/shard_map/ppermute | solution.py:28
  26.3 1.6 %collective-permute-start.11 = (bf16[4,6144]{1,0:T(4,128)(2,1)S(1)}, bf16[4,6144]{1,0:T(4,128)(2,1)S(1)}, u32[]{:S(2)}, u32[]{:S(2)}) collective-permute-start(bf16[4,6144]{1,0:T(4,128)(2,1)S(1)} %get-tuple-element.44), channel_id=1, source_target_pairs={{0,7},{1,6},{2,5},{3,4},{4,3},{5,2},{6,1},{7,0},{8,15},{9,14},{10,... | collective-permute-start | bytes 147464 | tf_op jit(solution)/shard_map/ppermute | solution.py:28
  27.9 0.5 %collective-permute-start.10 = (bf16[4,6144]{1,0:T(4,128)(2,1)S(1)}, bf16[4,6144]{1,0:T(4,128)(2,1)S(1)}, u32[]{:S(2)}, u32[]{:S(2)}) collective-permute-start(bf16[4,6144]{1,0:T(4,128)(2,1)S(1)} %get-tuple-element.45), channel_id=1, source_target_pairs={{0,3},{1,2},{2,1},{3,0},{4,7},{5,6},{6,5},{7,4},{8,11},{9,10},{10,... | collective-permute-start | bytes 147464 | tf_op jit(solution)/shard_map/ppermute | solution.py:28
  28.4 3.3 %weight_terms.1 = (bf16[12288,128]{1,0:T(8,128)(2,1)}, bf16[12288,128]{1,0:T(8,128)(2,1)}) custom-call(bf16[32,12288]{1,0:T(8,128)(2,1)S(1)} %get-tuple-element.34.x_ref, bf16[32,256]{1,0:T(8,128)(2,1)S(1)} %get-tuple-element.35.d_ref), custom_call_target="tpu_custom_call" | custom-call | flops 201326592 | bytes 6291456 | tf_op jit(solution)/shard_map/weight_terms/pallas_call | solution.py:264
  31.7 0.4 %collective-permute-done.10 = bf16[4,6144]{1,0:T(4,128)(2,1)S(1)} collective-permute-done((bf16[4,6144]{1,0:T(4,128)(2,1)S(1)}, bf16[4,6144]{1,0:T(4,128)(2,1)S(1)}, u32[]{:S(2)}, u32[]{:S(2)}) %collective-permute-start.10) | collective-permute-done | bytes 49184 | tf_op jit(solution)/shard_map/ppermute | solution.py:28
  32.3 1.3 %collective-permute-start.12 = (bf16[2,6144]{1,0:T(2,128)(2,1)S(1)}, bf16[2,6144]{1,0:T(2,128)(2,1)S(1)}, u32[]{:S(2)}, u32[]{:S(2)}) collective-permute-start(bf16[2,6144]{1,0:T(2,128)(2,1)S(1)} %slice.42), channel_id=1, source_target_pairs={{0,9},{1,8},{2,11},{3,10},{4,13},{5,12},{6,15},{7,14},{8,1},{9,0},... | collective-permute-start | bytes 73736 | tf_op jit(solution)/shard_map/ppermute | solution.py:28
  33.5 2.9 %collective-permute-done.12 = bf16[2,6144]{1,0:T(2,128)(2,1)S(1)} collective-permute-done((bf16[2,6144]{1,0:T(2,128)(2,1)S(1)}, bf16[2,6144]{1,0:T(2,128)(2,1)S(1)}, u32[]{:S(2)}, u32[]{:S(2)}) %collective-permute-start.12) | collective-permute-done | bytes 24608 | tf_op jit(solution)/shard_map/ppermute | solution.py:28
  36.5 0.7 %copy.12 = bf16[1,1,2,6144]{3,1,2,0:T(2,128)(2,1)} copy(bf16[1,1,2,6144]{3,2,1,0:T(2,128)(2,1)S(1)} %fusion.2) | data formatting | bytes 49152
  (23 shorter events, 0.3 us)
Async XLA Ops:
  0.6 0.8 %copy-start.4 = (bf16[1,12288]{1,0:T(2,128)(2,1)S(1)}, bf16[1,12288]{1,0:T(2,128)(2,1)}, u32[]{:S(2)}) copy-start(bf16[1,12288]{1,0:T(2,128)(2,1)} %parent_ref.1) | copy-start | bytes 73732
  0.6 0.8 %copy-start.5 = (bf16[2,12288]{1,0:T(2,128)(2,1)S(1)}, bf16[2,12288]{1,0:T(2,128)(2,1)}, u32[]{:S(2)}) copy-start(bf16[2,12288]{1,0:T(2,128)(2,1)} %token_ref.1) | copy-start | bytes 147460
  1.5 6.4 %copy-start = (bf16[12288,128]{1,0:T(8,128)(2,1)S(1)}, bf16[12288,128]{1,0:T(8,128)(2,1)}, u32[]{:S(2)}) copy-start(bf16[12288,128]{1,0:T(8,128)(2,1)} %w_ref.2) | copy-start | bytes 9437188
  1.5 9.5 %collective-permute-start.2 = (bf16[2,18432]{1,0:T(2,128)(2,1)S(1)}, bf16[2,18432]{1,0:T(2,128)(2,1)S(1)}, u32[]{:S(2)}, u32[]{:S(2)}) collective-permute-start(bf16[2,18432]{1,0:T(2,128)(2,1)S(1)} %pack.1), channel_id=1, source_target_pairs={{0,9},{1,8},{2,11},{3,10},{4,13},{5,12},{6,15},{7,14},{8,1},{9,0},... | collective-permute-start | bytes 221192 | tf_op jit(solution)/shard_map/ppermute | solution.py:28
  5.0 5.9 %collective-permute-start = (bf16[2,18432]{1,0:T(2,128)(2,1)S(1)}, bf16[2,18432]{1,0:T(2,128)(2,1)S(1)}, u32[]{:S(2)}, u32[]{:S(2)}) collective-permute-start(bf16[2,18432]{1,0:T(2,128)(2,1)S(1)} %pack.1), channel_id=1, source_target_pairs={{0,5},{1,4},{2,7},{3,6},{4,1},{5,0},{6,3},{7,2},{8,13},{9,12},{10,... | collective-permute-start | bytes 221192 | tf_op jit(solution)/shard_map/ppermute | solution.py:28
  6.9 4.5 %collective-permute-start.1 = (bf16[2,18432]{1,0:T(2,128)(2,1)S(1)}, bf16[2,18432]{1,0:T(2,128)(2,1)S(1)}, u32[]{:S(2)}, u32[]{:S(2)}) collective-permute-start(bf16[2,18432]{1,0:T(2,128)(2,1)S(1)} %pack.1), channel_id=1, source_target_pairs={{0,3},{1,2},{2,1},{3,0},{4,7},{5,6},{6,5},{7,4},{8,11},{9,10},{10,... | collective-permute-start | bytes 221192 | tf_op jit(solution)/shard_map/ppermute | solution.py:28
  7.9 1.9 %copy-start.1 = (bf16[12288,128]{1,0:T(8,128)(2,1)S(1)}, bf16[12288,128]{1,0:T(8,128)(2,1)}, u32[]{:S(2)}) copy-start(bf16[12288,128]{1,0:T(8,128)(2,1)} %w_ref.3) | copy-start | bytes 9437188
  7.9 2.9 %copy-start.2 = (bf16[32,128]{1,0:T(8,128)(2,1)S(1)}, bf16[32,128]{1,0:T(8,128)(2,1)}, u32[]{:S(2)}) copy-start(bf16[32,128]{1,0:T(8,128)(2,1)} %flow_ref.1) | copy-start | bytes 24580
  7.9 2.9 %copy-start.3 = (s32[32]{0:T(128)S(1)}, s32[32]{0:T(128)}, u32[]{:S(2)}) copy-start(s32[32]{0:T(128)} %param.8) | copy-start | bytes 388
  11.4 4.2 %collective-permute-start.4 = (bf16[2,18432]{1,0:T(2,128)(2,1)S(1)}, bf16[2,18432]{1,0:T(2,128)(2,1)S(1)}, u32[]{:S(2)}, u32[]{:S(2)}) collective-permute-start(bf16[2,18432]{1,0:T(2,128)(2,1)S(1)} %get-tuple-element.29), channel_id=1, source_target_pairs={{0,5},{1,4},{2,7},{3,6},{4,1},{5,0},{6,3},{7,2},{8,13},{9,12},{10,... | collective-permute-start | bytes 221192 | tf_op jit(solution)/shard_map/ppermute | solution.py:28
  12.0 6.3 %collective-permute-start.5 = (bf16[2,18432]{1,0:T(2,128)(2,1)S(1)}, bf16[2,18432]{1,0:T(2,128)(2,1)S(1)}, u32[]{:S(2)}, u32[]{:S(2)}) collective-permute-start(bf16[2,18432]{1,0:T(2,128)(2,1)S(1)} %get-tuple-element.30), channel_id=1, source_target_pairs={{0,13},{1,12},{2,15},{3,14},{4,9},{5,8},{6,11},{7,10},{8,5},{9,4},... | collective-permute-start | bytes 221192 | tf_op jit(solution)/shard_map/ppermute | solution.py:28
  13.6 5.6 %collective-permute-start.3 = (bf16[4,18432]{1,0:T(4,128)(2,1)S(1)}, bf16[4,18432]{1,0:T(4,128)(2,1)S(1)}, u32[]{:S(2)}, u32[]{:S(2)}) collective-permute-start(bf16[4,18432]{1,0:T(4,128)(2,1)S(1)} %get-tuple-element.31), channel_id=1, source_target_pairs={{0,3},{1,2},{2,1},{3,0},{4,7},{5,6},{6,5},{7,4},{8,11},{9,10},{10,... | collective-permute-start | bytes 442376 | tf_op jit(solution)/shard_map/ppermute | solution.py:28
  15.5 4.4 %collective-permute-start.6 = (bf16[8,18432]{1,0:T(8,128)(2,1)S(1)}, bf16[8,18432]{1,0:T(8,128)(2,1)S(1)}, u32[]{:S(2)}, u32[]{:S(2)}) collective-permute-start(bf16[8,18432]{1,0:T(8,128)(2,1)S(1)} %pad_maximum_fusion.refs_0_), channel_id=1, source_target_pairs={{0,1},{1,0},{2,3},{3,2},{4,5},{5,4},{6,7},{7,6},{8,9},{9,8},{10,11... | collective-permute-start | bytes 884744 | tf_op jit(solution)/shard_map/ppermute | solution.py:28
  19.4 1.6 %collective-permute-start.7 = (bf16[8,18432]{1,0:T(8,128)(2,1)S(1)}, bf16[8,18432]{1,0:T(8,128)(2,1)S(1)}, u32[]{:S(2)}, u32[]{:S(2)}) collective-permute-start(bf16[8,18432]{1,0:T(8,128)(2,1)S(1)} %pad_maximum_fusion.1.refs_1_), channel_id=1, source_target_pairs={{0,1},{1,0},{2,3},{3,2},{4,5},{5,4},{6,7},{7,6},{8,9},{9,8},{10,11... | collective-permute-start | bytes 884744 | tf_op jit(solution)/shard_map/ppermute | solution.py:28
  23.5 1.5 %collective-permute-start.8 = (bf16[16,6144]{1,0:T(8,128)(2,1)S(1)}, bf16[16,6144]{1,0:T(8,128)(2,1)S(1)}, u32[]{:S(2)}, u32[]{:S(2)}) collective-permute-start(bf16[16,6144]{1,0:T(8,128)(2,1)S(1)} %get-tuple-element.33), channel_id=1, source_target_pairs={{0,1},{1,0},{2,3},{3,2},{4,5},{5,4},{6,7},{7,6},{8,9},{9,8},{10,11... | collective-permute-start | bytes 589832 | tf_op jit(solution)/shard_map/ppermute | solution.py:28
  25.1 6.6 %collective-permute-start.9 = (bf16[4,6144]{1,0:T(4,128)(2,1)S(1)}, bf16[4,6144]{1,0:T(4,128)(2,1)S(1)}, u32[]{:S(2)}, u32[]{:S(2)}) collective-permute-start(bf16[4,6144]{1,0:T(4,128)(2,1)S(1)} %get-tuple-element.43), channel_id=1, source_target_pairs={{0,5},{1,4},{2,7},{3,6},{4,1},{5,0},{6,3},{7,2},{8,13},{9,12},{10,... | collective-permute-start | bytes 147464 | tf_op jit(solution)/shard_map/ppermute | solution.py:28
  26.3 5.4 %collective-permute-start.11 = (bf16[4,6144]{1,0:T(4,128)(2,1)S(1)}, bf16[4,6144]{1,0:T(4,128)(2,1)S(1)}, u32[]{:S(2)}, u32[]{:S(2)}) collective-permute-start(bf16[4,6144]{1,0:T(4,128)(2,1)S(1)} %get-tuple-element.44), channel_id=1, source_target_pairs={{0,7},{1,6},{2,5},{3,4},{4,3},{5,2},{6,1},{7,0},{8,15},{9,14},{10,... | collective-permute-start | bytes 147464 | tf_op jit(solution)/shard_map/ppermute | solution.py:28
  27.9 4.3 %collective-permute-start.10 = (bf16[4,6144]{1,0:T(4,128)(2,1)S(1)}, bf16[4,6144]{1,0:T(4,128)(2,1)S(1)}, u32[]{:S(2)}, u32[]{:S(2)}) collective-permute-start(bf16[4,6144]{1,0:T(4,128)(2,1)S(1)} %get-tuple-element.45), channel_id=1, source_target_pairs={{0,3},{1,2},{2,1},{3,0},{4,7},{5,6},{6,5},{7,4},{8,11},{9,10},{10,... | collective-permute-start | bytes 147464 | tf_op jit(solution)/shard_map/ppermute | solution.py:28
  32.3 4.2 %collective-permute-start.12 = (bf16[2,6144]{1,0:T(2,128)(2,1)S(1)}, bf16[2,6144]{1,0:T(2,128)(2,1)S(1)}, u32[]{:S(2)}, u32[]{:S(2)}) collective-permute-start(bf16[2,6144]{1,0:T(2,128)(2,1)S(1)} %slice.42), channel_id=1, source_target_pairs={{0,9},{1,8},{2,11},{3,10},{4,13},{5,12},{6,15},{7,14},{8,1},{9,0},... | collective-permute-start | bytes 73736 | tf_op jit(solution)/shard_map/ppermute | solution.py:28

commit v6 on v5

--- a/solution.py
+++ b/solution.py
@@ -51,7 +51,7 @@
     outer, inner, _ = factors(count)
     if (outer, inner) == (4, 2):
         near, far, side = across(1, 0, count), across(2, 0, count), across(0, 1, count)
-        plane = [0, near, far, side, side ^ near, side ^ far, near ^ far, across(3, 0, count) ^ side]
+        plane = [0, near, far, side, near ^ far, across(3, 0, count) ^ side, side ^ near, side ^ far]
     else:
         column = [0] + [across(z, 0, count) for z in range(1, outer)]
         plane = column + [across(0, y, count) ^ m for y in range(1, inner) for m in column]
@@ -84,7 +84,7 @@
         corner = to(side, 3, 0)
         pair = to(both, 0, 1)
         third = to(far, 1, 0)
-        plane = [jnp.concatenate([block, near, far, side], 0), jnp.concatenate([pair, third, corner], 0)]
+        plane = [jnp.concatenate([block, both, side], 0), jnp.concatenate([third, corner], 0), pair]
     else:
         column = jnp.concatenate([block] + [to(block, z, 0) for z in range(1, outer)], 0)
         (column,) = after((column,), beside)

time: 37.3 us -> 36.9 us (0.989)
    ppermute x13 -> x14, waiting for transfers between devices: 9.48 us -> 9.12 us  [send(): return lax.ppermute(x, 'blk', [(i, i ^ mask) for i in range(count)])]
    ppermute x13 -> x14, starting transfers between devices: 15.6 us -> 15.7 us  [send(): return lax.ppermute(x, 'blk', [(i, i ^ mask) for i in range(count)])]
  transfers between devices with their start and end apart: 13 -> 14, of which waited for: 7 -> 8; matrix products, arithmetic and copies ran while one was open for 2% -> 2% of each run, Pallas kernels for 15% -> 15%
where the time goes in v6:
time: 36.9 us; the launch traced here: 36.7 us
  starting transfers between devices  15.7 us (43%)
  waiting for transfers between devices  9.12 us (25%)
  Pallas kernels  7.99 us (22%)
  local copies, waits for them, and re-layouts  2.43 us (7%)
  between operations  0.77 us (2%)
  other arithmetic  0.69 us (2%)
    ppermute x14, starting transfers between devices, send(): return lax.ppermute(x, 'blk', [(i, i ^ mask) for i in range(count)])  15.7 us
    ppermute x14, waiting for transfers between devices, send(): return lax.ppermute(x, 'blk', [(i, i ^ mask) for i in range(count)])  9.12 us
    pallas_call x1, Pallas kernels, weight_terms(): pl.pallas_call(functools.partial(weight_kernel, step), out_shape=(shape,...  3.31 us
    pallas_call x1, Pallas kernels, forward(): pl.pallas_call(functools.partial(forward_kernel, len(columns)), out_shape...  2.45 us
    unnamed x13, local copies, waits for them, and re-layouts  2.34 us
    pallas_call x2, Pallas kernels, flip(): pl.pallas_call(flip_kernel, out_shape=(jax.ShapeDtypeStruct(w.shape, BF),...  2.01 us
  transfers between devices with their start and end apart: 14, of which 8 were waited for; matrix products, arithmetic and copies ran while one was open for 2% of the time, Pallas kernels for 15%

profile of v6, /device:TPU:0, one launch (start us, length us, event | category | flops | bytes accessed | tf_op | source)
XLA Modules:
  0.0 36.7 jit_solution(7599831234728248490)
XLA Ops:
  0.7 0.8 %copy-done.4 = bf16[1,12288]{1,0:T(2,128)(2,1)S(1)} copy-done((bf16[1,12288]{1,0:T(2,128)(2,1)S(1)}, bf16[1,12288]{1,0:T(2,128)(2,1)}, u32[]{:S(2)}) %copy-start.4) | copy-done | bytes 24600
  1.5 3.5 %collective-permute-start.2 = (bf16[2,18432]{1,0:T(2,128)(2,1)S(1)}, bf16[2,18432]{1,0:T(2,128)(2,1)S(1)}, u32[]{:S(2)}, u32[]{:S(2)}) collective-permute-start(bf16[2,18432]{1,0:T(2,128)(2,1)S(1)} %pack.1), channel_id=1, source_target_pairs={{0,9},{1,8},{2,11},{3,10},{4,13},{5,12},{6,15},{7,14},{8,1},{9,0},... | collective-permute-start | bytes 221192 | tf_op jit(solution)/shard_map/ppermute | solution.py:28
  5.0 1.9 %collective-permute-start.1 = (bf16[2,18432]{1,0:T(2,128)(2,1)S(1)}, bf16[2,18432]{1,0:T(2,128)(2,1)S(1)}, u32[]{:S(2)}, u32[]{:S(2)}) collective-permute-start(bf16[2,18432]{1,0:T(2,128)(2,1)S(1)} %pack.1), channel_id=1, source_target_pairs={{0,5},{1,4},{2,7},{3,6},{4,1},{5,0},{6,3},{7,2},{8,13},{9,12},{10,... | collective-permute-start | bytes 221192 | tf_op jit(solution)/shard_map/ppermute | solution.py:28
  6.9 1.0 %collective-permute-start = (bf16[2,18432]{1,0:T(2,128)(2,1)S(1)}, bf16[2,18432]{1,0:T(2,128)(2,1)S(1)}, u32[]{:S(2)}, u32[]{:S(2)}) collective-permute-start(bf16[2,18432]{1,0:T(2,128)(2,1)S(1)} %pack.1), channel_id=1, source_target_pairs={{0,3},{1,2},{2,1},{3,0},{4,7},{5,6},{6,5},{7,4},{8,11},{9,10},{10,... | collective-permute-start | bytes 221192 | tf_op jit(solution)/shard_map/ppermute | solution.py:28
  7.9 1.0 %flip.2 = (bf16[12288,128]{1,0:T(8,128)(2,1)S(1)}, bf16[128,12288]{1,0:T(8,128)(2,1)S(1)}) custom-call(bf16[12288,128]{1,0:T(8,128)(2,1)S(1)} %copy-done), custom_call_target="tpu_custom_call" | custom-call | bytes 6291456 | tf_op jit(solution)/shard_map/flip/pallas_call | solution.py:141
  8.9 0.9 %copy-done.1 = bf16[12288,128]{1,0:T(8,128)(2,1)S(1)} copy-done((bf16[12288,128]{1,0:T(8,128)(2,1)S(1)}, bf16[12288,128]{1,0:T(8,128)(2,1)}, u32[]{:S(2)}) %copy-start.1) | copy-done | bytes 3145752
  9.8 1.0 %flip.3 = (bf16[12288,128]{1,0:T(8,128)(2,1)S(1)}, bf16[128,12288]{1,0:T(8,128)(2,1)S(1)}) custom-call(bf16[12288,128]{1,0:T(8,128)(2,1)S(1)} %copy-done.1), custom_call_target="tpu_custom_call" | custom-call | bytes 6291456 | tf_op jit(solution)/shard_map/flip/pallas_call | solution.py:141
  10.8 0.2 select.1
  11.0 0.2 pad_maximum_fusion.1.refs_1_
  11.1 0.3 collective-permute-done.refs_0_
  11.4 0.6 %collective-permute-start.3 = (bf16[2,18432]{1,0:T(2,128)(2,1)S(1)}, bf16[2,18432]{1,0:T(2,128)(2,1)S(1)}, u32[]{:S(2)}, u32[]{:S(2)}) collective-permute-start(bf16[2,18432]{1,0:T(2,128)(2,1)S(1)} %get-tuple-element.31), channel_id=1, source_target_pairs={{0,5},{1,4},{2,7},{3,6},{4,1},{5,0},{6,3},{7,2},{8,13},{9,12},{10,... | collective-permute-start | bytes 221192 | tf_op jit(solution)/shard_map/ppermute | solution.py:28
  12.0 1.6 %collective-permute-start.4 = (bf16[2,18432]{1,0:T(2,128)(2,1)S(1)}, bf16[2,18432]{1,0:T(2,128)(2,1)S(1)}, u32[]{:S(2)}, u32[]{:S(2)}) collective-permute-start(bf16[2,18432]{1,0:T(2,128)(2,1)S(1)} %get-tuple-element.30), channel_id=1, source_target_pairs={{0,13},{1,12},{2,15},{3,14},{4,9},{5,8},{6,11},{7,10},{8,5},{9,4},... | collective-permute-start | bytes 221192 | tf_op jit(solution)/shard_map/ppermute | solution.py:28
  13.6 1.6 %collective-permute-start.5 = (bf16[4,18432]{1,0:T(4,128)(2,1)S(1)}, bf16[4,18432]{1,0:T(4,128)(2,1)S(1)}, u32[]{:S(2)}, u32[]{:S(2)}) collective-permute-start(bf16[4,18432]{1,0:T(4,128)(2,1)S(1)} %get-tuple-element.29), channel_id=1, source_target_pairs={{0,3},{1,2},{2,1},{3,0},{4,7},{5,6},{6,5},{7,4},{8,11},{9,10},{10,... | collective-permute-start | bytes 442376 | tf_op jit(solution)/shard_map/ppermute | solution.py:28
  15.1 0.2 pad_maximum_fusion.refs_0_
  15.4 0.1 collective-permute-start.6
  15.5 2.7 %collective-permute-done.4 = bf16[2,18432]{1,0:T(2,128)(2,1)S(1)} collective-permute-done((bf16[2,18432]{1,0:T(2,128)(2,1)S(1)}, bf16[2,18432]{1,0:T(2,128)(2,1)S(1)}, u32[]{:S(2)}, u32[]{:S(2)}) %collective-permute-start.4) | collective-permute-done | bytes 73760 | tf_op jit(solution)/shard_map/ppermute | solution.py:28
  18.2 0.2 pad_maximum_fusion.2.refs_1_
  18.5 0.7 %collective-permute-done.5.refs_2_ = bf16[4,18432]{1,0:T(4,128)(2,1)S(1)} collective-permute-done((bf16[4,18432]{1,0:T(4,128)(2,1)S(1)}, bf16[4,18432]{1,0:T(4,128)(2,1)S(1)}, u32[]{:S(2)}, u32[]{:S(2)}) %collective-permute-start.5) | collective-permute-done | bytes 147488 | tf_op jit(solution)/shard_map/ppermute | solution.py:28
  19.2 0.4 %collective-permute-start.8 = (bf16[4,18432]{1,0:T(4,128)(2,1)S(1)}, bf16[4,18432]{1,0:T(4,128)(2,1)S(1)}, u32[]{:S(2)}, u32[]{:S(2)}) collective-permute-start(bf16[4,18432]{1,0:T(4,128)(2,1)S(1)} %collective-permute-done.5.refs_2_), channel_id=1, source_target_pairs={{0,1},{1,0},{2,3},{3,2},{4,5},{5,4},{6,7},{7,6},{8,9},{9,8},{10,11... | collective-permute-start | bytes 442376 | tf_op jit(solution)/shard_map/ppermute | solution.py:28
  19.6 0.3 collective-permute-done.7.refs_4_
  19.8 0.8 %collective-permute-done.8.refs_5_ = bf16[4,18432]{1,0:T(4,128)(2,1)S(1)} collective-permute-done((bf16[4,18432]{1,0:T(4,128)(2,1)S(1)}, bf16[4,18432]{1,0:T(4,128)(2,1)S(1)}, u32[]{:S(2)}, u32[]{:S(2)}) %collective-permute-start.8) | collective-permute-done | bytes 147488 | tf_op jit(solution)/shard_map/ppermute | solution.py:28
  20.6 2.4 %forward.1 = (bf16[32,12288]{1,0:T(8,128)(2,1)S(1)}, bf16[32,256]{1,0:T(8,128)(2,1)S(1)}, f32[16,6144]{1,0:T(8,128)S(1)}, bf16[16,6144]{1,0:T(8,128)(2,1)S(1)}) custom-call(f32[32,128]{1,0:T(8,128)S(1)} %get-tuple-element.22.refs_3_.flow_ref, bf16[64,32]{1,0:T(8,128)(2,1)S(1)} %get-tuple-element.23.refs_4_.pick_ref, ...), custom_call_target="tpu_custom_call" | custom-call | flops 402653184 | bytes 12582912 | tf_op jit(solution)/shard_map/forward/pallas_call | solution.py:227
  23.0 0.4 %collective-permute-start.9 = (bf16[16,6144]{1,0:T(8,128)(2,1)S(1)}, bf16[16,6144]{1,0:T(8,128)(2,1)S(1)}, u32[]{:S(2)}, u32[]{:S(2)}) collective-permute-start(bf16[16,6144]{1,0:T(8,128)(2,1)S(1)} %get-tuple-element.33), channel_id=1, source_target_pairs={{0,1},{1,0},{2,3},{3,2},{4,5},{5,4},{6,7},{7,6},{8,9},{9,8},{10,11... | collective-permute-start | bytes 589832 | tf_op jit(solution)/shard_map/ppermute | solution.py:28
  23.4 1.1 %collective-permute-done.9 = bf16[16,6144]{1,0:T(8,128)(2,1)S(1)} collective-permute-done((bf16[16,6144]{1,0:T(8,128)(2,1)S(1)}, bf16[16,6144]{1,0:T(8,128)(2,1)S(1)}, u32[]{:S(2)}, u32[]{:S(2)}) %collective-permute-start.9) | collective-permute-done | bytes 196640 | tf_op jit(solution)/shard_map/ppermute | solution.py:28
  24.6 1.2 %collective-permute-start.10 = (bf16[4,6144]{1,0:T(4,128)(2,1)S(1)}, bf16[4,6144]{1,0:T(4,128)(2,1)S(1)}, u32[]{:S(2)}, u32[]{:S(2)}) collective-permute-start(bf16[4,6144]{1,0:T(4,128)(2,1)S(1)} %get-tuple-element.43), channel_id=1, source_target_pairs={{0,5},{1,4},{2,7},{3,6},{4,1},{5,0},{6,3},{7,2},{8,13},{9,12},{10,... | collective-permute-start | bytes 147464 | tf_op jit(solution)/shard_map/ppermute | solution.py:28
  25.8 1.6 %collective-permute-start.12 = (bf16[4,6144]{1,0:T(4,128)(2,1)S(1)}, bf16[4,6144]{1,0:T(4,128)(2,1)S(1)}, u32[]{:S(2)}, u32[]{:S(2)}) collective-permute-start(bf16[4,6144]{1,0:T(4,128)(2,1)S(1)} %get-tuple-element.44), channel_id=1, source_target_pairs={{0,7},{1,6},{2,5},{3,4},{4,3},{5,2},{6,1},{7,0},{8,15},{9,14},{10,... | collective-permute-start | bytes 147464 | tf_op jit(solution)/shard_map/ppermute | solution.py:28
  27.4 0.5 %collective-permute-start.11 = (bf16[4,6144]{1,0:T(4,128)(2,1)S(1)}, bf16[4,6144]{1,0:T(4,128)(2,1)S(1)}, u32[]{:S(2)}, u32[]{:S(2)}) collective-permute-start(bf16[4,6144]{1,0:T(4,128)(2,1)S(1)} %get-tuple-element.45), channel_id=1, source_target_pairs={{0,3},{1,2},{2,1},{3,0},{4,7},{5,6},{6,5},{7,4},{8,11},{9,10},{10,... | collective-permute-start | bytes 147464 | tf_op jit(solution)/shard_map/ppermute | solution.py:28
  27.9 3.3 %weight_terms.1 = (bf16[12288,128]{1,0:T(8,128)(2,1)}, bf16[12288,128]{1,0:T(8,128)(2,1)}) custom-call(bf16[32,12288]{1,0:T(8,128)(2,1)S(1)} %get-tuple-element.34.x_ref, bf16[32,256]{1,0:T(8,128)(2,1)S(1)} %get-tuple-element.35.d_ref), custom_call_target="tpu_custom_call" | custom-call | flops 201326592 | bytes 6291456 | tf_op jit(solution)/shard_map/weight_terms/pallas_call | solution.py:264
  31.2 0.5 %collective-permute-done.11 = bf16[4,6144]{1,0:T(4,128)(2,1)S(1)} collective-permute-done((bf16[4,6144]{1,0:T(4,128)(2,1)S(1)}, bf16[4,6144]{1,0:T(4,128)(2,1)S(1)}, u32[]{:S(2)}, u32[]{:S(2)}) %collective-permute-start.11) | collective-permute-done | bytes 49184 | tf_op jit(solution)/shard_map/ppermute | solution.py:28
  31.8 1.3 %collective-permute-start.13 = (bf16[2,6144]{1,0:T(2,128)(2,1)S(1)}, bf16[2,6144]{1,0:T(2,128)(2,1)S(1)}, u32[]{:S(2)}, u32[]{:S(2)}) collective-permute-start(bf16[2,6144]{1,0:T(2,128)(2,1)S(1)} %slice.42), channel_id=1, source_target_pairs={{0,9},{1,8},{2,11},{3,10},{4,13},{5,12},{6,15},{7,14},{8,1},{9,0},... | collective-permute-start | bytes 73736 | tf_op jit(solution)/shard_map/ppermute | solution.py:28
  33.0 2.9 %collective-permute-done.13 = bf16[2,6144]{1,0:T(2,128)(2,1)S(1)} collective-permute-done((bf16[2,6144]{1,0:T(2,128)(2,1)S(1)}, bf16[2,6144]{1,0:T(2,128)(2,1)S(1)}, u32[]{:S(2)}, u32[]{:S(2)}) %collective-permute-start.13) | collective-permute-done | bytes 24608 | tf_op jit(solution)/shard_map/ppermute | solution.py:28
  36.0 0.7 %copy.12 = bf16[1,1,2,6144]{3,1,2,0:T(2,128)(2,1)} copy(bf16[1,1,2,6144]{3,2,1,0:T(2,128)(2,1)S(1)} %fusion.2) | data formatting | bytes 49152
  (25 shorter events, 0.4 us)
Async XLA Ops:
  0.6 0.8 %copy-start.4 = (bf16[1,12288]{1,0:T(2,128)(2,1)S(1)}, bf16[1,12288]{1,0:T(2,128)(2,1)}, u32[]{:S(2)}) copy-start(bf16[1,12288]{1,0:T(2,128)(2,1)} %parent_ref.1) | copy-start | bytes 73732
  0.6 0.8 %copy-start.5 = (bf16[2,12288]{1,0:T(2,128)(2,1)S(1)}, bf16[2,12288]{1,0:T(2,128)(2,1)}, u32[]{:S(2)}) copy-start(bf16[2,12288]{1,0:T(2,128)(2,1)} %token_ref.1) | copy-start | bytes 147460
  1.5 6.4 %copy-start = (bf16[12288,128]{1,0:T(8,128)(2,1)S(1)}, bf16[12288,128]{1,0:T(8,128)(2,1)}, u32[]{:S(2)}) copy-start(bf16[12288,128]{1,0:T(8,128)(2,1)} %w_ref.2) | copy-start | bytes 9437188
  1.5 9.5 %collective-permute-start.2 = (bf16[2,18432]{1,0:T(2,128)(2,1)S(1)}, bf16[2,18432]{1,0:T(2,128)(2,1)S(1)}, u32[]{:S(2)}, u32[]{:S(2)}) collective-permute-start(bf16[2,18432]{1,0:T(2,128)(2,1)S(1)} %pack.1), channel_id=1, source_target_pairs={{0,9},{1,8},{2,11},{3,10},{4,13},{5,12},{6,15},{7,14},{8,1},{9,0},... | collective-permute-start | bytes 221192 | tf_op jit(solution)/shard_map/ppermute | solution.py:28
  5.0 5.9 %collective-permute-start.1 = (bf16[2,18432]{1,0:T(2,128)(2,1)S(1)}, bf16[2,18432]{1,0:T(2,128)(2,1)S(1)}, u32[]{:S(2)}, u32[]{:S(2)}) collective-permute-start(bf16[2,18432]{1,0:T(2,128)(2,1)S(1)} %pack.1), channel_id=1, source_target_pairs={{0,5},{1,4},{2,7},{3,6},{4,1},{5,0},{6,3},{7,2},{8,13},{9,12},{10,... | collective-permute-start | bytes 221192 | tf_op jit(solution)/shard_map/ppermute | solution.py:28
  6.9 4.5 %collective-permute-start = (bf16[2,18432]{1,0:T(2,128)(2,1)S(1)}, bf16[2,18432]{1,0:T(2,128)(2,1)S(1)}, u32[]{:S(2)}, u32[]{:S(2)}) collective-permute-start(bf16[2,18432]{1,0:T(2,128)(2,1)S(1)} %pack.1), channel_id=1, source_target_pairs={{0,3},{1,2},{2,1},{3,0},{4,7},{5,6},{6,5},{7,4},{8,11},{9,10},{10,... | collective-permute-start | bytes 221192 | tf_op jit(solution)/shard_map/ppermute | solution.py:28
  7.9 1.9 %copy-start.1 = (bf16[12288,128]{1,0:T(8,128)(2,1)S(1)}, bf16[12288,128]{1,0:T(8,128)(2,1)}, u32[]{:S(2)}) copy-start(bf16[12288,128]{1,0:T(8,128)(2,1)} %w_ref.3) | copy-start | bytes 9437188
  7.9 2.9 %copy-start.2 = (bf16[32,128]{1,0:T(8,128)(2,1)S(1)}, bf16[32,128]{1,0:T(8,128)(2,1)}, u32[]{:S(2)}) copy-start(bf16[32,128]{1,0:T(8,128)(2,1)} %flow_ref.1) | copy-start | bytes 24580
  7.9 2.9 %copy-start.3 = (s32[32]{0:T(128)S(1)}, s32[32]{0:T(128)}, u32[]{:S(2)}) copy-start(s32[32]{0:T(128)} %param.8) | copy-start | bytes 388
  11.4 4.1 %collective-permute-start.3 = (bf16[2,18432]{1,0:T(2,128)(2,1)S(1)}, bf16[2,18432]{1,0:T(2,128)(2,1)S(1)}, u32[]{:S(2)}, u32[]{:S(2)}) collective-permute-start(bf16[2,18432]{1,0:T(2,128)(2,1)S(1)} %get-tuple-element.31), channel_id=1, source_target_pairs={{0,5},{1,4},{2,7},{3,6},{4,1},{5,0},{6,3},{7,2},{8,13},{9,12},{10,... | collective-permute-start | bytes 221192 | tf_op jit(solution)/shard_map/ppermute | solution.py:28
  12.0 6.3 %collective-permute-start.4 = (bf16[2,18432]{1,0:T(2,128)(2,1)S(1)}, bf16[2,18432]{1,0:T(2,128)(2,1)S(1)}, u32[]{:S(2)}, u32[]{:S(2)}) collective-permute-start(bf16[2,18432]{1,0:T(2,128)(2,1)S(1)} %get-tuple-element.30), channel_id=1, source_target_pairs={{0,13},{1,12},{2,15},{3,14},{4,9},{5,8},{6,11},{7,10},{8,5},{9,4},... | collective-permute-start | bytes 221192 | tf_op jit(solution)/shard_map/ppermute | solution.py:28
  13.6 5.6 %collective-permute-start.5 = (bf16[4,18432]{1,0:T(4,128)(2,1)S(1)}, bf16[4,18432]{1,0:T(4,128)(2,1)S(1)}, u32[]{:S(2)}, u32[]{:S(2)}) collective-permute-start(bf16[4,18432]{1,0:T(4,128)(2,1)S(1)} %get-tuple-element.29), channel_id=1, source_target_pairs={{0,3},{1,2},{2,1},{3,0},{4,7},{5,6},{6,5},{7,4},{8,11},{9,10},{10,... | collective-permute-start | bytes 442376 | tf_op jit(solution)/shard_map/ppermute | solution.py:28
  15.4 5.2 %collective-permute-start.6 = (bf16[8,18432]{1,0:T(8,128)(2,1)S(1)}, bf16[8,18432]{1,0:T(8,128)(2,1)S(1)}, u32[]{:S(2)}, u32[]{:S(2)}) collective-permute-start(bf16[8,18432]{1,0:T(8,128)(2,1)S(1)} %pad_maximum_fusion.refs_0_), channel_id=1, source_target_pairs={{0,1},{1,0},{2,3},{3,2},{4,5},{5,4},{6,7},{7,6},{8,9},{9,8},{10,11... | collective-permute-start | bytes 884744 | tf_op jit(solution)/shard_map/ppermute | solution.py:28
  18.4 1.4 %collective-permute-start.7 = (bf16[4,18432]{1,0:T(4,128)(2,1)S(1)}, bf16[4,18432]{1,0:T(4,128)(2,1)S(1)}, u32[]{:S(2)}, u32[]{:S(2)}) collective-permute-start(bf16[4,18432]{1,0:T(4,128)(2,1)S(1)} %pad_maximum_fusion.2.refs_1_), channel_id=1, source_target_pairs={{0,1},{1,0},{2,3},{3,2},{4,5},{5,4},{6,7},{7,6},{8,9},{9,8},{10,11... | collective-permute-start | bytes 442376 | tf_op jit(solution)/shard_map/ppermute | solution.py:28
  19.2 1.4 %collective-permute-start.8 = (bf16[4,18432]{1,0:T(4,128)(2,1)S(1)}, bf16[4,18432]{1,0:T(4,128)(2,1)S(1)}, u32[]{:S(2)}, u32[]{:S(2)}) collective-permute-start(bf16[4,18432]{1,0:T(4,128)(2,1)S(1)} %collective-permute-done.5.refs_2_), channel_id=1, source_target_pairs={{0,1},{1,0},{2,3},{3,2},{4,5},{5,4},{6,7},{7,6},{8,9},{9,8},{10,11... | collective-permute-start | bytes 442376 | tf_op jit(solution)/shard_map/ppermute | solution.py:28
  23.0 1.5 %collective-permute-start.9 = (bf16[16,6144]{1,0:T(8,128)(2,1)S(1)}, bf16[16,6144]{1,0:T(8,128)(2,1)S(1)}, u32[]{:S(2)}, u32[]{:S(2)}) collective-permute-start(bf16[16,6144]{1,0:T(8,128)(2,1)S(1)} %get-tuple-element.33), channel_id=1, source_target_pairs={{0,1},{1,0},{2,3},{3,2},{4,5},{5,4},{6,7},{7,6},{8,9},{9,8},{10,11... | collective-permute-start | bytes 589832 | tf_op jit(solution)/shard_map/ppermute | solution.py:28
  24.6 6.6 %collective-permute-start.10 = (bf16[4,6144]{1,0:T(4,128)(2,1)S(1)}, bf16[4,6144]{1,0:T(4,128)(2,1)S(1)}, u32[]{:S(2)}, u32[]{:S(2)}) collective-permute-start(bf16[4,6144]{1,0:T(4,128)(2,1)S(1)} %get-tuple-element.43), channel_id=1, source_target_pairs={{0,5},{1,4},{2,7},{3,6},{4,1},{5,0},{6,3},{7,2},{8,13},{9,12},{10,... | collective-permute-start | bytes 147464 | tf_op jit(solution)/shard_map/ppermute | solution.py:28
  25.8 5.4 %collective-permute-start.12 = (bf16[4,6144]{1,0:T(4,128)(2,1)S(1)}, bf16[4,6144]{1,0:T(4,128)(2,1)S(1)}, u32[]{:S(2)}, u32[]{:S(2)}) collective-permute-start(bf16[4,6144]{1,0:T(4,128)(2,1)S(1)} %get-tuple-element.44), channel_id=1, source_target_pairs={{0,7},{1,6},{2,5},{3,4},{4,3},{5,2},{6,1},{7,0},{8,15},{9,14},{10,... | collective-permute-start | bytes 147464 | tf_op jit(solution)/shard_map/ppermute | solution.py:28
  27.4 4.3 %collective-permute-start.11 = (bf16[4,6144]{1,0:T(4,128)(2,1)S(1)}, bf16[4,6144]{1,0:T(4,128)(2,1)S(1)}, u32[]{:S(2)}, u32[]{:S(2)}) collective-permute-start(bf16[4,6144]{1,0:T(4,128)(2,1)S(1)} %get-tuple-element.45), channel_id=1, source_target_pairs={{0,3},{1,2},{2,1},{3,0},{4,7},{5,6},{6,5},{7,4},{8,11},{9,10},{10,... | collective-permute-start | bytes 147464 | tf_op jit(solution)/shard_map/ppermute | solution.py:28
  31.8 4.2 %collective-permute-start.13 = (bf16[2,6144]{1,0:T(2,128)(2,1)S(1)}, bf16[2,6144]{1,0:T(2,128)(2,1)S(1)}, u32[]{:S(2)}, u32[]{:S(2)}) collective-permute-start(bf16[2,6144]{1,0:T(2,128)(2,1)S(1)} %slice.42), channel_id=1, source_target_pairs={{0,9},{1,8},{2,11},{3,10},{4,13},{5,12},{6,15},{7,14},{8,1},{9,0},... | collective-permute-start | bytes 73736 | tf_op jit(solution)/shard_map/ppermute | solution.py:28

commit v7 on v6

--- a/solution.py
+++ b/solution.py
@@ -36,7 +36,7 @@
     outer, inner, _ = factors(count)
     z_steps = [1 << i for i in range(outer.bit_length() - 1)]
     y_steps = [1 << i for i in range(inner.bit_length() - 1)]
-    squares = [[0, across(z, 0, count), across(0, y, count), across(z, y, count)] for z, y in zip(z_steps, y_steps)]
+    squares = [[0, across(0, y, count), across(z, 0, count), across(z, y, count)] for z, y in zip(z_steps, y_steps)]
     return [[0, 1]] + squares + [[0, across(z, 0, count)] for z in z_steps[len(y_steps):]]
 
 
@@ -187,7 +187,7 @@
 def forward_kernel(columns, flow_ref, pick_ref, sums_ref, wg_ref, wu_ref, wgt_ref, wut_ref, *refs):
     cols, (x_ref, d_ref, own_ref, out_ref) = refs[:columns], refs[columns:]
     hyp = flow_ref.shape[0]
-    width = wg_ref.shape[0]
+    width, hidden = wg_ref.shape
     half = width // 2
     rows = sums_ref.shape[0] // 2
     count = rows // 2
@@ -210,12 +210,13 @@
     d = jnp.concatenate([d_gate, d_up], 1)
     d_ref[...] = d
     sums = jnp.dot(sums_ref[...], d, preferred_element_type=F32).astype(BF)
+    even, odd = sums[:rows], sums[rows:]
     for at in range(0, half, step):
         here, there = pl.ds(at, step), pl.ds(at + half, step)
-        w0 = jnp.concatenate([wgt_ref[:, here], wut_ref[:, here]], 0)
-        w1 = jnp.concatenate([wgt_ref[:, there], wut_ref[:, there]], 0)
-        term = jnp.dot(sums[:rows], w0, preferred_element_type=F32)
-        term = term + jnp.dot(sums[rows:], w1, preferred_element_type=F32)
+        term = jnp.dot(even[:, :hidden], wgt_ref[:, here], preferred_element_type=F32)
+        term = term + jnp.dot(even[:, hidden:], wut_ref[:, here], preferred_element_type=F32)
+        term = term + jnp.dot(odd[:, :hidden], wgt_ref[:, there], preferred_element_type=F32)
+        term = term + jnp.dot(odd[:, hidden:], wut_ref[:, there], preferred_element_type=F32)
         own_ref[:, here] = term[:count]
         out_ref[:, here] = term[count:].astype(BF)
 
@@ -240,41 +241,36 @@
     )(flow, pick, sums, w_gate, w_up, flip_gate, flip_up, *columns)
 
 
-def weight_kernel(step, x_ref, d_ref, gate_ref, up_ref, gate_buf, up_buf, sems):
+def weight_kernel(side, step, x_ref, d_ref, *refs):
+    out_ref, done_ref, buf, sems = refs[-4:]
     over = (((0,), (0,)), ((), ()))
-    hidden = gate_ref.shape[1]
+    hidden = out_ref.shape[1]
     copies = []
     for i in range(x_ref.shape[1] // step):
         rows = pl.ds(i * step, step)
-        term = lax.dot_general(x_ref[:, rows], d_ref[...], over, preferred_element_type=F32)
-        gate_buf[rows, :] = term[:, :hidden].astype(BF)
-        up_buf[rows, :] = term[:, hidden:].astype(BF)
-        for j, (buf, ref) in enumerate(((gate_buf, gate_ref), (up_buf, up_ref))):
-            copies.append(pltpu.make_async_copy(buf.at[rows], ref.at[rows], sems.at[2 * i + j]))
-            copies[-1].start()
+        d = d_ref[:, side * hidden:(side + 1) * hidden]
+        buf[rows, :] = lax.dot_general(x_ref[:, rows], d, over, preferred_element_type=F32).astype(BF)
+        copies.append(pltpu.make_async_copy(buf.at[rows], out_ref.at[rows], sems.at[i]))
+        copies[-1].start()
+    done_ref[...] = jnp.zeros_like(done_ref)
     for copy in copies:
         copy.wait()
 
 
-def weight_terms(x, d):
+def weight_terms(x, d, side, *deps):
     hyp, width = x.shape
     hidden = d.shape[1] // 2
     step = 1024
-    shape = jax.ShapeDtypeStruct((width, hidden), BF)
-    return pl.pallas_call(
-        functools.partial(weight_kernel, step),
-        out_shape=(shape, shape),
-        in_specs=[VMEM] * 2,
-        out_specs=(HBM,) * 2,
-        scratch_shapes=[
-            pltpu.VMEM((width, hidden), BF),
-            pltpu.VMEM((width, hidden), BF),
-            pltpu.SemaphoreType.DMA((2 * (width // step),)),
-        ],
+    return pl.pallas_call(
+        functools.partial(weight_kernel, side, step),
+        out_shape=(jax.ShapeDtypeStruct((width, hidden), BF), jax.ShapeDtypeStruct((8, 128), F32)),
+        in_specs=[VMEM] * 2 + [ANY] * len(deps),
+        out_specs=(HBM, VMEM),
+        scratch_shapes=[pltpu.VMEM((width, hidden), BF), pltpu.SemaphoreType.DMA((width // step,))],
         compiler_params=pltpu.CompilerParams(vmem_limit_bytes=24 * MIB),
-        cost_estimate=pl.CostEstimate(flops=4 * hyp * width * hidden, bytes_accessed=4 * width * hidden, transcendentals=0),
+        cost_estimate=pl.CostEstimate(flops=2 * hyp * width * hidden, bytes_accessed=2 * width * hidden, transcendentals=0),
         name="weight_terms",
-    )(x, d)
+    )(x, d, *deps)
 
 
 def body(parent_rows, token_rows, parent, d_hidden, w_gate, w_up):
@@ -289,15 +285,22 @@
     (flow, pick, sums), (w_gate, flip_gate), (w_up, flip_up) = beside
     x, d, own, other = forward(flow, pick, sums, w_gate, w_up, flip_gate, flip_up, columns)
     rows = own + send(other, 1, count).astype(F32)
-    for i, stage in enumerate(scatter_stages(count)[1:]):
+    grad_gate, done = weight_terms(x, d, 0)
+    stages = scatter_stages(count)[1:]
+    for i, stage in enumerate(stages):
         size = rows.shape[0] // len(stage)
         parts = [rows[j * size:(j + 1) * size] for j in range(len(stage))]
+        outgoing = [part.astype(BF) for part in parts[1:]]
+        if i == len(stages) - 1:
+            outgoing = after(outgoing, done)
+            grad_up, done = weight_terms(x, d, 1, outgoing[0])
+        arrived = [send(part, mask, count) for mask, part in zip(stage[1:], outgoing)]
+        if i == len(stages) - 1:
+            arrived = after(arrived, done)
         rows = parts[0]
-        for mask, part in zip(stage[1:], parts[1:]):
-            rows = rows + send(part.astype(BF), mask, count).astype(F32)
-        if i == 0:
-            rows, weights = lax.optimization_barrier((rows, weight_terms(x, d)))
-    return *weights, rows.astype(BF).reshape(1, width)
+        for part in arrived:
+            rows = rows + part.astype(F32)
+    return grad_gate, grad_up, rows.astype(BF).reshape(1, width)
 
 
 def solution(mesh):

time: 36.9 us -> 35.9 us (0.973)
  waiting for transfers between devices: 9.12 us -> 7.67 us
  Pallas kernels: 7.99 us -> 8.64 us
    ppermute x14, waiting for transfers between devices: 9.12 us -> 7.67 us  [send(): return lax.ppermute(x, 'blk', [(i, i ^ mask) for i in range(count)])]
    pallas_call x1 -> x2, Pallas kernels: 3.31 us -> 4.19 us  [weight_terms(): pl.pallas_call(functools.partial(weight_kernel, side, step), out_shape=(j...]
  transfers between devices with their start and end apart: 14 -> 14, of which waited for: 8 -> 9; matrix products, arithmetic and copies ran while one was open for 2% -> 2% of each run, Pallas kernels for 15% -> 18%
where the time goes in v7:
time: 35.9 us; the launch traced here: 35.8 us
  starting transfers between devices  15.5 us (43%)
  Pallas kernels  8.64 us (24%)
  waiting for transfers between devices  7.67 us (21%)
  local copies, waits for them, and re-layouts  2.43 us (7%)
  between operations  0.79 us (2%)
  other arithmetic  0.68 us (2%)
    ppermute x14, starting transfers between devices, send(): return lax.ppermute(x, 'blk', [(i, i ^ mask) for i in range(count)])  15.5 us
    ppermute x14, waiting for transfers between devices, send(): return lax.ppermute(x, 'blk', [(i, i ^ mask) for i in range(count)])  7.67 us
    pallas_call x2, Pallas kernels, weight_terms(): pl.pallas_call(functools.partial(weight_kernel, side, step), out_shape=(j...  4.19 us
    unnamed x13, local copies, waits for them, and re-layouts  2.34 us
    pallas_call x1, Pallas kernels, forward(): pl.pallas_call(functools.partial(forward_kernel, len(columns)), out_shape...  2.22 us
    pallas_call x2, Pallas kernels, flip(): pl.pallas_call(flip_kernel, out_shape=(jax.ShapeDtypeStruct(w.shape, BF),...  2.01 us
  transfers between devices with their start and end apart: 14, of which 9 were waited for; matrix products, arithmetic and copies ran while one was open for 2% of the time, Pallas kernels for 18%

profile of v7, /device:TPU:0, one launch (start us, length us, event | category | flops | bytes accessed | tf_op | source)
XLA Modules:
  0.0 35.8 jit_solution(15349841109575907606)
XLA Ops:
  0.7 0.8 %copy-done.4 = bf16[1,12288]{1,0:T(2,128)(2,1)S(1)} copy-done((bf16[1,12288]{1,0:T(2,128)(2,1)S(1)}, bf16[1,12288]{1,0:T(2,128)(2,1)}, u32[]{:S(2)}) %copy-start.4) | copy-done | bytes 24600
  1.5 3.5 %collective-permute-start.2 = (bf16[2,18432]{1,0:T(2,128)(2,1)S(1)}, bf16[2,18432]{1,0:T(2,128)(2,1)S(1)}, u32[]{:S(2)}, u32[]{:S(2)}) collective-permute-start(bf16[2,18432]{1,0:T(2,128)(2,1)S(1)} %pack.1), channel_id=1, source_target_pairs={{0,9},{1,8},{2,11},{3,10},{4,13},{5,12},{6,15},{7,14},{8,1},{9,0},... | collective-permute-start | bytes 221192 | tf_op jit(solution)/shard_map/ppermute | solution.py:28
  5.0 1.9 %collective-permute-start.1 = (bf16[2,18432]{1,0:T(2,128)(2,1)S(1)}, bf16[2,18432]{1,0:T(2,128)(2,1)S(1)}, u32[]{:S(2)}, u32[]{:S(2)}) collective-permute-start(bf16[2,18432]{1,0:T(2,128)(2,1)S(1)} %pack.1), channel_id=1, source_target_pairs={{0,5},{1,4},{2,7},{3,6},{4,1},{5,0},{6,3},{7,2},{8,13},{9,12},{10,... | collective-permute-start | bytes 221192 | tf_op jit(solution)/shard_map/ppermute | solution.py:28
  6.9 1.0 %collective-permute-start = (bf16[2,18432]{1,0:T(2,128)(2,1)S(1)}, bf16[2,18432]{1,0:T(2,128)(2,1)S(1)}, u32[]{:S(2)}, u32[]{:S(2)}) collective-permute-start(bf16[2,18432]{1,0:T(2,128)(2,1)S(1)} %pack.1), channel_id=1, source_target_pairs={{0,3},{1,2},{2,1},{3,0},{4,7},{5,6},{6,5},{7,4},{8,11},{9,10},{10,... | collective-permute-start | bytes 221192 | tf_op jit(solution)/shard_map/ppermute | solution.py:28
  7.9 1.0 %flip.2 = (bf16[12288,128]{1,0:T(8,128)(2,1)S(1)}, bf16[128,12288]{1,0:T(8,128)(2,1)S(1)}) custom-call(bf16[12288,128]{1,0:T(8,128)(2,1)S(1)} %copy-done), custom_call_target="tpu_custom_call" | custom-call | bytes 6291456 | tf_op jit(solution)/shard_map/flip/pallas_call | solution.py:141
  8.9 0.9 %copy-done.1 = bf16[12288,128]{1,0:T(8,128)(2,1)S(1)} copy-done((bf16[12288,128]{1,0:T(8,128)(2,1)S(1)}, bf16[12288,128]{1,0:T(8,128)(2,1)}, u32[]{:S(2)}) %copy-start.1) | copy-done | bytes 3145752
  9.8 1.0 %flip.3 = (bf16[12288,128]{1,0:T(8,128)(2,1)S(1)}, bf16[128,12288]{1,0:T(8,128)(2,1)S(1)}) custom-call(bf16[12288,128]{1,0:T(8,128)(2,1)S(1)} %copy-done.1), custom_call_target="tpu_custom_call" | custom-call | bytes 6291456 | tf_op jit(solution)/shard_map/flip/pallas_call | solution.py:141
  10.8 0.2 select.1
  11.0 0.2 pad_maximum_fusion.1.refs_1_
  11.1 0.3 collective-permute-done.refs_0_
  11.4 0.6 %collective-permute-start.3 = (bf16[2,18432]{1,0:T(2,128)(2,1)S(1)}, bf16[2,18432]{1,0:T(2,128)(2,1)S(1)}, u32[]{:S(2)}, u32[]{:S(2)}) collective-permute-start(bf16[2,18432]{1,0:T(2,128)(2,1)S(1)} %get-tuple-element.30), channel_id=1, source_target_pairs={{0,5},{1,4},{2,7},{3,6},{4,1},{5,0},{6,3},{7,2},{8,13},{9,12},{10,... | collective-permute-start | bytes 221192 | tf_op jit(solution)/shard_map/ppermute | solution.py:28
  12.0 1.6 %collective-permute-start.4 = (bf16[2,18432]{1,0:T(2,128)(2,1)S(1)}, bf16[2,18432]{1,0:T(2,128)(2,1)S(1)}, u32[]{:S(2)}, u32[]{:S(2)}) collective-permute-start(bf16[2,18432]{1,0:T(2,128)(2,1)S(1)} %get-tuple-element.29), channel_id=1, source_target_pairs={{0,13},{1,12},{2,15},{3,14},{4,9},{5,8},{6,11},{7,10},{8,5},{9,4},... | collective-permute-start | bytes 221192 | tf_op jit(solution)/shard_map/ppermute | solution.py:28
  13.6 1.6 %collective-permute-start.5 = (bf16[4,18432]{1,0:T(4,128)(2,1)S(1)}, bf16[4,18432]{1,0:T(4,128)(2,1)S(1)}, u32[]{:S(2)}, u32[]{:S(2)}) collective-permute-start(bf16[4,18432]{1,0:T(4,128)(2,1)S(1)} %get-tuple-element.28), channel_id=1, source_target_pairs={{0,3},{1,2},{2,1},{3,0},{4,7},{5,6},{6,5},{7,4},{8,11},{9,10},{10,... | collective-permute-start | bytes 442376 | tf_op jit(solution)/shard_map/ppermute | solution.py:28
  15.1 0.2 pad_maximum_fusion.refs_0_
  15.5 2.7 %collective-permute-done.4 = bf16[2,18432]{1,0:T(2,128)(2,1)S(1)} collective-permute-done((bf16[2,18432]{1,0:T(2,128)(2,1)S(1)}, bf16[2,18432]{1,0:T(2,128)(2,1)S(1)}, u32[]{:S(2)}, u32[]{:S(2)}) %collective-permute-start.4) | collective-permute-done | bytes 73760 | tf_op jit(solution)/shard_map/ppermute | solution.py:28
  18.5 0.7 %collective-permute-done.5.refs_2_ = bf16[4,18432]{1,0:T(4,128)(2,1)S(1)} collective-permute-done((bf16[4,18432]{1,0:T(4,128)(2,1)S(1)}, bf16[4,18432]{1,0:T(4,128)(2,1)S(1)}, u32[]{:S(2)}, u32[]{:S(2)}) %collective-permute-start.5) | collective-permute-done | bytes 147488 | tf_op jit(solution)/shard_map/ppermute | solution.py:28
  19.2 0.4 %collective-permute-start.8 = (bf16[4,18432]{1,0:T(4,128)(2,1)S(1)}, bf16[4,18432]{1,0:T(4,128)(2,1)S(1)}, u32[]{:S(2)}, u32[]{:S(2)}) collective-permute-start(bf16[4,18432]{1,0:T(4,128)(2,1)S(1)} %collective-permute-done.5.refs_2_), channel_id=1, source_target_pairs={{0,1},{1,0},{2,3},{3,2},{4,5},{5,4},{6,7},{7,6},{8,9},{9,8},{10,11... | collective-permute-start | bytes 442376 | tf_op jit(solution)/shard_map/ppermute | solution.py:28
  19.6 0.3 collective-permute-done.7.refs_4_
  19.8 0.8 %collective-permute-done.8.refs_5_ = bf16[4,18432]{1,0:T(4,128)(2,1)S(1)} collective-permute-done((bf16[4,18432]{1,0:T(4,128)(2,1)S(1)}, bf16[4,18432]{1,0:T(4,128)(2,1)S(1)}, u32[]{:S(2)}, u32[]{:S(2)}) %collective-permute-start.8) | collective-permute-done | bytes 147488 | tf_op jit(solution)/shard_map/ppermute | solution.py:28
  20.6 2.2 %forward.1 = (bf16[32,12288]{1,0:T(8,128)(2,1)S(1)}, bf16[32,256]{1,0:T(8,128)(2,1)S(1)}, f32[16,6144]{1,0:T(8,128)S(1)}, bf16[16,6144]{1,0:T(8,128)(2,1)S(1)}) custom-call(f32[32,128]{1,0:T(8,128)S(1)} %get-tuple-element.21.refs_3_.flow_ref, bf16[64,32]{1,0:T(8,128)(2,1)S(1)} %get-tuple-element.22.refs_4_.pick_ref, ...), custom_call_target="tpu_custom_call" | custom-call | flops 402653184 | bytes 12582912 | tf_op jit(solution)/shard_map/forward/pallas_call | solution.py:228
  22.8 0.4 %collective-permute-start.9 = (bf16[16,6144]{1,0:T(8,128)(2,1)S(1)}, bf16[16,6144]{1,0:T(8,128)(2,1)S(1)}, u32[]{:S(2)}, u32[]{:S(2)}) collective-permute-start(bf16[16,6144]{1,0:T(8,128)(2,1)S(1)} %get-tuple-element.35), channel_id=1, source_target_pairs={{0,1},{1,0},{2,3},{3,2},{4,5},{5,4},{6,7},{7,6},{8,9},{9,8},{10,11... | collective-permute-start | bytes 589832 | tf_op jit(solution)/shard_map/ppermute | solution.py:28
  23.2 1.1 %collective-permute-done.9 = bf16[16,6144]{1,0:T(8,128)(2,1)S(1)} collective-permute-done((bf16[16,6144]{1,0:T(8,128)(2,1)S(1)}, bf16[16,6144]{1,0:T(8,128)(2,1)S(1)}, u32[]{:S(2)}, u32[]{:S(2)}) %collective-permute-start.9) | collective-permute-done | bytes 196640 | tf_op jit(solution)/shard_map/ppermute | solution.py:28
  24.4 1.6 %collective-permute-start.10 = (bf16[4,6144]{1,0:T(4,128)(2,1)S(1)}, bf16[4,6144]{1,0:T(4,128)(2,1)S(1)}, u32[]{:S(2)}, u32[]{:S(2)}) collective-permute-start(bf16[4,6144]{1,0:T(4,128)(2,1)S(1)} %get-tuple-element.41), channel_id=1, source_target_pairs={{0,3},{1,2},{2,1},{3,0},{4,7},{5,6},{6,5},{7,4},{8,11},{9,10},{10,... | collective-permute-start | bytes 147464 | tf_op jit(solution)/shard_map/ppermute | solution.py:28
  26.0 1.1 %collective-permute-start.12 = (bf16[4,6144]{1,0:T(4,128)(2,1)S(1)}, bf16[4,6144]{1,0:T(4,128)(2,1)S(1)}, u32[]{:S(2)}, u32[]{:S(2)}) collective-permute-start(bf16[4,6144]{1,0:T(4,128)(2,1)S(1)} %get-tuple-element.42), channel_id=1, source_target_pairs={{0,7},{1,6},{2,5},{3,4},{4,3},{5,2},{6,1},{7,0},{8,15},{9,14},{10,... | collective-permute-start | bytes 147464 | tf_op jit(solution)/shard_map/ppermute | solution.py:28
  27.1 0.6 %collective-permute-start.11 = (bf16[4,6144]{1,0:T(4,128)(2,1)S(1)}, bf16[4,6144]{1,0:T(4,128)(2,1)S(1)}, u32[]{:S(2)}, u32[]{:S(2)}) collective-permute-start(bf16[4,6144]{1,0:T(4,128)(2,1)S(1)} %get-tuple-element.43), channel_id=1, source_target_pairs={{0,5},{1,4},{2,7},{3,6},{4,1},{5,0},{6,3},{7,2},{8,13},{9,12},{10,... | collective-permute-start | bytes 147464 | tf_op jit(solution)/shard_map/ppermute | solution.py:28
  27.7 2.1 %weight_terms.2 = (bf16[12288,128]{1,0:T(8,128)(2,1)}, f32[8,128]{1,0:T(8,128)S(1)}) custom-call(bf16[32,12288]{1,0:T(8,128)(2,1)S(1)} %get-tuple-element.31.x_ref, bf16[32,256]{1,0:T(8,128)(2,1)S(1)} %get-tuple-element.32.d_ref), custom_call_target="tpu_custom_call" | custom-call | flops 100663296 | bytes 3145728 | tf_op jit(solution)/shard_map/weight_terms/pallas_call | solution.py:264
  29.8 0.8 %collective-permute-done.12 = bf16[4,6144]{1,0:T(4,128)(2,1)S(1)} collective-permute-done((bf16[4,6144]{1,0:T(4,128)(2,1)S(1)}, bf16[4,6144]{1,0:T(4,128)(2,1)S(1)}, u32[]{:S(2)}, u32[]{:S(2)}) %collective-permute-start.12) | collective-permute-done | bytes 49184 | tf_op jit(solution)/shard_map/ppermute | solution.py:28
  30.6 0.2 collective-permute-done.11
  30.9 1.1 %collective-permute-start.13 = (bf16[2,6144]{1,0:T(2,128)(2,1)S(1)}, bf16[2,6144]{1,0:T(2,128)(2,1)S(1)}, u32[]{:S(2)}, u32[]{:S(2)}) collective-permute-start(bf16[2,6144]{1,0:T(2,128)(2,1)S(1)} %after.4.refs_0_), channel_id=1, source_target_pairs={{0,9},{1,8},{2,11},{3,10},{4,13},{5,12},{6,15},{7,14},{8,1},{9,0},... | collective-permute-start | bytes 73736 | tf_op jit(solution)/shard_map/ppermute | solution.py:28
  32.0 2.1 %weight_terms.3 = (bf16[12288,128]{1,0:T(8,128)(2,1)}, f32[8,128]{1,0:T(8,128)S(1)}) custom-call(bf16[32,12288]{1,0:T(8,128)(2,1)S(1)} %get-tuple-element.31.x_ref, bf16[32,256]{1,0:T(8,128)(2,1)S(1)} %get-tuple-element.32.d_ref, bf16[2,6144]{1,0:T(2,128)(2,1)S(1)} %after.4.refs_0_), custom_call_target="tpu_custom_call" | custom-call | flops 100663296 | bytes 3145728 | tf_op jit(solution)/shard_map/weight_terms/pallas_call | solution.py:264
  34.1 1.0 %collective-permute-done.13.refs_0_ = bf16[2,6144]{1,0:T(2,128)(2,1)S(1)} collective-permute-done((bf16[2,6144]{1,0:T(2,128)(2,1)S(1)}, bf16[2,6144]{1,0:T(2,128)(2,1)S(1)}, u32[]{:S(2)}, u32[]{:S(2)}) %collective-permute-start.13) | collective-permute-done | bytes 24608 | tf_op jit(solution)/shard_map/ppermute | solution.py:28
  35.1 0.7 %copy.14 = bf16[1,1,2,6144]{3,1,2,0:T(2,128)(2,1)} copy(bf16[1,1,2,6144]{3,2,1,0:T(2,128)(2,1)S(1)} %fusion.3) | data formatting | bytes 49152
  (28 shorter events, 0.7 us)
Async XLA Ops:
  0.6 0.8 %copy-start.4 = (bf16[1,12288]{1,0:T(2,128)(2,1)S(1)}, bf16[1,12288]{1,0:T(2,128)(2,1)}, u32[]{:S(2)}) copy-start(bf16[1,12288]{1,0:T(2,128)(2,1)} %parent_ref.1) | copy-start | bytes 73732
  0.6 0.8 %copy-start.5 = (bf16[2,12288]{1,0:T(2,128)(2,1)S(1)}, bf16[2,12288]{1,0:T(2,128)(2,1)}, u32[]{:S(2)}) copy-start(bf16[2,12288]{1,0:T(2,128)(2,1)} %token_ref.1) | copy-start | bytes 147460
  1.5 6.4 %copy-start = (bf16[12288,128]{1,0:T(8,128)(2,1)S(1)}, bf16[12288,128]{1,0:T(8,128)(2,1)}, u32[]{:S(2)}) copy-start(bf16[12288,128]{1,0:T(8,128)(2,1)} %w_ref.2) | copy-start | bytes 9437188
  1.5 9.5 %collective-permute-start.2 = (bf16[2,18432]{1,0:T(2,128)(2,1)S(1)}, bf16[2,18432]{1,0:T(2,128)(2,1)S(1)}, u32[]{:S(2)}, u32[]{:S(2)}) collective-permute-start(bf16[2,18432]{1,0:T(2,128)(2,1)S(1)} %pack.1), channel_id=1, source_target_pairs={{0,9},{1,8},{2,11},{3,10},{4,13},{5,12},{6,15},{7,14},{8,1},{9,0},... | collective-permute-start | bytes 221192 | tf_op jit(solution)/shard_map/ppermute | solution.py:28
  5.0 5.9 %collective-permute-start.1 = (bf16[2,18432]{1,0:T(2,128)(2,1)S(1)}, bf16[2,18432]{1,0:T(2,128)(2,1)S(1)}, u32[]{:S(2)}, u32[]{:S(2)}) collective-permute-start(bf16[2,18432]{1,0:T(2,128)(2,1)S(1)} %pack.1), channel_id=1, source_target_pairs={{0,5},{1,4},{2,7},{3,6},{4,1},{5,0},{6,3},{7,2},{8,13},{9,12},{10,... | collective-permute-start | bytes 221192 | tf_op jit(solution)/shard_map/ppermute | solution.py:28
  6.9 4.5 %collective-permute-start = (bf16[2,18432]{1,0:T(2,128)(2,1)S(1)}, bf16[2,18432]{1,0:T(2,128)(2,1)S(1)}, u32[]{:S(2)}, u32[]{:S(2)}) collective-permute-start(bf16[2,18432]{1,0:T(2,128)(2,1)S(1)} %pack.1), channel_id=1, source_target_pairs={{0,3},{1,2},{2,1},{3,0},{4,7},{5,6},{6,5},{7,4},{8,11},{9,10},{10,... | collective-permute-start | bytes 221192 | tf_op jit(solution)/shard_map/ppermute | solution.py:28
  7.9 1.9 %copy-start.1 = (bf16[12288,128]{1,0:T(8,128)(2,1)S(1)}, bf16[12288,128]{1,0:T(8,128)(2,1)}, u32[]{:S(2)}) copy-start(bf16[12288,128]{1,0:T(8,128)(2,1)} %w_ref.3) | copy-start | bytes 9437188
  7.9 2.9 %copy-start.2 = (bf16[32,128]{1,0:T(8,128)(2,1)S(1)}, bf16[32,128]{1,0:T(8,128)(2,1)}, u32[]{:S(2)}) copy-start(bf16[32,128]{1,0:T(8,128)(2,1)} %flow_ref.1) | copy-start | bytes 24580
  7.9 2.9 %copy-start.3 = (s32[32]{0:T(128)S(1)}, s32[32]{0:T(128)}, u32[]{:S(2)}) copy-start(s32[32]{0:T(128)} %param.8) | copy-start | bytes 388
  11.4 4.1 %collective-permute-start.3 = (bf16[2,18432]{1,0:T(2,128)(2,1)S(1)}, bf16[2,18432]{1,0:T(2,128)(2,1)S(1)}, u32[]{:S(2)}, u32[]{:S(2)}) collective-permute-start(bf16[2,18432]{1,0:T(2,128)(2,1)S(1)} %get-tuple-element.30), channel_id=1, source_target_pairs={{0,5},{1,4},{2,7},{3,6},{4,1},{5,0},{6,3},{7,2},{8,13},{9,12},{10,... | collective-permute-start | bytes 221192 | tf_op jit(solution)/shard_map/ppermute | solution.py:28
  12.0 6.3 %collective-permute-start.4 = (bf16[2,18432]{1,0:T(2,128)(2,1)S(1)}, bf16[2,18432]{1,0:T(2,128)(2,1)S(1)}, u32[]{:S(2)}, u32[]{:S(2)}) collective-permute-start(bf16[2,18432]{1,0:T(2,128)(2,1)S(1)} %get-tuple-element.29), channel_id=1, source_target_pairs={{0,13},{1,12},{2,15},{3,14},{4,9},{5,8},{6,11},{7,10},{8,5},{9,4},... | collective-permute-start | bytes 221192 | tf_op jit(solution)/shard_map/ppermute | solution.py:28
  13.6 5.6 %collective-permute-start.5 = (bf16[4,18432]{1,0:T(4,128)(2,1)S(1)}, bf16[4,18432]{1,0:T(4,128)(2,1)S(1)}, u32[]{:S(2)}, u32[]{:S(2)}) collective-permute-start(bf16[4,18432]{1,0:T(4,128)(2,1)S(1)} %get-tuple-element.28), channel_id=1, source_target_pairs={{0,3},{1,2},{2,1},{3,0},{4,7},{5,6},{6,5},{7,4},{8,11},{9,10},{10,... | collective-permute-start | bytes 442376 | tf_op jit(solution)/shard_map/ppermute | solution.py:28
  15.4 5.2 %collective-permute-start.6 = (bf16[8,18432]{1,0:T(8,128)(2,1)S(1)}, bf16[8,18432]{1,0:T(8,128)(2,1)S(1)}, u32[]{:S(2)}, u32[]{:S(2)}) collective-permute-start(bf16[8,18432]{1,0:T(8,128)(2,1)S(1)} %pad_maximum_fusion.refs_0_), channel_id=1, source_target_pairs={{0,1},{1,0},{2,3},{3,2},{4,5},{5,4},{6,7},{7,6},{8,9},{9,8},{10,11... | collective-permute-start | bytes 884744 | tf_op jit(solution)/shard_map/ppermute | solution.py:28
  18.4 1.4 %collective-permute-start.7 = (bf16[4,18432]{1,0:T(4,128)(2,1)S(1)}, bf16[4,18432]{1,0:T(4,128)(2,1)S(1)}, u32[]{:S(2)}, u32[]{:S(2)}) collective-permute-start(bf16[4,18432]{1,0:T(4,128)(2,1)S(1)} %pad_maximum_fusion.2.refs_1_), channel_id=1, source_target_pairs={{0,1},{1,0},{2,3},{3,2},{4,5},{5,4},{6,7},{7,6},{8,9},{9,8},{10,11... | collective-permute-start | bytes 442376 | tf_op jit(solution)/shard_map/ppermute | solution.py:28
  19.2 1.4 %collective-permute-start.8 = (bf16[4,18432]{1,0:T(4,128)(2,1)S(1)}, bf16[4,18432]{1,0:T(4,128)(2,1)S(1)}, u32[]{:S(2)}, u32[]{:S(2)}) collective-permute-start(bf16[4,18432]{1,0:T(4,128)(2,1)S(1)} %collective-permute-done.5.refs_2_), channel_id=1, source_target_pairs={{0,1},{1,0},{2,3},{3,2},{4,5},{5,4},{6,7},{7,6},{8,9},{9,8},{10,11... | collective-permute-start | bytes 442376 | tf_op jit(solution)/shard_map/ppermute | solution.py:28
  22.8 1.5 %collective-permute-start.9 = (bf16[16,6144]{1,0:T(8,128)(2,1)S(1)}, bf16[16,6144]{1,0:T(8,128)(2,1)S(1)}, u32[]{:S(2)}, u32[]{:S(2)}) collective-permute-start(bf16[16,6144]{1,0:T(8,128)(2,1)S(1)} %get-tuple-element.35), channel_id=1, source_target_pairs={{0,1},{1,0},{2,3},{3,2},{4,5},{5,4},{6,7},{7,6},{8,9},{9,8},{10,11... | collective-permute-start | bytes 589832 | tf_op jit(solution)/shard_map/ppermute | solution.py:28
  24.4 5.4 %collective-permute-start.10 = (bf16[4,6144]{1,0:T(4,128)(2,1)S(1)}, bf16[4,6144]{1,0:T(4,128)(2,1)S(1)}, u32[]{:S(2)}, u32[]{:S(2)}) collective-permute-start(bf16[4,6144]{1,0:T(4,128)(2,1)S(1)} %get-tuple-element.41), channel_id=1, source_target_pairs={{0,3},{1,2},{2,1},{3,0},{4,7},{5,6},{6,5},{7,4},{8,11},{9,10},{10,... | collective-permute-start | bytes 147464 | tf_op jit(solution)/shard_map/ppermute | solution.py:28
  26.0 4.6 %collective-permute-start.12 = (bf16[4,6144]{1,0:T(4,128)(2,1)S(1)}, bf16[4,6144]{1,0:T(4,128)(2,1)S(1)}, u32[]{:S(2)}, u32[]{:S(2)}) collective-permute-start(bf16[4,6144]{1,0:T(4,128)(2,1)S(1)} %get-tuple-element.42), channel_id=1, source_target_pairs={{0,7},{1,6},{2,5},{3,4},{4,3},{5,2},{6,1},{7,0},{8,15},{9,14},{10,... | collective-permute-start | bytes 147464 | tf_op jit(solution)/shard_map/ppermute | solution.py:28
  27.1 3.7 %collective-permute-start.11 = (bf16[4,6144]{1,0:T(4,128)(2,1)S(1)}, bf16[4,6144]{1,0:T(4,128)(2,1)S(1)}, u32[]{:S(2)}, u32[]{:S(2)}) collective-permute-start(bf16[4,6144]{1,0:T(4,128)(2,1)S(1)} %get-tuple-element.43), channel_id=1, source_target_pairs={{0,5},{1,4},{2,7},{3,6},{4,1},{5,0},{6,3},{7,2},{8,13},{9,12},{10,... | collective-permute-start | bytes 147464 | tf_op jit(solution)/shard_map/ppermute | solution.py:28
  30.9 4.2 %collective-permute-start.13 = (bf16[2,6144]{1,0:T(2,128)(2,1)S(1)}, bf16[2,6144]{1,0:T(2,128)(2,1)S(1)}, u32[]{:S(2)}, u32[]{:S(2)}) collective-permute-start(bf16[2,6144]{1,0:T(2,128)(2,1)S(1)} %after.4.refs_0_), channel_id=1, source_target_pairs={{0,9},{1,8},{2,11},{3,10},{4,13},{5,12},{6,15},{7,14},{8,1},{9,0},... | collective-permute-start | bytes 73736 | tf_op jit(solution)/shard_map/ppermute | solution.py:28

commit v8 on v7

--- a/solution.py
+++ b/solution.py
@@ -36,7 +36,7 @@
     outer, inner, _ = factors(count)
     z_steps = [1 << i for i in range(outer.bit_length() - 1)]
     y_steps = [1 << i for i in range(inner.bit_length() - 1)]
-    squares = [[0, across(0, y, count), across(z, 0, count), across(z, y, count)] for z, y in zip(z_steps, y_steps)]
+    squares = [[0, across(z, y, count), across(0, y, count), across(z, 0, count)] for z, y in zip(z_steps, y_steps)]
     return [[0, 1]] + squares + [[0, across(z, 0, count)] for z in z_steps[len(y_steps):]]
 
 
@@ -192,7 +192,7 @@
     rows = sums_ref.shape[0] // 2
     count = rows // 2
 
-    step = 1024
+    step = half if count <= 16 else 1024
     for at in range(0, half, step):
         here, there, held = (pl.ds(at + base, step) for base in (0, half, width))
         pairs = jnp.concatenate([c[:, held].astype(F32) for c in cols], 0).astype(BF)

time: 35.9 us -> 35.9 us (level)
  starting transfers between devices: 15.5 us -> 15.9 us
where the time goes in v8:
time: 35.9 us; the launch traced here: 35.7 us
  starting transfers between devices  15.9 us (44%)
  Pallas kernels  8.64 us (24%)
  waiting for transfers between devices  7.32 us (20%)
  local copies, waits for them, and re-layouts  2.43 us (7%)
  between operations  0.79 us (2%)
  other arithmetic  0.68 us (2%)
    ppermute x14, starting transfers between devices, send(): return lax.ppermute(x, 'blk', [(i, i ^ mask) for i in range(count)])  15.9 us
    ppermute x14, waiting for transfers between devices, send(): return lax.ppermute(x, 'blk', [(i, i ^ mask) for i in range(count)])  7.32 us
    pallas_call x2, Pallas kernels, weight_terms(): pl.pallas_call(functools.partial(weight_kernel, side, step), out_shape=(j...  4.19 us
    unnamed x13, local copies, waits for them, and re-layouts  2.34 us
    pallas_call x1, Pallas kernels, forward(): pl.pallas_call(functools.partial(forward_kernel, len(columns)), out_shape...  2.22 us
    pallas_call x2, Pallas kernels, flip(): pl.pallas_call(flip_kernel, out_shape=(jax.ShapeDtypeStruct(w.shape, BF),...  2.01 us
  transfers between devices with their start and end apart: 14, of which 9 were waited for; matrix products, arithmetic and copies ran while one was open for 2% of the time, Pallas kernels for 18%

profile of v8, /device:TPU:0, one launch (start us, length us, event | category | flops | bytes accessed | tf_op | source)
XLA Modules:
  0.0 35.7 jit_solution(13856172030933087446)
XLA Ops:
  0.7 0.8 %copy-done.4 = bf16[1,12288]{1,0:T(2,128)(2,1)S(1)} copy-done((bf16[1,12288]{1,0:T(2,128)(2,1)S(1)}, bf16[1,12288]{1,0:T(2,128)(2,1)}, u32[]{:S(2)}) %copy-start.4) | copy-done | bytes 24600
  1.5 3.5 %collective-permute-start.2 = (bf16[2,18432]{1,0:T(2,128)(2,1)S(1)}, bf16[2,18432]{1,0:T(2,128)(2,1)S(1)}, u32[]{:S(2)}, u32[]{:S(2)}) collective-permute-start(bf16[2,18432]{1,0:T(2,128)(2,1)S(1)} %pack.1), channel_id=1, source_target_pairs={{0,9},{1,8},{2,11},{3,10},{4,13},{5,12},{6,15},{7,14},{8,1},{9,0},... | collective-permute-start | bytes 221192 | tf_op jit(solution)/shard_map/ppermute | solution.py:28
  5.0 1.9 %collective-permute-start.1 = (bf16[2,18432]{1,0:T(2,128)(2,1)S(1)}, bf16[2,18432]{1,0:T(2,128)(2,1)S(1)}, u32[]{:S(2)}, u32[]{:S(2)}) collective-permute-start(bf16[2,18432]{1,0:T(2,128)(2,1)S(1)} %pack.1), channel_id=1, source_target_pairs={{0,5},{1,4},{2,7},{3,6},{4,1},{5,0},{6,3},{7,2},{8,13},{9,12},{10,... | collective-permute-start | bytes 221192 | tf_op jit(solution)/shard_map/ppermute | solution.py:28
  6.9 1.0 %collective-permute-start = (bf16[2,18432]{1,0:T(2,128)(2,1)S(1)}, bf16[2,18432]{1,0:T(2,128)(2,1)S(1)}, u32[]{:S(2)}, u32[]{:S(2)}) collective-permute-start(bf16[2,18432]{1,0:T(2,128)(2,1)S(1)} %pack.1), channel_id=1, source_target_pairs={{0,3},{1,2},{2,1},{3,0},{4,7},{5,6},{6,5},{7,4},{8,11},{9,10},{10,... | collective-permute-start | bytes 221192 | tf_op jit(solution)/shard_map/ppermute | solution.py:28
  7.9 1.0 %flip.2 = (bf16[12288,128]{1,0:T(8,128)(2,1)S(1)}, bf16[128,12288]{1,0:T(8,128)(2,1)S(1)}) custom-call(bf16[12288,128]{1,0:T(8,128)(2,1)S(1)} %copy-done), custom_call_target="tpu_custom_call" | custom-call | bytes 6291456 | tf_op jit(solution)/shard_map/flip/pallas_call | solution.py:141
  8.9 0.9 %copy-done.1 = bf16[12288,128]{1,0:T(8,128)(2,1)S(1)} copy-done((bf16[12288,128]{1,0:T(8,128)(2,1)S(1)}, bf16[12288,128]{1,0:T(8,128)(2,1)}, u32[]{:S(2)}) %copy-start.1) | copy-done | bytes 3145752
  9.8 1.0 %flip.3 = (bf16[12288,128]{1,0:T(8,128)(2,1)S(1)}, bf16[128,12288]{1,0:T(8,128)(2,1)S(1)}) custom-call(bf16[12288,128]{1,0:T(8,128)(2,1)S(1)} %copy-done.1), custom_call_target="tpu_custom_call" | custom-call | bytes 6291456 | tf_op jit(solution)/shard_map/flip/pallas_call | solution.py:141
  10.8 0.2 select.1
  11.0 0.2 pad_maximum_fusion.1.refs_1_
  11.1 0.3 collective-permute-done.refs_0_
  11.4 0.6 %collective-permute-start.3 = (bf16[2,18432]{1,0:T(2,128)(2,1)S(1)}, bf16[2,18432]{1,0:T(2,128)(2,1)S(1)}, u32[]{:S(2)}, u32[]{:S(2)}) collective-permute-start(bf16[2,18432]{1,0:T(2,128)(2,1)S(1)} %get-tuple-element.30), channel_id=1, source_target_pairs={{0,5},{1,4},{2,7},{3,6},{4,1},{5,0},{6,3},{7,2},{8,13},{9,12},{10,... | collective-permute-start | bytes 221192 | tf_op jit(solution)/shard_map/ppermute | solution.py:28
  12.0 1.6 %collective-permute-start.4 = (bf16[2,18432]{1,0:T(2,128)(2,1)S(1)}, bf16[2,18432]{1,0:T(2,128)(2,1)S(1)}, u32[]{:S(2)}, u32[]{:S(2)}) collective-permute-start(bf16[2,18432]{1,0:T(2,128)(2,1)S(1)} %get-tuple-element.29), channel_id=1, source_target_pairs={{0,13},{1,12},{2,15},{3,14},{4,9},{5,8},{6,11},{7,10},{8,5},{9,4},... | collective-permute-start | bytes 221192 | tf_op jit(solution)/shard_map/ppermute | solution.py:28
  13.6 1.6 %collective-permute-start.5 = (bf16[4,18432]{1,0:T(4,128)(2,1)S(1)}, bf16[4,18432]{1,0:T(4,128)(2,1)S(1)}, u32[]{:S(2)}, u32[]{:S(2)}) collective-permute-start(bf16[4,18432]{1,0:T(4,128)(2,1)S(1)} %get-tuple-element.28), channel_id=1, source_target_pairs={{0,3},{1,2},{2,1},{3,0},{4,7},{5,6},{6,5},{7,4},{8,11},{9,10},{10,... | collective-permute-start | bytes 442376 | tf_op jit(solution)/shard_map/ppermute | solution.py:28
  15.1 0.2 pad_maximum_fusion.refs_0_
  15.5 2.7 %collective-permute-done.4 = bf16[2,18432]{1,0:T(2,128)(2,1)S(1)} collective-permute-done((bf16[2,18432]{1,0:T(2,128)(2,1)S(1)}, bf16[2,18432]{1,0:T(2,128)(2,1)S(1)}, u32[]{:S(2)}, u32[]{:S(2)}) %collective-permute-start.4) | collective-permute-done | bytes 73760 | tf_op jit(solution)/shard_map/ppermute | solution.py:28
  18.5 0.7 %collective-permute-done.5.refs_2_ = bf16[4,18432]{1,0:T(4,128)(2,1)S(1)} collective-permute-done((bf16[4,18432]{1,0:T(4,128)(2,1)S(1)}, bf16[4,18432]{1,0:T(4,128)(2,1)S(1)}, u32[]{:S(2)}, u32[]{:S(2)}) %collective-permute-start.5) | collective-permute-done | bytes 147488 | tf_op jit(solution)/shard_map/ppermute | solution.py:28
  19.2 0.4 %collective-permute-start.8 = (bf16[4,18432]{1,0:T(4,128)(2,1)S(1)}, bf16[4,18432]{1,0:T(4,128)(2,1)S(1)}, u32[]{:S(2)}, u32[]{:S(2)}) collective-permute-start(bf16[4,18432]{1,0:T(4,128)(2,1)S(1)} %collective-permute-done.5.refs_2_), channel_id=1, source_target_pairs={{0,1},{1,0},{2,3},{3,2},{4,5},{5,4},{6,7},{7,6},{8,9},{9,8},{10,11... | collective-permute-start | bytes 442376 | tf_op jit(solution)/shard_map/ppermute | solution.py:28
  19.6 0.3 collective-permute-done.7.refs_4_
  19.8 0.8 %collective-permute-done.8.refs_5_ = bf16[4,18432]{1,0:T(4,128)(2,1)S(1)} collective-permute-done((bf16[4,18432]{1,0:T(4,128)(2,1)S(1)}, bf16[4,18432]{1,0:T(4,128)(2,1)S(1)}, u32[]{:S(2)}, u32[]{:S(2)}) %collective-permute-start.8) | collective-permute-done | bytes 147488 | tf_op jit(solution)/shard_map/ppermute | solution.py:28
  20.6 2.2 %forward.1 = (bf16[32,12288]{1,0:T(8,128)(2,1)S(1)}, bf16[32,256]{1,0:T(8,128)(2,1)S(1)}, f32[16,6144]{1,0:T(8,128)S(1)}, bf16[16,6144]{1,0:T(8,128)(2,1)S(1)}) custom-call(f32[32,128]{1,0:T(8,128)S(1)} %get-tuple-element.21.refs_3_.flow_ref, bf16[64,32]{1,0:T(8,128)(2,1)S(1)} %get-tuple-element.22.refs_4_.pick_ref, ...), custom_call_target="tpu_custom_call" | custom-call | flops 402653184 | bytes 12582912 | tf_op jit(solution)/shard_map/forward/pallas_call | solution.py:228
  22.8 0.4 %collective-permute-start.9 = (bf16[16,6144]{1,0:T(8,128)(2,1)S(1)}, bf16[16,6144]{1,0:T(8,128)(2,1)S(1)}, u32[]{:S(2)}, u32[]{:S(2)}) collective-permute-start(bf16[16,6144]{1,0:T(8,128)(2,1)S(1)} %get-tuple-element.35), channel_id=1, source_target_pairs={{0,1},{1,0},{2,3},{3,2},{4,5},{5,4},{6,7},{7,6},{8,9},{9,8},{10,11... | collective-permute-start | bytes 589832 | tf_op jit(solution)/shard_map/ppermute | solution.py:28
  23.2 1.1 %collective-permute-done.9 = bf16[16,6144]{1,0:T(8,128)(2,1)S(1)} collective-permute-done((bf16[16,6144]{1,0:T(8,128)(2,1)S(1)}, bf16[16,6144]{1,0:T(8,128)(2,1)S(1)}, u32[]{:S(2)}, u32[]{:S(2)}) %collective-permute-start.9) | collective-permute-done | bytes 196640 | tf_op jit(solution)/shard_map/ppermute | solution.py:28
  24.4 2.2 %collective-permute-start.10 = (bf16[4,6144]{1,0:T(4,128)(2,1)S(1)}, bf16[4,6144]{1,0:T(4,128)(2,1)S(1)}, u32[]{:S(2)}, u32[]{:S(2)}) collective-permute-start(bf16[4,6144]{1,0:T(4,128)(2,1)S(1)} %get-tuple-element.41), channel_id=1, source_target_pairs={{0,7},{1,6},{2,5},{3,4},{4,3},{5,2},{6,1},{7,0},{8,15},{9,14},{10,... | collective-permute-start | bytes 147464 | tf_op jit(solution)/shard_map/ppermute | solution.py:28
  26.6 0.6 %collective-permute-start.12 = (bf16[4,6144]{1,0:T(4,128)(2,1)S(1)}, bf16[4,6144]{1,0:T(4,128)(2,1)S(1)}, u32[]{:S(2)}, u32[]{:S(2)}) collective-permute-start(bf16[4,6144]{1,0:T(4,128)(2,1)S(1)} %get-tuple-element.42), channel_id=1, source_target_pairs={{0,5},{1,4},{2,7},{3,6},{4,1},{5,0},{6,3},{7,2},{8,13},{9,12},{10,... | collective-permute-start | bytes 147464 | tf_op jit(solution)/shard_map/ppermute | solution.py:28
  27.2 0.5 %collective-permute-start.11 = (bf16[4,6144]{1,0:T(4,128)(2,1)S(1)}, bf16[4,6144]{1,0:T(4,128)(2,1)S(1)}, u32[]{:S(2)}, u32[]{:S(2)}) collective-permute-start(bf16[4,6144]{1,0:T(4,128)(2,1)S(1)} %get-tuple-element.43), channel_id=1, source_target_pairs={{0,3},{1,2},{2,1},{3,0},{4,7},{5,6},{6,5},{7,4},{8,11},{9,10},{10,... | collective-permute-start | bytes 147464 | tf_op jit(solution)/shard_map/ppermute | solution.py:28
  27.7 2.1 %weight_terms.2 = (bf16[12288,128]{1,0:T(8,128)(2,1)}, f32[8,128]{1,0:T(8,128)S(1)}) custom-call(bf16[32,12288]{1,0:T(8,128)(2,1)S(1)} %get-tuple-element.31.x_ref, bf16[32,256]{1,0:T(8,128)(2,1)S(1)} %get-tuple-element.32.d_ref), custom_call_target="tpu_custom_call" | custom-call | flops 100663296 | bytes 3145728 | tf_op jit(solution)/shard_map/weight_terms/pallas_call | solution.py:264
  29.8 0.3 collective-permute-done.12
  30.1 0.6 %collective-permute-done.11 = bf16[4,6144]{1,0:T(4,128)(2,1)S(1)} collective-permute-done((bf16[4,6144]{1,0:T(4,128)(2,1)S(1)}, bf16[4,6144]{1,0:T(4,128)(2,1)S(1)}, u32[]{:S(2)}, u32[]{:S(2)}) %collective-permute-start.11) | collective-permute-done | bytes 49184 | tf_op jit(solution)/shard_map/ppermute | solution.py:28
  30.8 1.4 %collective-permute-start.13 = (bf16[2,6144]{1,0:T(2,128)(2,1)S(1)}, bf16[2,6144]{1,0:T(2,128)(2,1)S(1)}, u32[]{:S(2)}, u32[]{:S(2)}) collective-permute-start(bf16[2,6144]{1,0:T(2,128)(2,1)S(1)} %after.4.refs_0_), channel_id=1, source_target_pairs={{0,9},{1,8},{2,11},{3,10},{4,13},{5,12},{6,15},{7,14},{8,1},{9,0},... | collective-permute-start | bytes 73736 | tf_op jit(solution)/shard_map/ppermute | solution.py:28
  32.3 2.1 %weight_terms.3 = (bf16[12288,128]{1,0:T(8,128)(2,1)}, f32[8,128]{1,0:T(8,128)S(1)}) custom-call(bf16[32,12288]{1,0:T(8,128)(2,1)S(1)} %get-tuple-element.31.x_ref, bf16[32,256]{1,0:T(8,128)(2,1)S(1)} %get-tuple-element.32.d_ref, bf16[2,6144]{1,0:T(2,128)(2,1)S(1)} %after.4.refs_0_), custom_call_target="tpu_custom_call" | custom-call | flops 100663296 | bytes 3145728 | tf_op jit(solution)/shard_map/weight_terms/pallas_call | solution.py:264
  34.4 0.7 %collective-permute-done.13.refs_0_ = bf16[2,6144]{1,0:T(2,128)(2,1)S(1)} collective-permute-done((bf16[2,6144]{1,0:T(2,128)(2,1)S(1)}, bf16[2,6144]{1,0:T(2,128)(2,1)S(1)}, u32[]{:S(2)}, u32[]{:S(2)}) %collective-permute-start.13) | collective-permute-done | bytes 24608 | tf_op jit(solution)/shard_map/ppermute | solution.py:28
  35.1 0.7 %copy.14 = bf16[1,1,2,6144]{3,1,2,0:T(2,128)(2,1)} copy(bf16[1,1,2,6144]{3,2,1,0:T(2,128)(2,1)S(1)} %fusion.3) | data formatting | bytes 49152
  (28 shorter events, 0.7 us)
Async XLA Ops:
  0.6 0.8 %copy-start.4 = (bf16[1,12288]{1,0:T(2,128)(2,1)S(1)}, bf16[1,12288]{1,0:T(2,128)(2,1)}, u32[]{:S(2)}) copy-start(bf16[1,12288]{1,0:T(2,128)(2,1)} %parent_ref.1) | copy-start | bytes 73732
  0.6 0.8 %copy-start.5 = (bf16[2,12288]{1,0:T(2,128)(2,1)S(1)}, bf16[2,12288]{1,0:T(2,128)(2,1)}, u32[]{:S(2)}) copy-start(bf16[2,12288]{1,0:T(2,128)(2,1)} %token_ref.1) | copy-start | bytes 147460
  1.5 6.4 %copy-start = (bf16[12288,128]{1,0:T(8,128)(2,1)S(1)}, bf16[12288,128]{1,0:T(8,128)(2,1)}, u32[]{:S(2)}) copy-start(bf16[12288,128]{1,0:T(8,128)(2,1)} %w_ref.2) | copy-start | bytes 9437188
  1.5 9.5 %collective-permute-start.2 = (bf16[2,18432]{1,0:T(2,128)(2,1)S(1)}, bf16[2,18432]{1,0:T(2,128)(2,1)S(1)}, u32[]{:S(2)}, u32[]{:S(2)}) collective-permute-start(bf16[2,18432]{1,0:T(2,128)(2,1)S(1)} %pack.1), channel_id=1, source_target_pairs={{0,9},{1,8},{2,11},{3,10},{4,13},{5,12},{6,15},{7,14},{8,1},{9,0},... | collective-permute-start | bytes 221192 | tf_op jit(solution)/shard_map/ppermute | solution.py:28
  5.0 5.9 %collective-permute-start.1 = (bf16[2,18432]{1,0:T(2,128)(2,1)S(1)}, bf16[2,18432]{1,0:T(2,128)(2,1)S(1)}, u32[]{:S(2)}, u32[]{:S(2)}) collective-permute-start(bf16[2,18432]{1,0:T(2,128)(2,1)S(1)} %pack.1), channel_id=1, source_target_pairs={{0,5},{1,4},{2,7},{3,6},{4,1},{5,0},{6,3},{7,2},{8,13},{9,12},{10,... | collective-permute-start | bytes 221192 | tf_op jit(solution)/shard_map/ppermute | solution.py:28
  6.9 4.5 %collective-permute-start = (bf16[2,18432]{1,0:T(2,128)(2,1)S(1)}, bf16[2,18432]{1,0:T(2,128)(2,1)S(1)}, u32[]{:S(2)}, u32[]{:S(2)}) collective-permute-start(bf16[2,18432]{1,0:T(2,128)(2,1)S(1)} %pack.1), channel_id=1, source_target_pairs={{0,3},{1,2},{2,1},{3,0},{4,7},{5,6},{6,5},{7,4},{8,11},{9,10},{10,... | collective-permute-start | bytes 221192 | tf_op jit(solution)/shard_map/ppermute | solution.py:28
  7.9 1.9 %copy-start.1 = (bf16[12288,128]{1,0:T(8,128)(2,1)S(1)}, bf16[12288,128]{1,0:T(8,128)(2,1)}, u32[]{:S(2)}) copy-start(bf16[12288,128]{1,0:T(8,128)(2,1)} %w_ref.3) | copy-start | bytes 9437188
  7.9 2.9 %copy-start.2 = (bf16[32,128]{1,0:T(8,128)(2,1)S(1)}, bf16[32,128]{1,0:T(8,128)(2,1)}, u32[]{:S(2)}) copy-start(bf16[32,128]{1,0:T(8,128)(2,1)} %flow_ref.1) | copy-start | bytes 24580
  7.9 2.9 %copy-start.3 = (s32[32]{0:T(128)S(1)}, s32[32]{0:T(128)}, u32[]{:S(2)}) copy-start(s32[32]{0:T(128)} %param.8) | copy-start | bytes 388
  11.4 4.1 %collective-permute-start.3 = (bf16[2,18432]{1,0:T(2,128)(2,1)S(1)}, bf16[2,18432]{1,0:T(2,128)(2,1)S(1)}, u32[]{:S(2)}, u32[]{:S(2)}) collective-permute-start(bf16[2,18432]{1,0:T(2,128)(2,1)S(1)} %get-tuple-element.30), channel_id=1, source_target_pairs={{0,5},{1,4},{2,7},{3,6},{4,1},{5,0},{6,3},{7,2},{8,13},{9,12},{10,... | collective-permute-start | bytes 221192 | tf_op jit(solution)/shard_map/ppermute | solution.py:28
  12.0 6.3 %collective-permute-start.4 = (bf16[2,18432]{1,0:T(2,128)(2,1)S(1)}, bf16[2,18432]{1,0:T(2,128)(2,1)S(1)}, u32[]{:S(2)}, u32[]{:S(2)}) collective-permute-start(bf16[2,18432]{1,0:T(2,128)(2,1)S(1)} %get-tuple-element.29), channel_id=1, source_target_pairs={{0,13},{1,12},{2,15},{3,14},{4,9},{5,8},{6,11},{7,10},{8,5},{9,4},... | collective-permute-start | bytes 221192 | tf_op jit(solution)/shard_map/ppermute | solution.py:28
  13.6 5.6 %collective-permute-start.5 = (bf16[4,18432]{1,0:T(4,128)(2,1)S(1)}, bf16[4,18432]{1,0:T(4,128)(2,1)S(1)}, u32[]{:S(2)}, u32[]{:S(2)}) collective-permute-start(bf16[4,18432]{1,0:T(4,128)(2,1)S(1)} %get-tuple-element.28), channel_id=1, source_target_pairs={{0,3},{1,2},{2,1},{3,0},{4,7},{5,6},{6,5},{7,4},{8,11},{9,10},{10,... | collective-permute-start | bytes 442376 | tf_op jit(solution)/shard_map/ppermute | solution.py:28
  15.4 5.2 %collective-permute-start.6 = (bf16[8,18432]{1,0:T(8,128)(2,1)S(1)}, bf16[8,18432]{1,0:T(8,128)(2,1)S(1)}, u32[]{:S(2)}, u32[]{:S(2)}) collective-permute-start(bf16[8,18432]{1,0:T(8,128)(2,1)S(1)} %pad_maximum_fusion.refs_0_), channel_id=1, source_target_pairs={{0,1},{1,0},{2,3},{3,2},{4,5},{5,4},{6,7},{7,6},{8,9},{9,8},{10,11... | collective-permute-start | bytes 884744 | tf_op jit(solution)/shard_map/ppermute | solution.py:28
  18.4 1.4 %collective-permute-start.7 = (bf16[4,18432]{1,0:T(4,128)(2,1)S(1)}, bf16[4,18432]{1,0:T(4,128)(2,1)S(1)}, u32[]{:S(2)}, u32[]{:S(2)}) collective-permute-start(bf16[4,18432]{1,0:T(4,128)(2,1)S(1)} %pad_maximum_fusion.2.refs_1_), channel_id=1, source_target_pairs={{0,1},{1,0},{2,3},{3,2},{4,5},{5,4},{6,7},{7,6},{8,9},{9,8},{10,11... | collective-permute-start | bytes 442376 | tf_op jit(solution)/shard_map/ppermute | solution.py:28
  19.2 1.4 %collective-permute-start.8 = (bf16[4,18432]{1,0:T(4,128)(2,1)S(1)}, bf16[4,18432]{1,0:T(4,128)(2,1)S(1)}, u32[]{:S(2)}, u32[]{:S(2)}) collective-permute-start(bf16[4,18432]{1,0:T(4,128)(2,1)S(1)} %collective-permute-done.5.refs_2_), channel_id=1, source_target_pairs={{0,1},{1,0},{2,3},{3,2},{4,5},{5,4},{6,7},{7,6},{8,9},{9,8},{10,11... | collective-permute-start | bytes 442376 | tf_op jit(solution)/shard_map/ppermute | solution.py:28
  22.8 1.5 %collective-permute-start.9 = (bf16[16,6144]{1,0:T(8,128)(2,1)S(1)}, bf16[16,6144]{1,0:T(8,128)(2,1)S(1)}, u32[]{:S(2)}, u32[]{:S(2)}) collective-permute-start(bf16[16,6144]{1,0:T(8,128)(2,1)S(1)} %get-tuple-element.35), channel_id=1, source_target_pairs={{0,1},{1,0},{2,3},{3,2},{4,5},{5,4},{6,7},{7,6},{8,9},{9,8},{10,11... | collective-permute-start | bytes 589832 | tf_op jit(solution)/shard_map/ppermute | solution.py:28
  24.4 5.4 %collective-permute-start.10 = (bf16[4,6144]{1,0:T(4,128)(2,1)S(1)}, bf16[4,6144]{1,0:T(4,128)(2,1)S(1)}, u32[]{:S(2)}, u32[]{:S(2)}) collective-permute-start(bf16[4,6144]{1,0:T(4,128)(2,1)S(1)} %get-tuple-element.41), channel_id=1, source_target_pairs={{0,7},{1,6},{2,5},{3,4},{4,3},{5,2},{6,1},{7,0},{8,15},{9,14},{10,... | collective-permute-start | bytes 147464 | tf_op jit(solution)/shard_map/ppermute | solution.py:28
  26.6 3.5 %collective-permute-start.12 = (bf16[4,6144]{1,0:T(4,128)(2,1)S(1)}, bf16[4,6144]{1,0:T(4,128)(2,1)S(1)}, u32[]{:S(2)}, u32[]{:S(2)}) collective-permute-start(bf16[4,6144]{1,0:T(4,128)(2,1)S(1)} %get-tuple-element.42), channel_id=1, source_target_pairs={{0,5},{1,4},{2,7},{3,6},{4,1},{5,0},{6,3},{7,2},{8,13},{9,12},{10,... | collective-permute-start | bytes 147464 | tf_op jit(solution)/shard_map/ppermute | solution.py:28
  27.2 3.5 %collective-permute-start.11 = (bf16[4,6144]{1,0:T(4,128)(2,1)S(1)}, bf16[4,6144]{1,0:T(4,128)(2,1)S(1)}, u32[]{:S(2)}, u32[]{:S(2)}) collective-permute-start(bf16[4,6144]{1,0:T(4,128)(2,1)S(1)} %get-tuple-element.43), channel_id=1, source_target_pairs={{0,3},{1,2},{2,1},{3,0},{4,7},{5,6},{6,5},{7,4},{8,11},{9,10},{10,... | collective-permute-start | bytes 147464 | tf_op jit(solution)/shard_map/ppermute | solution.py:28
  30.8 4.2 %collective-permute-start.13 = (bf16[2,6144]{1,0:T(2,128)(2,1)S(1)}, bf16[2,6144]{1,0:T(2,128)(2,1)S(1)}, u32[]{:S(2)}, u32[]{:S(2)}) collective-permute-start(bf16[2,6144]{1,0:T(2,128)(2,1)S(1)} %after.4.refs_0_), channel_id=1, source_target_pairs={{0,9},{1,8},{2,11},{3,10},{4,13},{5,12},{6,15},{7,14},{8,1},{9,0},... | collective-permute-start | bytes 73736 | tf_op jit(solution)/shard_map/ppermute | solution.py:28
